TPU v7x, 32 devices: a whole 2x2x4 slice. The times are simulated.
32 devices in a mesh: rows: 16 (over z, y, x), blk: 2 (over core).
Axes of the slice: x: 2, y: 2, z: 4, core: 2. Of those that a mesh axis runs over, the one named last changes fastest.
Arguments:
- tokens: bfloat16 [16, 1024, 768], P('rows', 'blk'), may hold values from -6 to 6
- segments: int32 [16, 1024], P('rows'), may hold values from 0 to 1024, as said below
- w_qkv: bfloat16 [768, 2304], P(('rows', 'blk')), may hold values from -0.21875 to 0.21875
- w_out: bfloat16 [768, 768], P(('rows', 'blk')), may hold values from -1.25 to 1.25
- ln1_gain: bfloat16 [768], P(('rows', 'blk')), may hold values from 0.5 to 1.5
- ln1_bias: bfloat16 [768], P(('rows', 'blk')), may hold values from -1.796875 to 1.796875
- w_gate_up: bfloat16 [768, 6144], P(('rows', 'blk')), may hold values from -0.21875 to 0.21875
- w_down: bfloat16 [3072, 768], P(('rows', 'blk')), may hold values from -0.109375 to 0.109375
- ln2_gain: bfloat16 [768], P(('rows', 'blk')), may hold values from 0.5 to 1.5
- ln2_bias: bfloat16 [768], P(('rows', 'blk')), may hold values from -1.796875 to 1.796875
- out_grad: bfloat16 [16, 1024, 768], P('rows', 'blk'), may hold values from -6 to 6
Outputs:
- output: bfloat16 [16, 1024, 768], P('rows', 'blk')
- tokens_grad: bfloat16 [16, 1024, 768], P('rows', 'blk')
- w_qkv_grad: float32 [768, 2304], P(('rows', 'blk'))
- w_out_grad: float32 [768, 768], P(('rows', 'blk'))
- ln1_gain_grad: float32 [768], P(('rows', 'blk'))
- ln1_bias_grad: float32 [768], P(('rows', 'blk'))
- w_gate_up_grad: float32 [768, 6144], P(('rows', 'blk'))
- w_down_grad: float32 [3072, 768], P(('rows', 'blk'))
- ln2_gain_grad: float32 [768], P(('rows', 'blk'))
- ln2_bias_grad: float32 [768], P(('rows', 'blk'))
- stats: float32 [4], replicated
Inputs may be any that keep to these rules, and one draw needn't show every extreme that they name: `segments`: each packed row is a run of fragments labelled 0, 1, 2, ... in order, each of at most 512 positions (all but the last one before the padding at least 128), one of them exactly 512, followed by 1 to 255 padding positions labelled 1024.
All inputs are finite; a program needn't handle non-finite values.
Results may differ from a plain program's by a relative error of at most 0.014.
Values may be sent and summed in bfloat16 or wider, within the bound.
A program may use at most 192 MiB of HBM per device.

v0:
```python
import jax
import jax.numpy as jnp
from jax import lax
from jax.sharding import PartitionSpec as P

HEADS = 12


ln_eps = 1e-12
masked_score = -1e30
group_heads = 2
lane_width = 128


def extended(cells, sides, width):
    for axis, dim in sides:
        count = lax.axis_size(axis)
        ends = count - 1
        head = lax.slice_in_dim(cells, 0, width, axis=dim)
        tail = lax.slice_in_dim(cells, cells.shape[dim] - width, cells.shape[dim], axis=dim)
        cells = jnp.concatenate(
            [
                lax.ppermute(tail, axis, [(i, (i + 1) % count) for i in range(ends)]),
                cells,
                lax.ppermute(head, axis, [((i + 1) % count, i) for i in range(ends)]),
            ],
            axis=dim,
        )
    return cells


def layer_norm(resid, gain, bias):
    mean = jnp.mean(resid, -1, keepdims=True)
    centred = resid - mean
    spread = jnp.mean(centred * centred, -1, keepdims=True)
    return centred * lax.rsqrt(spread + ln_eps) * gain + bias


def geglu(gate_up):
    half = gate_up.shape[-1] // 2
    return jax.nn.gelu(gate_up[:, :half], approximate=False) * gate_up[:, half:]


def head_slopes(heads):
    order = jnp.arange(1, heads + 1, dtype=jnp.float32)
    return jnp.exp2(-8.0 * order / heads)


def permitted(labels_q, labels_k, pos_q, pos_k, pad_label):
    same_piece = (labels_q[:, None] == labels_k[None, :]) & (labels_k[None, :] != pad_label)
    return same_piece | (pos_q[:, None] == pos_k[None, :])


def times_transposed(left, right):
    return lax.dot_general(
        left, right, (((1,), (1,)), ((), ())), preferred_element_type=jnp.float32
    )


def transposed_times(left, right):
    return lax.dot_general(
        left, right, (((0,), (0,)), ((), ())), preferred_element_type=jnp.float32
    )


def split_heads(matrix, heads):
    count, width = matrix.shape
    return matrix.reshape(count, heads // group_heads, group_heads, width // heads).transpose(
        1, 2, 0, 3
    )


def merge_heads(groups):
    number, size, count, depth = groups.shape
    return groups.transpose(2, 0, 1, 3).reshape(count, number * size * depth)


def lane_rows(matrix):
    return matrix.reshape(-1, lane_width)


def owner_rows(flat, whole_rows, columns, owners):
    return flat.reshape(whole_rows // owners, columns)


def group_scores(q_grp, k_grp, slope_grp, distance, allowed):
    scale = q_grp.shape[-1] ** (-0.5)
    raw = jnp.einsum("gqd,gkd->gqk", q_grp, k_grp, preferred_element_type=jnp.float32) * scale
    raw = raw - slope_grp[:, None, None] * distance[None]
    return jnp.where(allowed[None], raw, masked_score)


def body(
    tokens,
    segments,
    w_qkv,
    w_out,
    ln1_gain,
    ln1_bias,
    w_gate_up,
    w_down,
    ln2_gain,
    ln2_bias,
    out_grad,
):
    inputs = tokens[0]
    tok_rows, width = inputs.shape
    heads = HEADS
    owners = lax.axis_size(("rows", "blk"))
    labels = segments[0]
    seq_len = labels.shape[0]
    first = lax.axis_index("blk") * tok_rows
    query_pos = first + jnp.arange(tok_rows, dtype=jnp.int32)
    window_pos = first - tok_rows + jnp.arange(3 * tok_rows, dtype=jnp.int32)
    query_labels = lax.dynamic_slice_in_dim(labels, first, tok_rows, 0)
    padded_labels = jnp.pad(labels, (tok_rows, tok_rows), constant_values=seq_len)
    window_labels = lax.dynamic_slice_in_dim(padded_labels, first, 3 * tok_rows, 0)
    slope_groups = head_slopes(heads).reshape(heads // group_heads, group_heads)
    allowed = permitted(query_labels, window_labels, query_pos, window_pos, seq_len)
    distance = jnp.abs(query_pos[:, None] - window_pos[None, :]).astype(jnp.float32)
    wqkv_full, wout_full, gain_one, bias_one = (
        lax.all_gather(w_qkv, ("rows", "blk"), axis=0, tiled=True),
        lax.all_gather(w_out, ("rows", "blk"), axis=0, tiled=True),
        lax.all_gather(ln1_gain, ("rows", "blk"), axis=0, tiled=True),
        lax.all_gather(ln1_bias, ("rows", "blk"), axis=0, tiled=True),
    )
    qkv = jnp.dot(inputs, wqkv_full, preferred_element_type=jnp.float32).astype(jnp.bfloat16)
    query = qkv[:, :width]
    window_kv = extended(qkv[:, width:], (("blk", 0),), tok_rows)
    q_groups = split_heads(query, heads)
    k_groups = split_heads(window_kv[:, :width], heads)
    v_groups = split_heads(window_kv[:, width:], heads)

    def forward_group(parts):
        q_grp, k_grp, v_grp, slope_grp = parts
        logits = group_scores(q_grp, k_grp, slope_grp, distance, allowed)
        top = jnp.max(logits, -1, keepdims=True)
        lse = top + jnp.log(jnp.sum(jnp.exp(logits - top), -1, keepdims=True))
        probs = jnp.exp(logits - lse).astype(jnp.bfloat16)
        mixed = jnp.einsum("gqk,gkd->gqd", probs, v_grp, preferred_element_type=jnp.float32)
        return (mixed, lse[..., 0])

    mixed_groups, lse_groups = lax.map(forward_group, (q_groups, k_groups, v_groups, slope_groups))
    attended = merge_heads(mixed_groups).astype(jnp.bfloat16)
    branch_a = jnp.dot(attended, wout_full, preferred_element_type=jnp.float32)
    inputs_float = inputs.astype(jnp.float32)
    resid_one = inputs_float + branch_a
    hidden1, norm_one_back = jax.vjp(
        layer_norm, resid_one, gain_one.astype(jnp.float32), bias_one.astype(jnp.float32)
    )
    hidden1_low = hidden1.astype(jnp.bfloat16)
    wgu_full, wdown_full, gain_two, bias_two = (
        lax.all_gather(w_gate_up, ("rows", "blk"), axis=0, tiled=True),
        lax.all_gather(w_down, ("rows", "blk"), axis=0, tiled=True),
        lax.all_gather(ln2_gain, ("rows", "blk"), axis=0, tiled=True),
        lax.all_gather(ln2_bias, ("rows", "blk"), axis=0, tiled=True),
    )
    gate_up = jnp.dot(hidden1_low, wgu_full, preferred_element_type=jnp.float32)
    act, glu_back = jax.vjp(geglu, gate_up)
    act_low = act.astype(jnp.bfloat16)
    branch_f = jnp.dot(act_low, wdown_full, preferred_element_type=jnp.float32)
    final, norm_two_back = jax.vjp(
        layer_norm, hidden1 + branch_f, gain_two.astype(jnp.float32), bias_two.astype(jnp.float32)
    )
    output = final.astype(jnp.bfloat16)[None]
    valid = (query_labels != seq_len).astype(jnp.float32)[:, None]
    squares = jnp.stack(
        [jnp.sum(valid * term * term) for term in (inputs_float, branch_a, hidden1, branch_f)]
    )
    square_sums, valid_count = lax.psum((squares, jnp.sum(valid)), ("rows", "blk"))
    stats = jnp.sqrt(square_sums / (valid_count * width))
    d_resid_two, d_gain_two, d_bias_two = norm_two_back(out_grad[0].astype(jnp.float32))
    d_branch_f = d_resid_two.astype(jnp.bfloat16)
    wgu_back, wdown_back = (
        lax.all_gather(w_gate_up, ("rows", "blk"), axis=0, tiled=True),
        lax.all_gather(w_down, ("rows", "blk"), axis=0, tiled=True),
    )
    d_act = times_transposed(d_branch_f, wdown_back)
    (d_gate_up,) = glu_back(d_act)
    d_gate_up_low = d_gate_up.astype(jnp.bfloat16)
    grad_down = transposed_times(act_low, d_branch_f)
    grad_gate_up = transposed_times(hidden1_low, d_gate_up_low)
    d_hidden1 = d_resid_two + times_transposed(d_gate_up_low, wgu_back)
    ffn_sums = (
        lax.psum_scatter(lane_rows(grad_gate_up), ("rows", "blk"), scatter_dimension=0, tiled=True),
        lax.psum_scatter(lane_rows(grad_down), ("rows", "blk"), scatter_dimension=0, tiled=True),
        lax.psum_scatter(d_gain_two, ("rows", "blk"), scatter_dimension=0, tiled=True),
        lax.psum_scatter(d_bias_two, ("rows", "blk"), scatter_dimension=0, tiled=True),
    )
    d_resid_one, d_gain_one, d_bias_one = norm_one_back(d_hidden1)
    d_branch_a = d_resid_one.astype(jnp.bfloat16)
    wqkv_back, wout_back = (
        lax.all_gather(w_qkv, ("rows", "blk"), axis=0, tiled=True),
        lax.all_gather(w_out, ("rows", "blk"), axis=0, tiled=True),
    )
    grad_out = transposed_times(attended, d_branch_a)
    d_attended = times_transposed(d_branch_a, wout_back).astype(jnp.bfloat16)
    do_groups = split_heads(d_attended, heads)
    scale = width // heads
    scale = scale ** (-0.5)

    def backward_group(parts):
        q_grp, k_grp, v_grp, slope_grp, do_grp, lse_grp = parts
        logits = group_scores(q_grp, k_grp, slope_grp, distance, allowed)
        probs = jnp.exp(logits - lse_grp[..., None])
        dprob = jnp.einsum("gqd,gkd->gqk", do_grp, v_grp, preferred_element_type=jnp.float32)
        delta = jnp.sum(probs * dprob, -1, keepdims=True)
        dlogit = (probs * (dprob - delta)).astype(jnp.bfloat16)
        dq = jnp.einsum("gqk,gkd->gqd", dlogit, k_grp, preferred_element_type=jnp.float32) * scale
        dk = jnp.einsum("gqk,gqd->gkd", dlogit, q_grp, preferred_element_type=jnp.float32) * scale
        dv = jnp.einsum(
            "gqk,gqd->gkd", probs.astype(jnp.bfloat16), do_grp, preferred_element_type=jnp.float32
        )
        return (dq, dk, dv)

    dq_groups, dk_groups, dv_groups = lax.map(
        backward_group, (q_groups, k_groups, v_groups, slope_groups, do_groups, lse_groups)
    )
    kv_terms = jnp.concatenate([merge_heads(dk_groups), merge_heads(dv_groups)], 1)
    outward = jnp.concatenate([kv_terms[:tok_rows], kv_terms[2 * tok_rows :]], 0)
    received = extended(outward.astype(jnp.bfloat16), (("blk", 0),), tok_rows).astype(outward.dtype)
    kv_own = kv_terms[tok_rows : 2 * tok_rows] + received[:tok_rows] + received[3 * tok_rows :]
    d_qkv = jnp.concatenate(
        [merge_heads(dq_groups).astype(jnp.bfloat16), kv_own.astype(jnp.bfloat16)], 1
    )
    grad_qkv = transposed_times(inputs, d_qkv)
    tokens_grad = (d_resid_one + times_transposed(d_qkv, wqkv_back)).astype(jnp.bfloat16)[None]
    attn_sums = (
        lax.psum_scatter(lane_rows(grad_qkv), ("rows", "blk"), scatter_dimension=0, tiled=True),
        lax.psum_scatter(lane_rows(grad_out), ("rows", "blk"), scatter_dimension=0, tiled=True),
        lax.psum_scatter(d_gain_one, ("rows", "blk"), scatter_dimension=0, tiled=True),
        lax.psum_scatter(d_bias_one, ("rows", "blk"), scatter_dimension=0, tiled=True),
    )
    qkv_part = owner_rows(attn_sums[0], width, 3 * width, owners)
    out_part = owner_rows(attn_sums[1], width, width, owners)
    gate_up_part = owner_rows(ffn_sums[0], width, grad_gate_up.shape[1], owners)
    down_part = owner_rows(ffn_sums[1], grad_down.shape[0], width, owners)
    return (
        output,
        tokens_grad,
        qkv_part,
        out_part,
        attn_sums[2],
        attn_sums[3],
        gate_up_part,
        down_part,
        ffn_sums[2],
        ffn_sums[3],
        stats,
    )


def solution(mesh):
    placed = (
        P("rows", "blk", None),
        P("rows", None),
        P(("rows", "blk"), None),
        P(("rows", "blk"), None),
        P(("rows", "blk")),
        P(("rows", "blk")),
        P(("rows", "blk"), None),
        P(("rows", "blk"), None),
        P(("rows", "blk")),
        P(("rows", "blk")),
        P("rows", "blk", None),
    )
    return jax.shard_map(
        body,
        mesh=mesh,
        in_specs=placed,
        out_specs=(
            P("rows", "blk", None),
            P("rows", "blk", None),
            P(("rows", "blk"), None),
            P(("rows", "blk"), None),
            P(("rows", "blk")),
            P(("rows", "blk")),
            P(("rows", "blk"), None),
            P(("rows", "blk"), None),
            P(("rows", "blk")),
            P(("rows", "blk")),
            P(),
        ),
        check_vma=False,
    )
```

profile of v0, /device:TPU:0, one launch (start us, length us, event | category | flops | bytes accessed | tf_op | source)
XLA Modules:
  0.0 953.2 jit_solution(2447428222219007034)
XLA Ops:
  9.4 64.3 %all-gather.5.cloned.1.call-done = bf16[768,2304]{1,0:T(8,128)(2,1)} async-done(((bf16[24,2304]{1,0:T(8,128)(2,1)}), bf16[768,2304]{1,0:T(8,128)(2,1)}) %all-gather.5.cloned.1.call-update) | async-done | bytes 3538960 | tf_op jit(solution)/shard_map/all_gather | solution.py:122
  73.7 4.2 convolution_convert_fusion
  79.4 3.3 collective-permute-start
  85.1 40.9 %all-reduce.12 = (bf16[768]{0:T(1024)(128)(2,1)S(1)}, bf16[768]{0:T(1024)(128)(2,1)S(1)}, bf16[768]{0:T(1024)(128)(2,1)S(1)}, bf16[768]{0:T(1024)(128)(2,1)S(1)}) all-reduce(bf16[768]{0:T(1024)(128)(2,1)S(1)} %dynamic-update-slice.1, bf16[768]{0:T(1024)(128)(2,1)S(1)} %dynamic-update-slice, ...), channel_id=1, replica_groups=mesh['rows'=16,'blk'=2] {'rows','blk'}, use_global_device_ids=true, to_apply=%add.4 | all-reduce | flops 3072 | bytes 12288
  135.3 2.8 copy.33
  138.2 41.7 %while.30 = (s32[]{:T(128)}, bf16[6,2,512,64]{2,3,1,0:T(8,128)(2,1)S(1)}, f32[6,2,512]{2,1,0:T(2,128)S(1)}, bf16[6,2,512,64]{2,3,1,0:T(8,128)(2,1)}, bf16[6,2,15...) while((s32[]{:T(128)}, ...), condition=%wide.region_3.4_spmd.clone.clone, body=%wide.region_0.3_spmd.clone.clone.sunk | while | flops 422312960 | bytes 27979420 | solution.py:143
  139.8 3.2 fusion.140
  146.7 3.2 fusion.140
  153.7 3.2 fusion.140
  160.6 3.2 fusion.140
  167.6 3.2 fusion.140
  174.5 3.2 fusion.140
  182.1 3.9 fusion.103
  186.3 27.2 %all-gather.9.cloned.1.call-done = bf16[768,6144]{1,0:T(8,128)(2,1)} async-done(((bf16[24,6144]{1,0:T(8,128)(2,1)}), bf16[768,6144]{1,0:T(8,128)(2,1)}) %all-gather.9.cloned.1.call-update) | async-done | bytes 9437200 | tf_op jit(solution)/shard_map/all_gather | solution.py:153
  213.4 7.8 fusion.96
  221.3 4.6 copy-done.1
  225.8 15.0 %multiply_convert_fusion.1 = (bf16[512,3072]{1,0:T(8,128)(2,1)}, f32[512,3072]{1,0:T(8,128)}) fusion(f32[512,6144]{1,0:T(8,128)S(1)} %fusion.96), kind=kLoop, calls=%fused_computation.71 | loop fusion | flops 103809024 | bytes 22020096 | tf_op jit(solution)/shard_map/convert_element_type | solution.py:160
  240.8 37.7 %all-gather.11.cloned.1.call-done = bf16[3072,768]{1,0:T(8,128)(2,1)} async-done(((bf16[96,768]{1,0:T(8,128)(2,1)}), bf16[3072,768]{1,0:T(8,128)(2,1)}) %all-gather.11.cloned.1.call-update) | async-done | bytes 4718608 | tf_op jit(solution)/shard_map/all_gather | solution.py:154
  278.5 7.2 fusion.100
  288.9 12.0 %fusion.66 = (f32[512,3072]{1,0:T(8,128)}, f32[512,3072]{1,0:T(8,128)}) fusion(f32[512,3072]{1,0:T(8,128)S(1)} %copy-done.6, f32[512,6144]{1,0:T(8,128)} %copy-done.1, bf16[3072,768]{1,0:T(8,128)(2,1)} %all-gather.11.cloned.1.call-done, f32[512,768]{1,0:T(8,128)S(1)} %get-tuple-element.358, f32[512]{0:T(512)S(1)} %negate_multiply_fusion.2), kind=kOutput, calls=%fused_computation.101 | convolution fusion | flops 2441871360 | bytes 37750784 | tf_op jit(solution)/shard_map/dot_general | solution.py:55
  300.9 14.7 %multiply_reduce_fusion.1 = (f32[768]{0:T(1024)}, f32[512]{0:T(512)S(1)}, f32[]{:T(128)}, f32[768]{0:T(1024)}, f32[]{:T(128)}, /*index=5*/f32[]{:T(128)}, f32[]{:T(128)}, f32[512,768]{1,0:T(8,128)}) fusion(f32[512,768]{1,0:T(8,128)S(1)} %get-tuple-element.364, f32[512]{0:T(512)S(1)} %fusion.86, f32[512]{0:T(512)S(1)} %broadcast_multiply_fusion.1, ...), kind=kOutput, calls=%fused_computation.118 | convolution fusion | flops 4847958016 | bytes 30693392 | tf_op jit(solution)/shard_map/dot_general | solution.py:55
  321.2 3.3 reshape.211
  324.6 3.1 convolution_convert_fusion.1
  331.0 96.8 %while.31 = (s32[]{:T(128)}, bf16[6,2,512,64]{2,3,1,0:T(8,128)(2,1)}, f32[6,2,1536,64]{2,3,1,0:T(8,128)}, f32[6,2,1536,64]{2,3,1,0:T(8,128)}, bf16[6,2,512,64]{2...) while((s32[]{:T(128)}, ...), condition=%wide.region_14.15_spmd.clone.clone, body=%wide.region_12.14_spmd.clone.clone.sunk | while | flops 1029700608 | bytes 58641076 | solution.py:216
  334.6 4.2 multiply_reduce_fusion.6
  344.4 2.7 fusion.152
  350.8 4.2 multiply_reduce_fusion.6
  366.9 4.2 multiply_reduce_fusion.6
  376.7 2.7 fusion.152
  383.0 4.2 multiply_reduce_fusion.6
  392.8 2.7 fusion.152
  399.2 4.2 multiply_reduce_fusion.6
  408.9 2.7 fusion.152
  415.3 4.2 multiply_reduce_fusion.6
  427.8 6.7 fusion.54
  444.3 3.7 fusion.65
  449.2 6.1 convolution_bitcast_fusion
  455.4 8.0 copy.35
  463.4 7.9 reshape.209
  471.4 8.7 fusion.92
  480.1 11.0 %reshape.215 = f32[18432,128]{1,0:T(8,128)} reshape(f32[3072,768]{1,0:T(8,128)} %fusion.92) | data formatting | bytes 18874368 | tf_op jit(solution)/shard_map/reshape | solution.py:79
  491.1 14.6 %fusion.79 = f32[768,6144]{1,0:T(8,128)} fusion(f32[512,3072]{1,0:T(8,128)} %get-tuple-element.372, f32[512,3072]{1,0:T(8,128)} %get-tuple-element.371, f32[512,768]{1,0:T(8,128)S(1)} %get-tuple-element.364, f32[768]{0:T(1024)S(1)} %convert_element_type.106, f32[768]{0:T(1024)S(1)} %convert_element_type.105, f32[512]{0:T(512)S(1)} %fusion.86, ...), kind=kOutput, calls=%fused_computation.131 | convolution fusion | flops 4840095744 | bytes 33040384 | tf_op jit(solution)/shard_map/dot_general | solution.py:61
  505.7 19.5 %reshape.213 = f32[36864,128]{1,0:T(8,128)} reshape(f32[768,6144]{1,0:T(8,128)} %fusion.79) | data formatting | bytes 37748736 | tf_op jit(solution)/shard_map/reshape | solution.py:79
  529.2 40.9 %all-reduce.11 = (f32[768]{0:T(1024)S(1)}, f32[768]{0:T(1024)S(1)}, f32[768]{0:T(1024)S(1)}, f32[768]{0:T(1024)S(1)}, f32[4]{0:T(128)S(1)}, /*index=5*/f32[]{:T(128)}) all-reduce(f32[768]{0:T(1024)S(1)} %copy-done.17, f32[768]{0:T(1024)S(1)} %copy-done.18, ...), channel_id=4, replica_groups=mesh['rows'=16,'blk'=2] {'rows','blk'}, use_global_device_ids=true, to_apply=%region_18.19.clone | all-reduce | flops 3077 | bytes 24616
  573.6 5.7 fusion.78
  580.8 9.3 reduce-scatter.5.cloned.1.call-done
  591.7 139.2 %reduce-scatter.11.cloned.1.call-done = f32[576,128]{1,0:T(8,128)} async-done(((f32[18432,128]{1,0:T(8,128)}), f32[576,128]{1,0:T(8,128)}) %reduce-scatter.11.cloned.1.call-update) | async-done | bytes 294928 | tf_op jit(solution)/shard_map/reduce_scatter | solution.py:186
  732.7 211.5 %reduce-scatter.9.cloned.1.call-done = f32[1152,128]{1,0:T(8,128)} async-done(((f32[36864,128]{1,0:T(8,128)}), f32[1152,128]{1,0:T(8,128)}) %reduce-scatter.9.cloned.1.call-update) | async-done | bytes 589840 | tf_op jit(solution)/shard_map/reduce_scatter | solution.py:185
  (217 shorter events, 137.3 us)
Async XLA Ops:
  7.2 66.5 %all-gather.5.cloned.1.call-start = ((), (), s32[]{:S(2)}) async-start(), calls=%async_computation.4 | async-start | bytes 3649536 | tf_op jit(solution)/shard_map/all_gather | solution.py:122
  7.9 172.1 %all-gather.7.cloned.1.call-start = ((), (), s32[]{:S(2)}) async-start(), calls=%async_computation.5 | async-start | bytes 1216512 | tf_op jit(solution)/shard_map/all_gather | solution.py:123
  8.7 204.8 %all-gather.9.cloned.1.call-start = ((), (), s32[]{:S(2)}) async-start(), calls=%async_computation.6 | async-start | bytes 9732096 | tf_op jit(solution)/shard_map/all_gather | solution.py:153
  9.4 269.1 %all-gather.11.cloned.1.call-start = ((), (), s32[]{:S(2)}) async-start(), calls=%async_computation.7 | async-start | bytes 4866048 | tf_op jit(solution)/shard_map/all_gather | solution.py:154
  78.0 1.4 copy-start.9
  78.0 6.2 copy-start.19
  78.0 6.4 copy-start.20
  78.0 6.6 copy-start.21
  78.0 6.9 copy-start.22
  78.0 48.0 %copy-start.16 = (s32[1,1024]{1,0:T(1,128)S(1)}, s32[1,1024]{1,0:T(1,128)}, u32[]{:S(2)}) copy-start(s32[1,1024]{1,0:T(1,128)} %param.16) | copy-start | bytes 12292
  79.4 49.7 %collective-permute-start = (bf16[512,1536]{1,0:T(8,128)(2,1)S(1)}, bf16[512,1536]{1,0:T(8,128)(2,1)}, u32[]{:S(2)}, u32[]{:S(2)}) collective-permute-start(bf16[512,1536]{1,0:T(8,128)(2,1)S(1)} %slice.49), channel_id=1, source_target_pairs={{0,1},{2,3},{4,5},{6,7},{8,9},{10,11},{12,13},{14,15},{16,17},{18,... | collective-permute-start | bytes 4718600 | tf_op jit(solution)/shard_map/ppermute | solution.py:23
  82.7 46.3 %collective-permute-start.1 = (bf16[512,1536]{1,0:T(8,128)(2,1)S(1)}, bf16[512,1536]{1,0:T(8,128)(2,1)}, u32[]{:S(2)}, u32[]{:S(2)}) collective-permute-start(bf16[512,1536]{1,0:T(8,128)(2,1)S(1)} %slice.49), channel_id=1, source_target_pairs={{1,0},{3,2},{5,4},{7,6},{9,8},{11,10},{13,12},{15,14},{17,16},{19,... | collective-permute-start | bytes 4718600 | tf_op jit(solution)/shard_map/ppermute | solution.py:25
  84.0 495.2 %reduce-scatter.7.cloned.1.call-start = ((), (), s32[]{:S(2)}) async-start(), calls=%async_computation.9 | async-start | bytes 2433024 | tf_op jit(solution)/shard_map/reduce_scatter | solution.py:230
  180.0 1.6 copy-start
  180.0 2.1 copy-start.4
  221.3 4.6 copy-start.1
  278.5 7.5 copy-start.2
  286.0 2.9 copy-start.6
  288.9 12.0 %copy-start.11 = (f32[512,768]{1,0:T(8,128)}, f32[512,768]{1,0:T(8,128)S(1)}, u32[]{:S(2)}) copy-start(f32[512,768]{1,0:T(8,128)S(1)} %get-tuple-element.358) | copy-start | bytes 4718596
  288.9 12.0 %copy-start.13 = (bf16[1,512,768]{2,1,0:T(8,128)(2,1)S(1)}, bf16[1,512,768]{2,1,0:T(8,128)(2,1)}, u32[]{:S(2)}) copy-start(bf16[1,512,768]{2,1,0:T(8,128)(2,1)} %param.15) | copy-start | bytes 2359300
  315.6 3.3 copy-start.5
  317.7 1.2 copy-start.7
  321.2 3.4 copy-start.12
  324.5 265.5 %reduce-scatter.5.cloned.1.call-start = ((), (), s32[]{:S(2)}) async-start(), calls=%async_computation.8 | async-start | bytes 7299072 | tf_op jit(solution)/shard_map/reduce_scatter | solution.py:229
  427.8 16.5 %slice-start = ((s8[4718592]{0:T(1024)(128)(4,1)}), s8[4194304]{0:T(1024)(128)(4,1)S(1)}, s32[]{:S(2)}) async-start(s8[4718592]{0:T(1024)(128)(4,1)} %bitcast.175), calls=%async_computation.12 | async-start | bytes 8388608
  427.8 16.5 %slice-start.1 = ((s8[4718592]{0:T(1024)(128)(4,1)}), s8[524288]{0:T(1024)(128)(4,1)S(1)}, s32[]{:S(2)}) async-start(s8[4718592]{0:T(1024)(128)(4,1)} %bitcast.175), calls=%async_computation.13 | async-start | bytes 1048576
  436.6 5.2 collective-permute-start.2
  438.8 10.4 %copy-start.14 = (bf16[1,512,768]{2,1,0:T(8,128)(2,1)S(1)}, bf16[1,512,768]{2,1,0:T(8,128)(2,1)}, u32[]{:S(2)}) copy-start(bf16[1,512,768]{2,1,0:T(8,128)(2,1)} %param.15) | copy-start | bytes 2359300
  438.9 5.4 collective-permute-start.3
  448.0 1.2 copy-start.10
  471.3 259.6 %reduce-scatter.11.cloned.1.call-start = ((), (), s32[]{:S(2)}) async-start(), calls=%async_computation.11 | async-start | bytes 9732096 | tf_op jit(solution)/shard_map/reduce_scatter | solution.py:186
  491.1 453.1 %reduce-scatter.9.cloned.1.call-start = ((), (), s32[]{:S(2)}) async-start(), calls=%async_computation.10 | async-start | bytes 19464192 | tf_op jit(solution)/shard_map/reduce_scatter | solution.py:185
  525.2 1.1 copy-start.3
  525.2 3.9 copy-start.15
  525.2 3.9 copy-start.17
  525.2 3.9 copy-start.18
  525.2 48.4 %copy-start.8 = (f32[512,768]{1,0:T(8,128)S(1)}, f32[512,768]{1,0:T(8,128)}, u32[]{:S(2)}) copy-start(f32[512,768]{1,0:T(8,128)} %copy-done.7) | copy-start | bytes 4718596
Sparse Core Ops, SparseCore 0:
  10.9 62.7 all-gather.4
  76.6 52.9 all-gather.6
  132.5 80.8 all-gather.8
  216.2 62.2 all-gather.10
  324.7 97.9 reduce-scatter.6
  471.4 118.5 reduce-scatter.4
  596.0 134.9 reduce-scatter.10
  738.5 205.6 reduce-scatter.8
where the time goes:
time: 959 us; the launch traced here: 953 us
  waiting for transfers between devices  495 us (52%)
  matrix products  200 us (21%)
  local copies, waits for them, and re-layouts  86.4 us (9%)
  blocking collectives  81.8 us (9%)
  other arithmetic  64.7 us (7%)
  between operations  15.4 us (2%)
    reduce_scatter x1, waiting for transfers between devices, body(): lax.psum_scatter(lane_rows(grad_gate_up), ('rows', 'blk'), scatter_dimens...  211 us
    reduce_scatter x1, waiting for transfers between devices, body(): lax.psum_scatter(lane_rows(grad_down), ('rows', 'blk'), scatter_dimension...  139 us
    unnamed x2, blocking collectives  81.8 us
    all_gather x1, waiting for transfers between devices, body(): lax.all_gather(w_qkv, ('rows', 'blk'), axis=0, tiled=True)  64.3 us
    dot_general x12, matrix products, group_scores(): jnp.einsum('gqd,gkd->gqk', q_grp, k_grp, preferred_element_type=jnp.float32)  44.4 us
    reshape x4, local copies, waits for them, and re-layouts, lane_rows(): return matrix.reshape(-1, lane_width)  41.7 us
    all_gather x1, waiting for transfers between devices, body(): lax.all_gather(w_down, ('rows', 'blk'), axis=0, tiled=True)  37.7 us
    dot_general x4, matrix products, times_transposed(): lax.dot_general(left, right, (((1,), (1,)), ((), ())), preferred_element_...  35.4 us
  transfers between devices with their start and end apart: 12, of which 8 were waited for; matrix products, arithmetic and copies ran while one was open for 31% of the time, Pallas kernels for 0%

commit v1 on v0

--- a/solution.py
+++ b/solution.py
@@ -1,7 +1,397 @@
 import jax
 import jax.numpy as jnp
 from jax import lax
+from jax.experimental import pallas as pl
+from jax.experimental.pallas import tpu as pltpu
 from jax.sharding import PartitionSpec as P
+
+MESH = pl.DeviceIdType.MESH
+
+
+class Place:
+    def __init__(self):
+        r, self.c = lax.axis_index("rows"), lax.axis_index("blk")
+        self.x, self.y, self.z = r % 2, (r // 2) % 2, r // 4
+        self.sib = (r, 1 - self.c)
+        self.xn = (self.at(0, "x"), self.c)
+        self.yn = (self.at(0, "y"), self.c)
+        self.zn = {k: (self.at(k, "o"), self.c) for k in (1, 2, 3)}
+
+    def plane(self, k):
+        z, low = self.z % 2, self.z // 2
+        if k % 2:
+            z = 1 - z
+        if k // 2:
+            low = 1 - low
+        return low * 2 + z
+
+    def at(self, k, j):
+        x = 1 - self.x if j in "xd" else self.x
+        y = 1 - self.y if j in "yd" else self.y
+        return self.plane(k) * 4 + y * 2 + x
+
+    def greet(self):
+        barrier = pltpu.get_barrier_semaphore()
+        peers = [self.sib, self.xn, self.yn] + [self.zn[k] for k in (1, 2, 3)]
+        for peer in peers:
+            pl.semaphore_signal(barrier, inc=1, device_id=peer, device_id_type=MESH)
+        pl.semaphore_wait(barrier, len(peers))
+
+
+class Copies:
+    def __init__(self, send, recv):
+        self.send, self.recv, self.open = send, recv, []
+
+    def put(self, src, dst, slot, peer):
+        copy = pltpu.make_async_remote_copy(
+            src_ref=src, dst_ref=dst, send_sem=self.send.at[slot], recv_sem=self.recv.at[slot],
+            device_id=peer, device_id_type=MESH,
+        )
+        copy.start()
+        self.open.append(copy)
+
+    def got(self, dst, slot, peer):
+        pltpu.make_async_remote_copy(
+            src_ref=dst, dst_ref=dst, send_sem=self.send.at[slot], recv_sem=self.recv.at[slot],
+            device_id=peer, device_id_type=MESH,
+        ).wait_recv()
+
+    def drain(self):
+        for copy in self.open:
+            copy.wait_send()
+        self.open = []
+
+
+class Gather:
+    def __init__(self, place, copies, base, own, out):
+        self.p, self.cp, self.base, self.own, self.out = place, copies, base, own, out
+
+    def slot(self, kind, k, j="o"):
+        start = {"z": -1, "x": 3, "y": 7, "d": 11, "s": 15}[kind]
+        return self.base + start + (4 * k + "oxyd".index(j) if kind == "s" else k)
+
+    def block(self, k, j):
+        return self.out(self.p.c, self.p.at(k, j))
+
+    def push(self, src, k, j):
+        self.cp.put(src, self.block(k, j), self.slot("s", k, j), self.p.sib)
+
+    def own_z(self):
+        for k in (1, 2, 3):
+            self.cp.put(self.own, self.block(0, "o"), self.slot("z", k), self.p.zn[k])
+
+    def own_xy(self):
+        self.spread(self.own, 0)
+
+    def spread(self, src, k):
+        dst = self.block(k, "o")
+        self.cp.put(src, dst, self.slot("x", k), self.p.xn)
+        self.cp.put(src, dst, self.slot("y", k), self.p.yn)
+        self.push(src, k, "o")
+
+    def from_z(self, k):
+        block = self.block(k, "o")
+        self.cp.got(block, self.slot("z", k), self.p.zn[k])
+        self.spread(block, k)
+
+    def from_xy(self, k):
+        x, y = self.block(k, "x"), self.block(k, "y")
+        self.cp.got(x, self.slot("x", k), self.p.xn)
+        if k >= 2:
+            self.cp.put(x, x, self.slot("d", k), self.p.yn)
+        self.push(x, k, "x")
+        self.cp.got(y, self.slot("y", k), self.p.yn)
+        if k < 2:
+            self.cp.put(y, y, self.slot("d", k), self.p.xn)
+        self.push(y, k, "y")
+
+    def from_d(self, k):
+        block = self.block(k, "d")
+        self.cp.got(block, self.slot("d", k), self.p.xn)
+        self.push(block, k, "d")
+
+    def from_sib(self):
+        for k in range(4):
+            for j in "oxyd":
+                block = self.out(1 - self.p.c, self.p.at(k, j))
+                self.cp.got(block, self.slot("s", k, j), self.p.sib)
+
+
+def low_add(left, right):
+    return left + right
+
+
+class Scatter:
+    def __init__(self, place, copies, base, local, grad, own, sib, rly, xin, yin, out, zin):
+        self.p, self.cp, self.base, self.local, self.grad = place, copies, base, local, grad
+        self.own, self.sib, self.rly, self.xin, self.yin, self.out, self.zin = own, sib, rly, xin, yin, out, zin
+
+    def slot(self, kind, k):
+        return self.base + {"s": 0, "r": 4, "x": 8, "y": 12, "z": 15}[kind] + k
+
+    def load(self, k):
+        four = pl.ds(self.p.plane(k) * 4, 4)
+        return pltpu.make_async_copy(self.grad(self.p.c, four), self.own.at[four], self.local.at[self.base + k])
+
+    def begin(self, k):
+        four = pl.ds(self.p.plane(k) * 4, 4)
+        self.cp.put(self.grad(1 - self.p.c, four), self.sib.at[four], self.slot("s", k), self.p.sib)
+        self.load(k).start()
+
+    def pair(self, k):
+        p = self.p
+        four = pl.ds(p.plane(k) * 4, 4)
+        self.load(k).wait()
+        self.cp.got(self.sib.at[four], self.slot("s", k), p.sib)
+        d, x, y = p.at(k, "d"), p.at(k, "x"), p.at(k, "y")
+        self.own[d] = low_add(self.own[d], self.sib[d])
+        self.cp.put(self.own.at[d], self.rly.at[k], self.slot("r", k), p.xn if k < 2 else p.yn)
+        if k < 2:
+            self.own[x] = low_add(self.own[x], self.sib[x])
+            self.cp.put(self.own.at[x], self.xin.at[k], self.slot("x", k), p.xn)
+        else:
+            self.own[y] = low_add(self.own[y], self.sib[y])
+            self.cp.put(self.own.at[y], self.yin.at[k], self.slot("y", k), p.yn)
+
+    def relay(self, k):
+        p = self.p
+        x, y = p.at(k, "x"), p.at(k, "y")
+        self.cp.got(self.rly.at[k], self.slot("r", k), p.xn)
+        if k < 2:
+            self.own[y] = low_add(low_add(self.own[y], self.sib[y]), self.rly[k])
+            self.cp.put(self.own.at[y], self.yin.at[k], self.slot("y", k), p.yn)
+        else:
+            self.own[x] = low_add(low_add(self.own[x], self.sib[x]), self.rly[k])
+            self.cp.put(self.own.at[x], self.xin.at[k], self.slot("x", k), p.xn)
+
+    def plane(self, k):
+        p = self.p
+        o = p.at(k, "o")
+        self.cp.got(self.xin.at[k], self.slot("x", k), p.xn)
+        self.cp.got(self.yin.at[k], self.slot("y", k), p.yn)
+        wide = jnp.float32
+        total = (self.own[o].astype(wide) + self.sib[o].astype(wide)) + (
+            self.xin[k].astype(wide) + self.yin[k].astype(wide)
+        )
+        self.out[k] = total.astype(jnp.bfloat16)
+        if k:
+            self.cp.put(self.out.at[k], self.zin.at[k - 1], self.slot("z", k), p.zn[k])
+
+    def total(self):
+        for k in (1, 2, 3):
+            self.cp.got(self.zin.at[k - 1], self.slot("z", k), self.p.zn[k])
+        wide = jnp.float32
+        return (self.out[0].astype(wide) + self.zin[0].astype(wide)) + (
+            self.zin[1].astype(wide) + self.zin[2].astype(wide)
+        )
+
+
+rows_chip = 48
+gather_slots, scatter_slots = 31, 19
+
+
+def gather_kernel(a_shard, g_shard, d_own, a_full, g_full, d_full, a_pair, g_pair, a_own, g_own, pair_sem, send, recv, local):
+    place = Place()
+    place.greet()
+    c = place.c
+    pairs = Copies(pair_sem.at[0], pair_sem.at[1])
+    for i, (shard, other) in enumerate(((a_shard, a_pair), (g_shard, g_pair))):
+        pairs.put(shard.at[1 - c], other, i, place.sib)
+    copies = Copies(send, recv)
+    a_out = lambda half, r: a_full.at[half, r]
+    g_out = lambda half, r: g_full.at[half, r]
+    d_out = lambda half, r: d_full.at[r, half]
+    mats = [
+        Gather(place, copies, 0, a_own, a_out),
+        Gather(place, copies, gather_slots, g_own, g_out),
+        Gather(place, copies, 2 * gather_slots, d_own, d_out),
+    ]
+    att, gat, dow = mats
+
+    def assemble(shard, other, own, i):
+        pairs.got(other, i, place.sib)
+        mine = shard[c, :24, :].astype(jnp.float32)
+        theirs = other[:24, :].astype(jnp.float32)
+        first = c == 0
+        top = jnp.where(first, mine, theirs)
+        low = jnp.where(first, theirs, mine)
+        own[...] = jnp.concatenate([top, low], 0).astype(jnp.bfloat16)
+
+    kept = [pltpu.make_async_copy(m.own, m.block(0, "o"), local.at[i]) for i, m in enumerate(mats)]
+    assemble(a_shard, a_pair, a_own, 0)
+    att.own_z()
+    att.own_xy()
+    kept[0].start()
+    assemble(g_shard, g_pair, g_own, 1)
+    gat.own_z()
+    dow.own_z()
+    kept[1].start()
+    kept[2].start()
+    for k in (1, 2, 3):
+        att.from_z(k)
+    for k in range(4):
+        att.from_xy(k)
+    gat.own_xy()
+    for k in (1, 2, 3):
+        gat.from_z(k)
+    for k in range(4):
+        att.from_d(k)
+    for k in range(4):
+        gat.from_xy(k)
+    dow.own_xy()
+    for k in (1, 2, 3):
+        dow.from_z(k)
+    for k in range(4):
+        gat.from_d(k)
+    for k in range(4):
+        dow.from_xy(k)
+    for k in range(4):
+        dow.from_d(k)
+    for m in mats:
+        m.from_sib()
+    for copy in kept:
+        copy.wait()
+    pairs.drain()
+    copies.drain()
+
+
+def gather_weights(a_shard, g_shard, d_shard):
+    half_a, half_g = a_shard.shape[-1], g_shard.shape[-1]
+    low = jnp.bfloat16
+    return pl.pallas_call(
+        gather_kernel,
+        out_shape=(
+            jax.ShapeDtypeStruct((2, 16, rows_chip, half_a), low),
+            jax.ShapeDtypeStruct((2, 16, rows_chip, half_g), low),
+            jax.ShapeDtypeStruct((16, 2) + d_shard.shape, low),
+        ),
+        in_specs=[pl.BlockSpec(memory_space=pltpu.VMEM)] * 3,
+        out_specs=(pl.BlockSpec(memory_space=pl.ANY),) * 3,
+        scratch_shapes=[
+            pltpu.VMEM(a_shard.shape[1:], low),
+            pltpu.VMEM(g_shard.shape[1:], low),
+            pltpu.VMEM((rows_chip, half_a), low),
+            pltpu.VMEM((rows_chip, half_g), low),
+            pltpu.SemaphoreType.DMA((2, 2)),
+            pltpu.SemaphoreType.DMA((3 * gather_slots,)),
+            pltpu.SemaphoreType.DMA((3 * gather_slots,)),
+            pltpu.SemaphoreType.DMA((3,)),
+        ],
+        compiler_params=pltpu.CompilerParams(
+            collective_id=0, has_side_effects=True, vmem_limit_bytes=32 * 2**20
+        ),
+        name="gather_weights",
+    )(a_shard, g_shard, d_shard)
+
+
+def scatter_kernel(
+    a_grad, g_grad, d_grad, small, qkv_out, wout_out, gu_out, down_out, small_out, *scratch
+):
+    place = Place()
+    place.greet()
+    c = place.c
+    bufs, (a_sum, g_sum, a_fin, g_fin, small_buf, send, recv, local, fin_sem) = scratch[:21], scratch[21:]
+    copies = Copies(send, recv)
+    last = Copies(fin_sem.at[0], fin_sem.at[1])
+    a_at = lambda half, four: a_grad.at[half, four]
+    g_at = lambda half, four: g_grad.at[half, four]
+    d_at = lambda half, four: d_grad.at[four, half]
+    mats = [
+        Scatter(place, copies, i * scatter_slots, local, at, *bufs[7 * i : 7 * i + 7])
+        for i, at in enumerate((g_at, d_at, a_at))
+    ]
+    order = [(m, k) for m in mats for k in (3, 2, 1, 0)]
+    depth = 3
+    steps = ["begin", "pair", "relay", "plane"]
+    hops = ((place.sib, 0), (place.xn, 1), (place.yn, 2))
+
+    def exchange(i):
+        peer, slot = hops[i]
+        last.put(small_buf.at[i], small_buf.at[4 + i], slot, peer)
+
+    def combine(i):
+        peer, slot = hops[i]
+        last.got(small_buf.at[4 + i], slot, peer)
+        small_buf[i + 1] = small_buf[i] + small_buf[4 + i]
+
+    small_buf[0] = small[...]
+    exchange(0)
+    for t in range(len(order) + depth):
+        for s, name in enumerate(steps):
+            if 0 <= t - s < len(order):
+                m, k = order[t - s]
+                getattr(m, name)(k)
+        if 1 <= t <= 3:
+            combine(t - 1)
+            if t < 3:
+                exchange(t)
+            else:
+                for k in (1, 2, 3):
+                    last.put(small_buf.at[3], small_buf.at[6 + k], 2 + k, place.zn[k])
+    for k in (1, 2, 3):
+        last.got(small_buf.at[6 + k], 2 + k, place.zn[k])
+    small_out[...] = (small_buf[3] + small_buf[7]) + (small_buf[8] + small_buf[9])
+    gate, down, att = mats
+    down_out[...] = down.total()
+    g_sum[...] = gate.total()
+    mine, theirs = pl.ds(pl.multiple_of(24 * c, 8), 24), pl.ds(pl.multiple_of(24 - 24 * c, 8), 24)
+    last.put(g_sum.at[theirs], g_fin, 6, place.sib)
+    a_sum[...] = att.total()
+    last.put(a_sum.at[theirs], a_fin, 7, place.sib)
+    first = c == 0
+    last.got(g_fin, 6, place.sib)
+    last.got(a_fin, 7, place.sib)
+    half_g = g_fin.shape[1]
+    gu_out[:, :half_g] = jnp.where(first, g_sum[mine], g_fin[...])
+    gu_out[:, half_g:] = jnp.where(first, g_fin[...], g_sum[mine])
+    left = jnp.where(first, a_sum[mine], a_fin[...])
+    right = jnp.where(first, a_fin[...], a_sum[mine])
+    cut = qkv_out.shape[1] - left.shape[1]
+    qkv_out[:, : left.shape[1]] = left
+    qkv_out[:, left.shape[1] :] = right[:, :cut]
+    wout_out[...] = right[:, cut:]
+    copies.drain()
+    last.drain()
+
+
+def scatter_grads(a_grad, g_grad, d_grad, small):
+    low = jnp.bfloat16
+    bufs = []
+    for rows, half in ((rows_chip, g_grad.shape[-1]), d_grad.shape[2:], (rows_chip, a_grad.shape[-1])):
+        for count in (16, 16, 4, 4, 4, 4, 3):
+            bufs.append(pltpu.VMEM((count, rows, half), low))
+    half_a, half_g = a_grad.shape[-1], g_grad.shape[-1]
+    width = d_grad.shape[-1]
+    wide = jnp.float32
+    return pl.pallas_call(
+        scatter_kernel,
+        out_shape=(
+            jax.ShapeDtypeStruct((24, 3 * width), wide),
+            jax.ShapeDtypeStruct((24, width), wide),
+            jax.ShapeDtypeStruct((24, 2 * half_g), wide),
+            jax.ShapeDtypeStruct(d_grad.shape[2:], wide),
+            jax.ShapeDtypeStruct(small.shape, wide),
+        ),
+        in_specs=[pl.BlockSpec(memory_space=pl.ANY)] * 3 + [pl.BlockSpec(memory_space=pltpu.VMEM)],
+        out_specs=(pl.BlockSpec(memory_space=pltpu.VMEM),) * 5,
+        scratch_shapes=bufs
+        + [
+            pltpu.VMEM((rows_chip, half_a), wide),
+            pltpu.VMEM((rows_chip, half_g), wide),
+            pltpu.VMEM((24, half_a), wide),
+            pltpu.VMEM((24, half_g), wide),
+            pltpu.VMEM((10,) + small.shape, wide),
+            pltpu.SemaphoreType.DMA((3 * scatter_slots,)),
+            pltpu.SemaphoreType.DMA((3 * scatter_slots,)),
+            pltpu.SemaphoreType.DMA((3 * scatter_slots,)),
+            pltpu.SemaphoreType.DMA((2, 8)),
+        ],
+        compiler_params=pltpu.CompilerParams(
+            collective_id=1, has_side_effects=True, vmem_limit_bytes=60 * 2**20
+        ),
+        name="scatter_grads",
+    )(a_grad, g_grad, d_grad, small)
+
 
 HEADS = 12
 
@@ -118,12 +508,8 @@
     slope_groups = head_slopes(heads).reshape(heads // group_heads, group_heads)
     allowed = permitted(query_labels, window_labels, query_pos, window_pos, seq_len)
     distance = jnp.abs(query_pos[:, None] - window_pos[None, :]).astype(jnp.float32)
-    wqkv_full, wout_full, gain_one, bias_one = (
-        lax.all_gather(w_qkv, ("rows", "blk"), axis=0, tiled=True),
-        lax.all_gather(w_out, ("rows", "blk"), axis=0, tiled=True),
-        lax.all_gather(ln1_gain, ("rows", "blk"), axis=0, tiled=True),
-        lax.all_gather(ln1_bias, ("rows", "blk"), axis=0, tiled=True),
-    )
+    gathered = gathered_weights(w_qkv, w_out, ln1_gain, ln1_bias, w_gate_up, w_down, ln2_gain, ln2_bias)
+    wqkv_full, wout_full, wgu_full, wdown_full, gain_one, bias_one, gain_two, bias_two = gathered
     qkv = jnp.dot(inputs, wqkv_full, preferred_element_type=jnp.float32).astype(jnp.bfloat16)
     query = qkv[:, :width]
     window_kv = extended(qkv[:, width:], (("blk", 0),), tok_rows)
@@ -149,12 +535,6 @@
         layer_norm, resid_one, gain_one.astype(jnp.float32), bias_one.astype(jnp.float32)
     )
     hidden1_low = hidden1.astype(jnp.bfloat16)
-    wgu_full, wdown_full, gain_two, bias_two = (
-        lax.all_gather(w_gate_up, ("rows", "blk"), axis=0, tiled=True),
-        lax.all_gather(w_down, ("rows", "blk"), axis=0, tiled=True),
-        lax.all_gather(ln2_gain, ("rows", "blk"), axis=0, tiled=True),
-        lax.all_gather(ln2_bias, ("rows", "blk"), axis=0, tiled=True),
-    )
     gate_up = jnp.dot(hidden1_low, wgu_full, preferred_element_type=jnp.float32)
     act, glu_back = jax.vjp(geglu, gate_up)
     act_low = act.astype(jnp.bfloat16)
@@ -167,32 +547,17 @@
     squares = jnp.stack(
         [jnp.sum(valid * term * term) for term in (inputs_float, branch_a, hidden1, branch_f)]
     )
-    square_sums, valid_count = lax.psum((squares, jnp.sum(valid)), ("rows", "blk"))
-    stats = jnp.sqrt(square_sums / (valid_count * width))
     d_resid_two, d_gain_two, d_bias_two = norm_two_back(out_grad[0].astype(jnp.float32))
     d_branch_f = d_resid_two.astype(jnp.bfloat16)
-    wgu_back, wdown_back = (
-        lax.all_gather(w_gate_up, ("rows", "blk"), axis=0, tiled=True),
-        lax.all_gather(w_down, ("rows", "blk"), axis=0, tiled=True),
-    )
+    wgu_back, wdown_back, wqkv_back, wout_back = wgu_full, wdown_full, wqkv_full, wout_full
     d_act = times_transposed(d_branch_f, wdown_back)
     (d_gate_up,) = glu_back(d_act)
     d_gate_up_low = d_gate_up.astype(jnp.bfloat16)
     grad_down = transposed_times(act_low, d_branch_f)
     grad_gate_up = transposed_times(hidden1_low, d_gate_up_low)
     d_hidden1 = d_resid_two + times_transposed(d_gate_up_low, wgu_back)
-    ffn_sums = (
-        lax.psum_scatter(lane_rows(grad_gate_up), ("rows", "blk"), scatter_dimension=0, tiled=True),
-        lax.psum_scatter(lane_rows(grad_down), ("rows", "blk"), scatter_dimension=0, tiled=True),
-        lax.psum_scatter(d_gain_two, ("rows", "blk"), scatter_dimension=0, tiled=True),
-        lax.psum_scatter(d_bias_two, ("rows", "blk"), scatter_dimension=0, tiled=True),
-    )
     d_resid_one, d_gain_one, d_bias_one = norm_one_back(d_hidden1)
     d_branch_a = d_resid_one.astype(jnp.bfloat16)
-    wqkv_back, wout_back = (
-        lax.all_gather(w_qkv, ("rows", "blk"), axis=0, tiled=True),
-        lax.all_gather(w_out, ("rows", "blk"), axis=0, tiled=True),
-    )
     grad_out = transposed_times(attended, d_branch_a)
     d_attended = times_transposed(d_branch_a, wout_back).astype(jnp.bfloat16)
     do_groups = split_heads(d_attended, heads)
@@ -225,29 +590,73 @@
     )
     grad_qkv = transposed_times(inputs, d_qkv)
     tokens_grad = (d_resid_one + times_transposed(d_qkv, wqkv_back)).astype(jnp.bfloat16)[None]
-    attn_sums = (
-        lax.psum_scatter(lane_rows(grad_qkv), ("rows", "blk"), scatter_dimension=0, tiled=True),
-        lax.psum_scatter(lane_rows(grad_out), ("rows", "blk"), scatter_dimension=0, tiled=True),
-        lax.psum_scatter(d_gain_one, ("rows", "blk"), scatter_dimension=0, tiled=True),
-        lax.psum_scatter(d_bias_one, ("rows", "blk"), scatter_dimension=0, tiled=True),
-    )
-    qkv_part = owner_rows(attn_sums[0], width, 3 * width, owners)
-    out_part = owner_rows(attn_sums[1], width, width, owners)
-    gate_up_part = owner_rows(ffn_sums[0], width, grad_gate_up.shape[1], owners)
-    down_part = owner_rows(ffn_sums[1], grad_down.shape[0], width, owners)
+    parts, vectors, square_sums, valid_count = summed_grads(
+        grad_qkv, grad_out, grad_gate_up, grad_down,
+        (d_gain_one, d_bias_one, d_gain_two, d_bias_two), squares, jnp.sum(valid),
+    )
+    stats = jnp.sqrt(square_sums / (valid_count * width))
     return (
-        output,
-        tokens_grad,
-        qkv_part,
-        out_part,
-        attn_sums[2],
-        attn_sums[3],
-        gate_up_part,
-        down_part,
-        ffn_sums[2],
-        ffn_sums[3],
-        stats,
-    )
+        output, tokens_grad, parts[0], parts[1], vectors[0], vectors[1],
+        parts[2], parts[3], vectors[2], vectors[3], stats,
+    )
+
+
+def on_chip_grid():
+    return lax.axis_size("rows") == 16 and lax.axis_size("blk") == 2
+
+
+def gathered_weights(w_qkv, w_out, ln1_gain, ln1_bias, w_gate_up, w_down, ln2_gain, ln2_bias):
+    vectors = (ln1_gain, ln1_bias, ln2_gain, ln2_bias)
+    both = ("rows", "blk")
+    if not on_chip_grid():
+        mats = [lax.all_gather(w, both, axis=0, tiled=True) for w in (w_qkv, w_out, w_gate_up, w_down)]
+        table = lax.all_gather(jnp.stack(vectors, 1), both, axis=0, tiled=True)
+        return (*mats, *(table[:, i] for i in range(4)))
+    width = w_out.shape[1]
+    rows = w_out.shape[0]
+    table = jnp.pad(jnp.stack(vectors, 1), ((0, 0), (0, lane_width - 4)))
+    left = jnp.concatenate([w_qkv[:, : 2 * width], table], 1)
+    right = jnp.concatenate([w_qkv[:, 2 * width :], w_out, jnp.zeros_like(table)], 1)
+    spare = ((0, 0), (0, 32 - rows), (0, 0))
+    a_shard = jnp.pad(jnp.stack([left, right]), spare)
+    ff = w_gate_up.shape[1] // 2
+    g_shard = jnp.pad(jnp.stack([w_gate_up[:, :ff], w_gate_up[:, ff:]]), spare)
+    a_full, g_full, d_full = gather_weights(a_shard, g_shard, w_down)
+    a_left, a_right = a_full.reshape(2, width, -1)
+    wqkv = jnp.concatenate([a_left[:, : 2 * width], a_right[:, :width]], 1)
+    wout = a_right[:, width : 2 * width]
+    wgu = jnp.concatenate([*g_full.reshape(2, width, ff)], 1)
+    columns = (a_left[:, 2 * width + i] for i in range(4))
+    return (wqkv, wout, wgu, d_full.reshape(-1, width), *columns)
+
+
+def summed_grads(grad_qkv, grad_out, grad_gate_up, grad_down, vectors, squares, count):
+    both = ("rows", "blk")
+    width = grad_out.shape[1]
+    owners = lax.axis_size(both)
+    if not on_chip_grid():
+        parts = [
+            lax.psum_scatter(g, both, scatter_dimension=0, tiled=True)
+            for g in (grad_qkv, grad_out, grad_gate_up, grad_down)
+        ]
+        vectors = [lax.psum_scatter(v, both, scatter_dimension=0, tiled=True) for v in vectors]
+        return (parts, vectors, *lax.psum((squares, count), both))
+    low = jnp.bfloat16
+    left = grad_qkv[:, : 2 * width]
+    right = jnp.concatenate([grad_qkv[:, 2 * width :], grad_out], 1)
+    ff = grad_gate_up.shape[1] // 2
+    chips = lambda m: m.astype(low).reshape(16, -1, m.shape[1])
+    a_grad = jnp.stack([chips(left), chips(right)])
+    g_grad = jnp.stack([chips(grad_gate_up[:, :ff]), chips(grad_gate_up[:, ff:])])
+    d_grad = grad_down.astype(low).reshape(16, 2, -1, width)
+    flat = jnp.concatenate([*vectors, squares, count[None]])
+    small = jnp.pad(flat, (0, 32 * lane_width - flat.shape[0])).reshape(32, lane_width)
+    *parts, small = scatter_grads(a_grad, g_grad, d_grad, small)
+    flat = small.reshape(-1)
+    me = lax.axis_index("rows") * 2 + lax.axis_index("blk")
+    share = width // owners
+    mine = [lax.dynamic_slice_in_dim(flat, i * width + me * share, share) for i in range(4)]
+    return (parts, mine, flat[4 * width : 4 * width + 4], flat[4 * width + 4])
 
 
 def solution(mesh):

time: 959 us -> 537 us (0.56)
  waiting for transfers between devices: 495 us -> 0.01 us
  Pallas kernels: 0 us -> 197 us
  blocking collectives: 81.8 us -> 0 us
  local copies, waits for them, and re-layouts: 86.4 us -> 55.7 us
  matrix products: 200 us -> 185 us
  between operations: 15.4 us -> 1.99 us
  other arithmetic: 64.7 us -> 77.9 us
    reduce_scatter x4 -> x0, waiting for transfers between devices: 360 us -> none  [the longest x1 211 us: body(): lax.psum_scatter(lane_rows(grad_gate_up), ('rows', 'blk'), scatter_dimens...]
    pallas_call x0 -> x2, Pallas kernels: none -> 197 us  [the longest x1 103 us: scatter_grads(): pl.pallas_call(scatter_kernel, out_shape=(jax.ShapeDtypeStruct((24, 3 * w...]
    all_gather x4 -> x0, waiting for transfers between devices: 129 us -> none  [the longest x1 64.3 us: body(): lax.all_gather(w_qkv, ('rows', 'blk'), axis=0, tiled=True)]
    unnamed x2 -> x0, blocking collectives: 81.8 us -> none
    reshape x8 -> x1, local copies, waits for them, and re-layouts: 48.6 us -> 0.61 us  [summed_grads(): jnp.pad(flat, (0, 32 * lane_width - flat.shape[0])).reshape(32, lane_width)]
    another operation x2 -> x6, local copies, waits for them, and re-layouts: 1.03 us -> 11.2 us  [the longest x1 8.65 us: gathered_weights(): wgu = jnp.concatenate([*g_full.reshape(2, width, ff)], 1)]
    another operation x4 -> x9, other arithmetic: 9.34 us -> 19.2 us  [the longest x1 8.39 us: summed_grads(): jnp.stack([chips(grad_gate_up[:, :ff]), chips(grad_gate_up[:, ff:])])]
  transfers between devices with their start and end apart: 12 -> 4, of which waited for: 8 -> 0; matrix products, arithmetic and copies ran while one was open for 31% -> 8% of each run, Pallas kernels for 0% -> 0%
where the time goes in v1:
time: 537 us; the launch traced here: 530 us
  Pallas kernels  197 us (37%)
  matrix products  185 us (34%)
  other arithmetic  77.9 us (15%)
  local copies, waits for them, and re-layouts  55.7 us (10%)
  starting transfers between devices  11.6 us (2%)
    pallas_call x1, Pallas kernels, scatter_grads(): pl.pallas_call(scatter_kernel, out_shape=(jax.ShapeDtypeStruct((24, 3 * w...  103 us
    pallas_call x1, Pallas kernels, gather_weights(): pl.pallas_call(gather_kernel, out_shape=(jax.ShapeDtypeStruct((2, 16, row...  94 us
    dot_general x12, matrix products, group_scores(): jnp.einsum('gqd,gkd->gqk', q_grp, k_grp, preferred_element_type=jnp.float32)  43.5 us
    dot_general x4, matrix products, times_transposed(): lax.dot_general(left, right, (((1,), (1,)), ((), ())), preferred_element_...  32.7 us
    dot_general x4, matrix products, transposed_times(): lax.dot_general(left, right, (((0,), (0,)), ((), ())), preferred_element_...  25.1 us
    unnamed x62, local copies, waits for them, and re-layouts  21.9 us
    dot_general x6, matrix products, backward_group(): jnp.einsum('gqk,gkd->gqd', dlogit, k_grp, preferred_element_type=jnp.floa...  16.3 us
    convert_element_type x1, other arithmetic, body(): act_low = act.astype(jnp.bfloat16)  16.1 us
  transfers between devices with their start and end apart: 4, of which 0 were waited for; matrix products, arithmetic and copies ran while one was open for 8% of the time, Pallas kernels for 0%

profile of v1, /device:TPU:0, one launch (start us, length us, event | category | flops | bytes accessed | tf_op | source)
XLA Modules:
  0.0 530.1 jit_solution(11184782150452758384)
XLA Ops:
  5.9 94.0 %gather_weights.1 = (bf16[2,16,48,1664]{3,2,1,0:T(8,128)(2,1)S(1)}, bf16[2,16,48,3072]{3,2,1,0:T(8,128)(2,1)S(1)}, bf16[16,2,96,768]{3,2,1,0:T(8,128)(2,1)S(1)}) custom-call(bf16[2,32,1664]{2,1,0:T(8,128)(2,1)S(1)} %fusion.98.a_shard, bf16[2,32,3072]{2,1,0:T(8,128)(2,1)S(1)} %fusion.97.g_shard, bf16[96,768]{1,0:T(8,128)(2,1)S(1)} %copy-done.1), custom_call_target="tpu_custom_call" | custom-call | tf_op jit(solution)/shard_map/gather_weights/pallas_call | solution.py:261
  99.9 3.6 copy-done
  110.7 3.6 collective-permute-start
  121.6 8.7 %fusion.124 = (bf16[1,16,48,3072]{3,2,1,0:T(8,128)(2,1)}, bf16[1,16,48,3072]{3,2,1,0:T(8,128)(2,1)}) fusion(bf16[2,16,48,3072]{3,2,1,0:T(8,128)(2,1)} %copy-done), kind=kLoop, calls=%fused_computation.208 | loop fusion | bytes 18874368 | tf_op jit(solution)/shard_map/unstack | solution.py:628
  130.2 3.0 pad_maximum_fusion.5
  133.2 2.4 fusion.127
  135.7 47.3 %while.30 = (s32[]{:T(128)}, bf16[6,2,512,64]{2,3,1,0:T(8,128)(2,1)S(1)}, f32[6,2,512]{2,1,0:T(2,128)S(1)}, bf16[6,2,512,64]{2,3,1,0:T(8,128)(2,1)S(1)}, bf16[6,...) while((s32[]{:T(128)}, ...), condition=%wide.region_3.4_spmd.clone.clone, body=%wide.region_0.3_spmd.clone.clone.sunk | while | flops 422312960 | bytes 27979924 | solution.py:529
  137.2 3.1 fusion.157
  141.4 2.2 fusion.158
  145.1 3.1 fusion.157
  153.0 3.1 fusion.157
  160.9 3.1 fusion.157
  165.1 2.2 fusion.158
  168.8 3.1 fusion.157
  176.7 3.1 fusion.157
  184.0 3.9 fusion.121
  188.1 13.6 %fusion.62 = f32[512,6144]{1,0:T(8,128)} fusion(bf16[768,3072]{1,0:T(8,128)(2,1)} %bitcast.229, bf16[768,3072]{1,0:T(8,128)(2,1)} %bitcast.227, f32[512,768]{1,0:T(8,128)S(1)} %get-tuple-element.370, f32[768]{0:T(1024)S(1)} %convert_reduce_fusion.3, f32[768]{0:T(1024)S(1)} %convert_reduce_fusion.4, f32[512]{0:T(512)S(1)} %fusion.103, ...), kind=kOutput, calls=%fused_computation.89 | convolution fusion | flops 4852678656 | bytes 23603200 | tf_op jit(solution)/shard_map/dot_general | solution.py:538
  201.7 16.1 %multiply_convert_fusion.1 = (bf16[512,3072]{1,0:T(8,128)(2,1)S(1)}, f32[512,3072]{1,0:T(8,128)}) fusion(f32[512,6144]{1,0:T(8,128)} %fusion.62), kind=kLoop, calls=%fused_computation.74 | loop fusion | flops 103809024 | bytes 22020096 | tf_op jit(solution)/shard_map/convert_element_type | solution.py:540
  217.8 3.8 fusion.118
  224.3 11.9 %fusion.71 = (f32[512,3072]{1,0:T(8,128)}, f32[512,3072]{1,0:T(8,128)}) fusion(f32[512,3072]{1,0:T(8,128)} %get-tuple-element.368, f32[512,6144]{1,0:T(8,128)} %fusion.62, bf16[3072,768]{1,0:T(8,128)(2,1)S(1)} %bitcast.209, f32[512,768]{1,0:T(8,128)S(1)} %get-tuple-element.364, f32[512]{0:T(512)S(1)} %negate_multiply_fusion.2), kind=kOutput, calls=%fused_computation.112 | convolution fusion | flops 2441871360 | bytes 37750784 | tf_op jit(solution)/shard_map/dot_general | solution.py:445
  236.2 12.5 %convolution_convert_fusion = bf16[768,6144]{1,0:T(8,128)(2,1)} fusion(f32[512,3072]{1,0:T(8,128)} %get-tuple-element.378, f32[512,3072]{1,0:T(8,128)} %get-tuple-element.377, f32[512,768]{1,0:T(8,128)S(1)} %get-tuple-element.370, f32[768]{0:T(1024)S(1)} %convert_reduce_fusion.3, f32[768]{0:T(1024)S(1)} %convert_reduce_fusion.4, f32[512]{0:T(512)S(1)} %fusion.103, ...), kind=kOutput, calls=%fused_computation.67 | convolution fusion | flops 4844814336 | bytes 23603200 | tf_op jit(solution)/shard_map/dot_general | solution.py:451
  248.6 14.5 %multiply_reduce_fusion.1 = (f32[768]{0:T(1024)S(1)}, f32[512]{0:T(512)S(1)}, f32[]{:T(128)}, f32[768]{0:T(1024)S(1)}, f32[]{:T(128)}, /*index=5*/f32[]{:T(128)}, f32[]{:T(128)}, f32[512,768]{1,0:T(8,128)}) fusion(f32[512,768]{1,0:T(8,128)S(1)} %get-tuple-element.370, f32[512]{0:T(512)S(1)} %fusion.103, f32[512]{0:T(512)S(1)} %broadcast_multiply_fusion.1, ...), kind=kOutput, calls=%fused_computation.129 | convolution fusion | flops 4866832384 | bytes 30693392 | tf_op jit(solution)/shard_map/dot_general | solution.py:445
  269.8 85.1 %while.31 = (s32[]{:T(128)}, bf16[6,2,512,64]{2,3,1,0:T(8,128)(2,1)}, f32[6,2,1536,64]{2,3,1,0:T(8,128)}, f32[6,2,1536,64]{2,3,1,0:T(8,128)}, bf16[6,2,512,64]{2...) while((s32[]{:T(128)}, ...), condition=%wide.region_14.15_spmd.clone.clone, body=%wide.region_12.14_spmd.clone.clone.sunk | while | flops 1029700608 | bytes 58641580 | solution.py:581
  273.3 4.1 multiply_reduce_fusion.6
  281.2 2.7 fusion.169
  287.4 4.1 multiply_reduce_fusion.6
  295.4 2.7 fusion.169
  301.6 4.1 multiply_reduce_fusion.6
  309.5 2.7 fusion.169
  315.8 4.1 multiply_reduce_fusion.6
  323.7 2.7 fusion.169
  330.0 4.1 multiply_reduce_fusion.6
  337.9 2.7 fusion.169
  344.1 4.1 multiply_reduce_fusion.6
  352.0 2.7 fusion.169
  354.9 6.9 %fusion.54 = bf16[1536,1536]{0,1:T(8,128)(2,1)} fusion(f32[1536,768]{0,1:T(8,128)} %bitcast.214, f32[1536,768]{0,1:T(8,128)} %bitcast.212), kind=kLoop, calls=%fused_computation.69 | loop fusion | flops 9437184 | bytes 14155776 | tf_op jit(solution)/shard_map/convert.14
  361.8 4.0 fusion.126
  365.9 5.3 %collective-permute-start.2 = (bf16[512,1536]{0,1:T(8,128)(2,1)}, bf16[512,1536]{0,1:T(8,128)(2,1)}, u32[]{:S(2)}, u32[]{:S(2)}) collective-permute-start(bf16[512,1536]{0,1:T(8,128)(2,1)} %get-tuple-element.385), channel_id=1, source_target_pairs={{0,1},{2,3},{4,5},{6,7},{8,9},{10,11},{12,13},{14,15},{16,17},{18,... | collective-permute-start | bytes 4718600 | tf_op jit(solution)/shard_map/ppermute | solution.py:413
  372.7 4.6 fusion.123
  377.3 3.3 concatenate.56
  381.2 3.6 fusion.82
  384.7 8.4 %pad_maximum_fusion.2.g_grad = bf16[2,16,48,3072]{3,2,1,0:T(8,128)(2,1)} fusion(bf16[1,16,48,3072]{3,2,1,0:T(8,128)(2,1)} %bitcast.217, bf16[1,16,48,3072]{3,2,1,0:T(8,128)(2,1)} %bitcast.216), kind=kLoop, calls=%fused_computation.71 | loop fusion | flops 4718592 | bytes 18874368 | tf_op jit(solution)/shard_map/stack | solution.py:650
  393.1 5.9 %convolution_convert_fusion.1 = bf16[3072,768]{1,0:T(8,128)(2,1)} fusion(bf16[512,3072]{1,0:T(8,128)(2,1)S(1)} %copy-done.8, f32[512,768]{1,0:T(8,128)} %copy-done.11, f32[512]{0:T(512)S(1)} %negate_multiply_fusion.2), kind=kOutput, calls=%fused_computation.92 | convolution fusion | flops 2419064832 | bytes 9439232 | tf_op jit(solution)/shard_map/dot_general | solution.py:451
  399.1 4.3 fusion.69
  403.4 3.2 fusion.64
  409.0 4.2 fusion.88
  413.2 2.4 maximum_maximum_fusion.a_grad
  415.6 103.0 %scatter_grads.1 = (f32[24,2304]{1,0:T(8,128)}, f32[24,768]{1,0:T(8,128)}, f32[24,6144]{1,0:T(8,128)}, f32[96,768]{1,0:T(8,128)}, f32[32,128]{1,0:T(8,128)}) custom-call(bf16[2,16,48,1536]{3,2,1,0:T(8,128)(2,1)} %maximum_maximum_fusion.a_grad, bf16[2,16,48,3072]{3,2,1,0:T(8,128)(2,1)} %pad_maximum_fusion.2.g_grad, bf16[16,2,96,768]{3,2,1,0:T(8,128)(2,1)} %bitcast.231, ...), custom_call_target="tpu_custom_call" | custom-call | tf_op jit(solution)/shard_map/scatter_grads/pallas_call | solution.py:366
  (206 shorter events, 112.6 us)
Async XLA Ops:
  5.0 0.9 copy-start.1
  99.9 3.6 copy-start
  103.6 2.1 copy-start.2
  105.7 3.8 copy-start.4
  105.7 1.7 copy-start.17
  105.7 3.7 copy-start.15
  107.3 2.1 copy-start.9
  109.5 20.8 %copy-start.3 = (bf16[512,2304]{0,1:T(8,128)(2,1)}, bf16[512,2304]{0,1:T(8,128)(2,1)S(1)}, u32[]{:S(2)}) copy-start(bf16[512,2304]{0,1:T(8,128)(2,1)S(1)} %fusion.65) | copy-start | bytes 7077892
  109.5 10.5 %copy-start.21 = (s32[1,1024]{1,0:T(1,128)S(1)}, s32[1,1024]{1,0:T(1,128)}, u32[]{:S(2)}) copy-start(s32[1,1024]{1,0:T(1,128)} %param.16) | copy-start | bytes 12292
  109.5 11.3 %copy-start.5 = (bf16[1,512,768]{2,1,0:T(8,128)(2,1)S(1)}, bf16[1,512,768]{2,1,0:T(8,128)(2,1)}, u32[]{:S(2)}) copy-start(bf16[1,512,768]{2,1,0:T(8,128)(2,1)} %param.25) | copy-start | bytes 2359300
  110.7 19.5 %collective-permute-start = (bf16[512,1536]{0,1:T(8,128)(2,1)}, bf16[512,1536]{0,1:T(8,128)(2,1)}, u32[]{:S(2)}, u32[]{:S(2)}) collective-permute-start(bf16[512,1536]{0,1:T(8,128)(2,1)} %slice.127), channel_id=1, source_target_pairs={{0,1},{2,3},{4,5},{6,7},{8,9},{10,11},{12,13},{14,15},{16,17},{18,... | collective-permute-start | bytes 4718600 | tf_op jit(solution)/shard_map/ppermute | solution.py:413
  114.4 15.9 %collective-permute-start.1 = (bf16[512,1536]{0,1:T(8,128)(2,1)}, bf16[512,1536]{0,1:T(8,128)(2,1)}, u32[]{:S(2)}, u32[]{:S(2)}) collective-permute-start(bf16[512,1536]{0,1:T(8,128)(2,1)} %slice.127), channel_id=1, source_target_pairs={{1,0},{3,2},{5,4},{7,6},{9,8},{11,10},{13,12},{15,14},{17,16},{19,... | collective-permute-start | bytes 4718600 | tf_op jit(solution)/shard_map/ppermute | solution.py:415
  133.2 2.5 slice-start.5
  183.1 0.9 copy-start.6
  184.0 33.8 %slice-start = ((s8[4718592]{0:T(1024)(128)(4,1)}), s8[4194304]{0:T(1024)(128)(4,1)S(1)}, s32[]{:S(2)}) async-start(s8[4718592]{0:T(1024)(128)(4,1)} %bitcast.206), calls=%async_computation | async-start | bytes 8388608
  188.1 29.7 %slice-start.1 = ((s8[4718592]{0:T(1024)(128)(4,1)}), s8[524288]{0:T(1024)(128)(4,1)S(1)}, s32[]{:S(2)}) async-start(s8[4718592]{0:T(1024)(128)(4,1)} %bitcast.206), calls=%async_computation.1 | async-start | bytes 1048576
  217.8 3.8 copy-start.7
  224.3 11.9 %copy-start.11 = (f32[512,768]{1,0:T(8,128)}, f32[512,768]{1,0:T(8,128)S(1)}, u32[]{:S(2)}) copy-start(f32[512,768]{1,0:T(8,128)S(1)} %get-tuple-element.364) | copy-start | bytes 4718596
  236.2 12.5 %copy-start.18 = (bf16[1,512,768]{2,1,0:T(8,128)(2,1)S(1)}, bf16[1,512,768]{2,1,0:T(8,128)(2,1)}, u32[]{:S(2)}) copy-start(bf16[1,512,768]{2,1,0:T(8,128)(2,1)} %param.15) | copy-start | bytes 2359300
  265.2 1.2 copy-start.12
  354.9 17.7 %slice-start.2 = ((s8[9437184]{0:T(1024)(128)(4,1)}), s8[4194304]{0:T(1024)(128)(4,1)S(1)}, s32[]{:S(2)}) async-start(s8[9437184]{0:T(1024)(128)(4,1)} %bitcast.210), calls=%async_computation.2 | async-start | bytes 8388608
  354.9 17.7 %slice-start.3 = ((s8[9437184]{0:T(1024)(128)(4,1)}), s8[4194304]{0:T(1024)(128)(4,1)S(1)}, s32[]{:S(2)}) async-start(s8[9437184]{0:T(1024)(128)(4,1)} %bitcast.210), calls=%async_computation.3 | async-start | bytes 8388608
  354.9 17.7 %slice-start.4 = ((s8[9437184]{0:T(1024)(128)(4,1)}), s8[1048576]{0:T(1024)(128)(4,1)S(1)}, s32[]{:S(2)}) async-start(s8[9437184]{0:T(1024)(128)(4,1)} %bitcast.210), calls=%async_computation.4 | async-start | bytes 2097152
  365.9 33.2 %collective-permute-start.2 = (bf16[512,1536]{0,1:T(8,128)(2,1)}, bf16[512,1536]{0,1:T(8,128)(2,1)}, u32[]{:S(2)}, u32[]{:S(2)}) collective-permute-start(bf16[512,1536]{0,1:T(8,128)(2,1)} %get-tuple-element.385), channel_id=1, source_target_pairs={{0,1},{2,3},{4,5},{6,7},{8,9},{10,11},{12,13},{14,15},{16,17},{18,... | collective-permute-start | bytes 4718600 | tf_op jit(solution)/shard_map/ppermute | solution.py:413
  371.2 6.0 %copy-start.20 = (f32[768]{0:T(1024)S(1)}, f32[768]{0:T(1024)}, u32[]{:S(2)}) copy-start(f32[768]{0:T(1024)} %convert_reduce_fusion) | copy-start | bytes 9220
  371.2 27.9 %collective-permute-start.3 = (bf16[512,1536]{0,1:T(8,128)(2,1)}, bf16[512,1536]{0,1:T(8,128)(2,1)}, u32[]{:S(2)}, u32[]{:S(2)}) collective-permute-start(bf16[512,1536]{0,1:T(8,128)(2,1)} %get-tuple-element.386), channel_id=1, source_target_pairs={{1,0},{3,2},{5,4},{7,6},{9,8},{11,10},{13,12},{15,14},{17,16},{19,... | collective-permute-start | bytes 4718600 | tf_op jit(solution)/shard_map/ppermute | solution.py:415
  384.7 8.4 %copy-start.8 = (bf16[512,3072]{1,0:T(8,128)(2,1)S(1)}, bf16[512,3072]{1,0:T(8,128)(2,1)}, u32[]{:S(2)}) copy-start(bf16[512,3072]{1,0:T(8,128)(2,1)} %copy-done.7) | copy-start | bytes 9437188
  399.1 4.3 copy-start.19
  406.6 1.7 copy-start.10
  406.6 2.1 copy-start.13
  406.6 2.4 copy-start.16
  409.0 4.2 copy-start.14

commit v2 on v1

--- a/solution.py
+++ b/solution.py
@@ -4,6 +4,26 @@
 from jax.experimental import pallas as pl
 from jax.experimental.pallas import tpu as pltpu
 from jax.sharding import PartitionSpec as P
+
+HEADS = 12
+
+
+ln_eps = 1e-12
+far = 1e33
+lane_width = 128
+
+
+def times_transposed(left, right):
+    return lax.dot_general(
+        left, right, (((1,), (1,)), ((), ())), preferred_element_type=jnp.float32
+    )
+
+
+def transposed_times(left, right):
+    return lax.dot_general(
+        left, right, (((0,), (0,)), ((), ())), preferred_element_type=jnp.float32
+    )
+
 
 MESH = pl.DeviceIdType.MESH
 
@@ -393,212 +413,348 @@
     )(a_grad, g_grad, d_grad, small)
 
 
-HEADS = 12
-
-
-ln_eps = 1e-12
-masked_score = -1e30
-group_heads = 2
-lane_width = 128
-
-
-def extended(cells, sides, width):
-    for axis, dim in sides:
-        count = lax.axis_size(axis)
-        ends = count - 1
-        head = lax.slice_in_dim(cells, 0, width, axis=dim)
-        tail = lax.slice_in_dim(cells, cells.shape[dim] - width, cells.shape[dim], axis=dim)
-        cells = jnp.concatenate(
-            [
-                lax.ppermute(tail, axis, [(i, (i + 1) % count) for i in range(ends)]),
-                cells,
-                lax.ppermute(head, axis, [((i + 1) % count, i) for i in range(ends)]),
-            ],
-            axis=dim,
-        )
-    return cells
-
-
-def layer_norm(resid, gain, bias):
-    mean = jnp.mean(resid, -1, keepdims=True)
-    centred = resid - mean
-    spread = jnp.mean(centred * centred, -1, keepdims=True)
-    return centred * lax.rsqrt(spread + ln_eps) * gain + bias
-
-
-def geglu(gate_up):
-    half = gate_up.shape[-1] // 2
-    return jax.nn.gelu(gate_up[:, :half], approximate=False) * gate_up[:, half:]
-
-
-def head_slopes(heads):
-    order = jnp.arange(1, heads + 1, dtype=jnp.float32)
-    return jnp.exp2(-8.0 * order / heads)
-
-
-def permitted(labels_q, labels_k, pos_q, pos_k, pad_label):
-    same_piece = (labels_q[:, None] == labels_k[None, :]) & (labels_k[None, :] != pad_label)
-    return same_piece | (pos_q[:, None] == pos_k[None, :])
-
-
-def times_transposed(left, right):
-    return lax.dot_general(
-        left, right, (((1,), (1,)), ((), ())), preferred_element_type=jnp.float32
-    )
-
-
-def transposed_times(left, right):
-    return lax.dot_general(
-        left, right, (((0,), (0,)), ((), ())), preferred_element_type=jnp.float32
-    )
-
-
-def split_heads(matrix, heads):
-    count, width = matrix.shape
-    return matrix.reshape(count, heads // group_heads, group_heads, width // heads).transpose(
-        1, 2, 0, 3
-    )
-
-
-def merge_heads(groups):
-    number, size, count, depth = groups.shape
-    return groups.transpose(2, 0, 1, 3).reshape(count, number * size * depth)
-
-
-def lane_rows(matrix):
-    return matrix.reshape(-1, lane_width)
-
-
-def owner_rows(flat, whole_rows, columns, owners):
-    return flat.reshape(whole_rows // owners, columns)
-
-
-def group_scores(q_grp, k_grp, slope_grp, distance, allowed):
-    scale = q_grp.shape[-1] ** (-0.5)
-    raw = jnp.einsum("gqd,gkd->gqk", q_grp, k_grp, preferred_element_type=jnp.float32) * scale
-    raw = raw - slope_grp[:, None, None] * distance[None]
-    return jnp.where(allowed[None], raw, masked_score)
-
-
-def body(
-    tokens,
-    segments,
-    w_qkv,
-    w_out,
-    ln1_gain,
-    ln1_bias,
-    w_gate_up,
-    w_down,
-    ln2_gain,
-    ln2_bias,
-    out_grad,
+def dot(left, right, dims=((1,), (0,))):
+    return lax.dot_general(left, right, (dims, ((), ())), preferred_element_type=jnp.float32)
+
+
+def row_mean(values):
+    return jnp.mean(values, -1, keepdims=True)
+
+
+def normalized(resid):
+    centred = resid - row_mean(resid)
+    inverse = lax.rsqrt(row_mean(centred * centred) + ln_eps)
+    return centred * inverse, inverse
+
+
+def norm_back(grad, gain, norm, inverse):
+    e = grad * gain
+    return inverse * (e - row_mean(e) - norm * row_mean(e * norm))
+
+
+def column_sum(values):
+    return jnp.sum(values, 0, keepdims=True)
+
+
+def ffn_kernel(
+    tokens, attended, w_out, vectors, valid, out_grad, w_gu, w_down,
+    output, d_resid_one, d_att, grad_out, grad_gu, grad_down, small,
+    hid, hid_low, hid_t, norm_one, inv_one, slope_gate, slope_up, act, total, d_hid, d_branch,
 ):
-    inputs = tokens[0]
-    tok_rows, width = inputs.shape
-    heads = HEADS
-    owners = lax.axis_size(("rows", "blk"))
-    labels = segments[0]
+    i = pl.program_id(0)
+    tiles = pl.num_programs(0) // 2
+    low = jnp.bfloat16
+    wide = jnp.float32
+
+    @pl.when(i == 0)
+    def _():
+        branch = dot(attended[...], w_out[0])
+        toks = tokens[...].astype(wide)
+        norm, inverse = normalized(toks + branch)
+        norm_one[...] = norm
+        inv_one[...] = inverse
+        hidden = norm * vectors[0:1, :] + vectors[1:2, :]
+        hid[...] = hidden
+        hid_low[...] = hidden.astype(low)
+        hid_t[...] = hidden.T.astype(low)
+        mask = valid[...]
+        small[4:5, :] = column_sum(mask * toks * toks)
+        small[5:6, :] = column_sum(mask * branch * branch)
+        small[6:7, :] = column_sum(mask * hidden * hidden)
+        small[8:16, :] = jnp.zeros((8, small.shape[1]), wide)
+        small[8:9, :] = jnp.broadcast_to(jnp.sum(mask, 0, keepdims=True), (1, small.shape[1]))
+        total[...] = jnp.zeros_like(total)
+
+    @pl.when(i < tiles)
+    def _():
+        h = hid_low[...]
+        gate = dot(h, w_gu[0])
+        up = dot(h, w_gu[1])
+        cdf = 0.5 + 0.5 * lax.erf(gate * 0.7071067811865476)
+        glu = gate * cdf
+        density = 0.3989422804014327 * jnp.exp(-0.5 * gate * gate)
+        slope_up[i] = glu
+        slope_gate[i] = up * (cdf + gate * density)
+        a = (glu * up).astype(low)
+        act[i] = a
+        total[...] += dot(a, w_down[...])
+
+    @pl.when(i == tiles - 1)
+    def _():
+        branch = total[...]
+        mask = valid[...]
+        small[7:8, :] = column_sum(mask * branch * branch)
+        norm, inverse = normalized(hid[...] + branch)
+        gain = vectors[2:3, :]
+        output[...] = (norm * gain + vectors[3:4, :]).astype(low)
+        grad = out_grad[...].astype(wide)
+        small[2:3, :] = column_sum(grad * norm)
+        small[3:4, :] = column_sum(grad)
+        back = norm_back(grad, gain, norm, inverse)
+        d_hid[...] = back
+        d_branch[...] = back.astype(low)
+
+    @pl.when(i >= tiles)
+    def _():
+        j = i - tiles
+        db = d_branch[...]
+        grad_down[...] = dot(act[j].T, db).astype(low)
+        d_act = dot(db, w_down[...], ((1,), (1,)))
+        d_gate = (d_act * slope_gate[j]).astype(low)
+        d_up = (d_act * slope_up[j]).astype(low)
+        h_t = hid_t[...]
+        grad_gu[0] = dot(h_t, d_gate).astype(low)
+        grad_gu[1] = dot(h_t, d_up).astype(low)
+        d_hid[...] += dot(d_gate, w_gu[0], ((1,), (1,))) + dot(d_up, w_gu[1], ((1,), (1,)))
+
+    @pl.when(i == 2 * tiles - 1)
+    def _():
+        grad = d_hid[...]
+        norm = norm_one[...]
+        small[0:1, :] = column_sum(grad * norm)
+        small[1:2, :] = column_sum(grad)
+        back = norm_back(grad, vectors[0:1, :], norm, inv_one[...])
+        d_resid_one[...] = back
+        db = back.astype(low)
+        grad_out[...] = dot(attended[...].T, db).astype(low)
+        d_att[...] = dot(db, w_out[0], ((1,), (1,))).astype(low)
+
+
+def ffn(tokens, attended, a_full, vectors, valid, out_grad, w_gu, w_down):
+    rows, width = tokens.shape
+    ff = w_down.shape[0]
+    tile = 512
+    tiles = ff // tile
+    low, wide = jnp.bfloat16, jnp.float32
+    whole = lambda *shape: pl.BlockSpec(shape, lambda i: (0,) * len(shape))
+    at = lambda i: jnp.where(i < tiles, i, i - tiles)
+    late = lambda i: jnp.maximum(i - tiles, 0)
+    return pl.pallas_call(
+        ffn_kernel,
+        grid=(2 * tiles,),
+        out_shape=(
+            jax.ShapeDtypeStruct((rows, width), low),
+            jax.ShapeDtypeStruct((rows, width), wide),
+            jax.ShapeDtypeStruct((rows, width), low),
+            jax.ShapeDtypeStruct((width, width), low),
+            jax.ShapeDtypeStruct((2, width, ff), low),
+            jax.ShapeDtypeStruct((ff, width), low),
+            jax.ShapeDtypeStruct((16, width), wide),
+        ),
+        in_specs=[
+            whole(rows, width),
+            whole(rows, width),
+            pl.BlockSpec((1, width, width), lambda i: (1, 0, 1)),
+            whole(8, width),
+            whole(rows, 1),
+            whole(rows, width),
+            pl.BlockSpec((2, width, tile), lambda i: (0, 0, at(i))),
+            pl.BlockSpec((tile, width), lambda i: (at(i), 0)),
+        ],
+        out_specs=(
+            whole(rows, width),
+            whole(rows, width),
+            whole(rows, width),
+            whole(width, width),
+            pl.BlockSpec((2, width, tile), lambda i: (0, 0, late(i))),
+            pl.BlockSpec((tile, width), lambda i: (late(i), 0)),
+            whole(16, width),
+        ),
+        scratch_shapes=[
+            pltpu.VMEM((rows, width), wide),
+            pltpu.VMEM((rows, width), low),
+            pltpu.VMEM((width, rows), low),
+            pltpu.VMEM((rows, width), wide),
+            pltpu.VMEM((rows, 1), wide),
+            pltpu.VMEM((tiles, rows, tile), wide),
+            pltpu.VMEM((tiles, rows, tile), wide),
+            pltpu.VMEM((tiles, rows, tile), low),
+            pltpu.VMEM((rows, width), wide),
+            pltpu.VMEM((rows, width), wide),
+            pltpu.VMEM((rows, width), low),
+        ],
+        compiler_params=pltpu.CompilerParams(vmem_limit_bytes=60 * 2**20),
+        cost_estimate=pl.CostEstimate(
+            flops=2 * rows * width * (9 * ff + 3 * width), bytes_accessed=18 * ff * width, transcendentals=2 * rows * ff
+        ),
+        name="feed_forward",
+    )(tokens, attended, a_full, vectors, valid, out_grad, w_gu, w_down)
+
+
+def half_of(block, axis, second):
+    place = lax.broadcasted_iota(jnp.int32, block.shape, axis)
+    depth = block.shape[axis] // 2
+    keep = place >= depth if second else place < depth
+    return jnp.where(keep, block, jnp.zeros_like(block))
+
+
+def attend_kernel(heads, q, k, v, span, attended, lse, out_t, q_t, v_t):
+    low = jnp.bfloat16
+    rows, width = q.shape
+    lanes = lane_width
+    depth = width // heads
+    chunk = 256
+
+    q_t[...] = (q[...].astype(jnp.float32) * depth**-0.5).T.astype(low)
+    v_t[...] = v[...].astype(jnp.float32).T.astype(low)
+
+    @pl.loop(0, heads // 2)
+    def _(pair):
+        at = pl.ds(pl.multiple_of(pair * lanes, lanes), lanes)
+        keys = k[:, at]
+        for h in (0, 1):
+            slope = jnp.exp2(jnp.full((1, 1), -8.0 / heads, jnp.float32) * (2 * pair + h + 1).astype(jnp.float32))
+            values_t = v_t[pl.ds(pl.multiple_of(pair * lanes + h * depth, depth), depth), :]
+            for c in range(rows // chunk):
+                here = pl.ds(c * chunk, chunk)
+                logits = dot(keys, half_of(q_t[at, here], 0, h)) - slope * span[:, here]
+                top = jnp.max(logits, 0, keepdims=True)
+                weights = jnp.exp(logits - top)
+                norm = jnp.sum(weights, 0, keepdims=True)
+                lse[pl.ds(2 * pair + h, 1), here] = top + jnp.log(norm)
+                mixed = dot(values_t, weights.astype(low))
+                out_t[pl.ds(pl.multiple_of(pair * lanes + h * depth, depth), depth), here] = mixed / norm
+
+    attended[...] = out_t[...].T.astype(low)
+
+
+def attend(q, k, v, span, heads):
+    rows, width = q.shape
+    keys = k.shape[0]
+    low, wide = jnp.bfloat16, jnp.float32
+    return pl.pallas_call(
+        lambda *refs: attend_kernel(heads, *refs),
+        out_shape=(
+            jax.ShapeDtypeStruct((rows, width), low),
+            jax.ShapeDtypeStruct((16, rows), wide),
+        ),
+        in_specs=[pl.BlockSpec(memory_space=pltpu.VMEM)] * 4,
+        out_specs=(pl.BlockSpec(memory_space=pltpu.VMEM),) * 2,
+        scratch_shapes=[
+            pltpu.VMEM((width, rows), wide),
+            pltpu.VMEM((width, rows), low),
+            pltpu.VMEM((width, keys), low),
+        ],
+        compiler_params=pltpu.CompilerParams(vmem_limit_bytes=60 * 2**20),
+        cost_estimate=pl.CostEstimate(flops=4 * rows * keys * width, bytes_accessed=8 * keys * width, transcendentals=heads * rows * keys),
+        name="attend",
+    )(q, k, v, span)
+
+
+def attend_back_kernel(heads, q, k, v, span, lse, att, d_att, dq, dk, dv, q_t, k_t, do_t, dq_t, delta, dk_sum, dv_sum):
+    low, wide = jnp.bfloat16, jnp.float32
+    rows, width = q.shape
+    lanes = lane_width
+    depth = width // heads
+    chunk = 256
+    scale = depth**-0.5
+
+    q_t[...] = (q[...].astype(wide) * scale).T.astype(low)
+    k_t[...] = k[...].astype(wide).T.astype(low)
+    do_wide = d_att[...].astype(wide)
+    do_t[...] = do_wide.T.astype(low)
+    both_t = (do_wide * att[...].astype(wide)).T
+    delta[...] = jnp.sum(both_t.reshape(heads, depth, rows), 1)
+
+    @pl.loop(0, heads // 2)
+    def _(pair):
+        at = pl.ds(pl.multiple_of(pair * lanes, lanes), lanes)
+        keys, values = k[:, at], v[:, at]
+        for c in range(rows // chunk):
+            here = pl.ds(c * chunk, chunk)
+            q_here = (q[here, at].astype(wide) * scale).astype(low)
+            do_here = d_att[here, at]
+            dk_part, dv_part = None, None
+            for h in (0, 1):
+                head = 2 * pair + h
+                own = pl.ds(pl.multiple_of(pair * lanes + h * depth, depth), depth)
+                slope = jnp.exp2(jnp.full((1, 1), -8.0 / heads, jnp.float32) * (head + 1).astype(wide))
+                logits = dot(keys, half_of(q_t[at, here], 0, h)) - slope * span[:, here]
+                probs = jnp.exp(logits - lse[pl.ds(head, 1), here])
+                d_probs = dot(values, half_of(do_t[at, here], 0, h))
+                d_logits = (probs * (d_probs - delta[pl.ds(head, 1), here])).astype(low)
+                dv_term = dot(probs.astype(low), half_of(do_here, 1, h))
+                dk_term = dot(d_logits, half_of(q_here, 1, h))
+                dv_part = dv_term if dv_part is None else dv_part + dv_term
+                dk_part = dk_term if dk_part is None else dk_part + dk_term
+                dq_t[own, here] = dot(k_t[own, :], d_logits) * scale
+            if c == 0:
+                dk_sum[...] = dk_part
+                dv_sum[...] = dv_part
+            else:
+                dk_sum[...] += dk_part
+                dv_sum[...] += dv_part
+        dk[:, at] = dk_sum[...].astype(dk.dtype)
+        dv[:, at] = dv_sum[...].astype(dv.dtype)
+
+    dq[...] = dq_t[...].T.astype(low)
+
+
+def attend_back(q, k, v, span, lse, att, d_att, heads):
+    rows, width = q.shape
+    keys = k.shape[0]
+    low, wide = jnp.bfloat16, jnp.float32
+    return pl.pallas_call(
+        lambda *refs: attend_back_kernel(heads, *refs),
+        out_shape=(
+            jax.ShapeDtypeStruct((rows, width), low),
+            jax.ShapeDtypeStruct((keys, width), wide),
+            jax.ShapeDtypeStruct((keys, width), wide),
+        ),
+        in_specs=[pl.BlockSpec(memory_space=pltpu.VMEM)] * 7,
+        out_specs=(pl.BlockSpec(memory_space=pltpu.VMEM),) * 3,
+        scratch_shapes=[
+            pltpu.VMEM((width, rows), low),
+            pltpu.VMEM((width, keys), low),
+            pltpu.VMEM((width, rows), low),
+            pltpu.VMEM((width, rows), wide),
+            pltpu.VMEM((heads, rows), wide),
+            pltpu.VMEM((keys, lane_width), wide),
+            pltpu.VMEM((keys, lane_width), wide),
+        ],
+        compiler_params=pltpu.CompilerParams(vmem_limit_bytes=60 * 2**20),
+        cost_estimate=pl.CostEstimate(flops=10 * rows * keys * width, bytes_accessed=16 * keys * width, transcendentals=heads * rows * keys),
+        name="attend_back",
+    )(q, k, v, span, lse, att, d_att)
+
+
+def window(cells, width):
+    count = lax.axis_size("blk")
+    if count == 2:
+        other = lax.ppermute(cells, "blk", [(0, 1), (1, 0)])
+        first = lax.axis_index("blk") == 0
+        return jnp.concatenate([jnp.where(first, cells, other), jnp.where(first, other, cells)], 0)
+    before = lax.ppermute(cells, "blk", [(i, i + 1) for i in range(count - 1)])
+    after = lax.ppermute(cells, "blk", [(i + 1, i) for i in range(count - 1)])
+    return jnp.concatenate([before, cells, after], 0)
+
+
+def window_back(terms, width):
+    count = lax.axis_size("blk")
+    low = jnp.bfloat16
+    if count == 2:
+        first = lax.axis_index("blk") == 0
+        upper, lower = terms[:width], terms[width:]
+        other = lax.ppermute(jnp.where(first, lower, upper).astype(low), "blk", [(0, 1), (1, 0)])
+        return jnp.where(first, upper, lower) + other.astype(terms.dtype)
+    before = lax.ppermute(terms[2 * width :].astype(low), "blk", [(i, i + 1) for i in range(count - 1)])
+    after = lax.ppermute(terms[:width].astype(low), "blk", [(i + 1, i) for i in range(count - 1)])
+    return terms[width : 2 * width] + before.astype(terms.dtype) + after.astype(terms.dtype)
+
+
+def key_spans(labels, first, tok_rows):
     seq_len = labels.shape[0]
-    first = lax.axis_index("blk") * tok_rows
     query_pos = first + jnp.arange(tok_rows, dtype=jnp.int32)
-    window_pos = first - tok_rows + jnp.arange(3 * tok_rows, dtype=jnp.int32)
     query_labels = lax.dynamic_slice_in_dim(labels, first, tok_rows, 0)
-    padded_labels = jnp.pad(labels, (tok_rows, tok_rows), constant_values=seq_len)
-    window_labels = lax.dynamic_slice_in_dim(padded_labels, first, 3 * tok_rows, 0)
-    slope_groups = head_slopes(heads).reshape(heads // group_heads, group_heads)
-    allowed = permitted(query_labels, window_labels, query_pos, window_pos, seq_len)
-    distance = jnp.abs(query_pos[:, None] - window_pos[None, :]).astype(jnp.float32)
-    gathered = gathered_weights(w_qkv, w_out, ln1_gain, ln1_bias, w_gate_up, w_down, ln2_gain, ln2_bias)
-    wqkv_full, wout_full, wgu_full, wdown_full, gain_one, bias_one, gain_two, bias_two = gathered
-    qkv = jnp.dot(inputs, wqkv_full, preferred_element_type=jnp.float32).astype(jnp.bfloat16)
-    query = qkv[:, :width]
-    window_kv = extended(qkv[:, width:], (("blk", 0),), tok_rows)
-    q_groups = split_heads(query, heads)
-    k_groups = split_heads(window_kv[:, :width], heads)
-    v_groups = split_heads(window_kv[:, width:], heads)
-
-    def forward_group(parts):
-        q_grp, k_grp, v_grp, slope_grp = parts
-        logits = group_scores(q_grp, k_grp, slope_grp, distance, allowed)
-        top = jnp.max(logits, -1, keepdims=True)
-        lse = top + jnp.log(jnp.sum(jnp.exp(logits - top), -1, keepdims=True))
-        probs = jnp.exp(logits - lse).astype(jnp.bfloat16)
-        mixed = jnp.einsum("gqk,gkd->gqd", probs, v_grp, preferred_element_type=jnp.float32)
-        return (mixed, lse[..., 0])
-
-    mixed_groups, lse_groups = lax.map(forward_group, (q_groups, k_groups, v_groups, slope_groups))
-    attended = merge_heads(mixed_groups).astype(jnp.bfloat16)
-    branch_a = jnp.dot(attended, wout_full, preferred_element_type=jnp.float32)
-    inputs_float = inputs.astype(jnp.float32)
-    resid_one = inputs_float + branch_a
-    hidden1, norm_one_back = jax.vjp(
-        layer_norm, resid_one, gain_one.astype(jnp.float32), bias_one.astype(jnp.float32)
-    )
-    hidden1_low = hidden1.astype(jnp.bfloat16)
-    gate_up = jnp.dot(hidden1_low, wgu_full, preferred_element_type=jnp.float32)
-    act, glu_back = jax.vjp(geglu, gate_up)
-    act_low = act.astype(jnp.bfloat16)
-    branch_f = jnp.dot(act_low, wdown_full, preferred_element_type=jnp.float32)
-    final, norm_two_back = jax.vjp(
-        layer_norm, hidden1 + branch_f, gain_two.astype(jnp.float32), bias_two.astype(jnp.float32)
-    )
-    output = final.astype(jnp.bfloat16)[None]
-    valid = (query_labels != seq_len).astype(jnp.float32)[:, None]
-    squares = jnp.stack(
-        [jnp.sum(valid * term * term) for term in (inputs_float, branch_a, hidden1, branch_f)]
-    )
-    d_resid_two, d_gain_two, d_bias_two = norm_two_back(out_grad[0].astype(jnp.float32))
-    d_branch_f = d_resid_two.astype(jnp.bfloat16)
-    wgu_back, wdown_back, wqkv_back, wout_back = wgu_full, wdown_full, wqkv_full, wout_full
-    d_act = times_transposed(d_branch_f, wdown_back)
-    (d_gate_up,) = glu_back(d_act)
-    d_gate_up_low = d_gate_up.astype(jnp.bfloat16)
-    grad_down = transposed_times(act_low, d_branch_f)
-    grad_gate_up = transposed_times(hidden1_low, d_gate_up_low)
-    d_hidden1 = d_resid_two + times_transposed(d_gate_up_low, wgu_back)
-    d_resid_one, d_gain_one, d_bias_one = norm_one_back(d_hidden1)
-    d_branch_a = d_resid_one.astype(jnp.bfloat16)
-    grad_out = transposed_times(attended, d_branch_a)
-    d_attended = times_transposed(d_branch_a, wout_back).astype(jnp.bfloat16)
-    do_groups = split_heads(d_attended, heads)
-    scale = width // heads
-    scale = scale ** (-0.5)
-
-    def backward_group(parts):
-        q_grp, k_grp, v_grp, slope_grp, do_grp, lse_grp = parts
-        logits = group_scores(q_grp, k_grp, slope_grp, distance, allowed)
-        probs = jnp.exp(logits - lse_grp[..., None])
-        dprob = jnp.einsum("gqd,gkd->gqk", do_grp, v_grp, preferred_element_type=jnp.float32)
-        delta = jnp.sum(probs * dprob, -1, keepdims=True)
-        dlogit = (probs * (dprob - delta)).astype(jnp.bfloat16)
-        dq = jnp.einsum("gqk,gkd->gqd", dlogit, k_grp, preferred_element_type=jnp.float32) * scale
-        dk = jnp.einsum("gqk,gqd->gkd", dlogit, q_grp, preferred_element_type=jnp.float32) * scale
-        dv = jnp.einsum(
-            "gqk,gqd->gkd", probs.astype(jnp.bfloat16), do_grp, preferred_element_type=jnp.float32
-        )
-        return (dq, dk, dv)
-
-    dq_groups, dk_groups, dv_groups = lax.map(
-        backward_group, (q_groups, k_groups, v_groups, slope_groups, do_groups, lse_groups)
-    )
-    kv_terms = jnp.concatenate([merge_heads(dk_groups), merge_heads(dv_groups)], 1)
-    outward = jnp.concatenate([kv_terms[:tok_rows], kv_terms[2 * tok_rows :]], 0)
-    received = extended(outward.astype(jnp.bfloat16), (("blk", 0),), tok_rows).astype(outward.dtype)
-    kv_own = kv_terms[tok_rows : 2 * tok_rows] + received[:tok_rows] + received[3 * tok_rows :]
-    d_qkv = jnp.concatenate(
-        [merge_heads(dq_groups).astype(jnp.bfloat16), kv_own.astype(jnp.bfloat16)], 1
-    )
-    grad_qkv = transposed_times(inputs, d_qkv)
-    tokens_grad = (d_resid_one + times_transposed(d_qkv, wqkv_back)).astype(jnp.bfloat16)[None]
-    parts, vectors, square_sums, valid_count = summed_grads(
-        grad_qkv, grad_out, grad_gate_up, grad_down,
-        (d_gain_one, d_bias_one, d_gain_two, d_bias_two), squares, jnp.sum(valid),
-    )
-    stats = jnp.sqrt(square_sums / (valid_count * width))
-    return (
-        output, tokens_grad, parts[0], parts[1], vectors[0], vectors[1],
-        parts[2], parts[3], vectors[2], vectors[3], stats,
-    )
+    if seq_len == 2 * tok_rows:
+        key_pos, key_labels = jnp.arange(seq_len, dtype=jnp.int32), labels
+    else:
+        key_pos = first - tok_rows + jnp.arange(3 * tok_rows, dtype=jnp.int32)
+        padded = jnp.pad(labels, (tok_rows, tok_rows), constant_values=seq_len)
+        key_labels = lax.dynamic_slice_in_dim(padded, first, 3 * tok_rows, 0)
+    same = (key_labels[:, None] == query_labels[None, :]) & (key_labels[:, None] != seq_len)
+    gap = jnp.abs(key_pos[:, None] - query_pos[None, :])
+    return jnp.where(same | (gap == 0), gap.astype(jnp.float32), far)
 
 
 def on_chip_grid():
@@ -606,57 +762,83 @@
 
 
 def gathered_weights(w_qkv, w_out, ln1_gain, ln1_bias, w_gate_up, w_down, ln2_gain, ln2_bias):
-    vectors = (ln1_gain, ln1_bias, ln2_gain, ln2_bias)
-    both = ("rows", "blk")
-    if not on_chip_grid():
-        mats = [lax.all_gather(w, both, axis=0, tiled=True) for w in (w_qkv, w_out, w_gate_up, w_down)]
-        table = lax.all_gather(jnp.stack(vectors, 1), both, axis=0, tiled=True)
-        return (*mats, *(table[:, i] for i in range(4)))
-    width = w_out.shape[1]
-    rows = w_out.shape[0]
-    table = jnp.pad(jnp.stack(vectors, 1), ((0, 0), (0, lane_width - 4)))
+    rows, width = w_out.shape
+    ff = w_gate_up.shape[1] // 2
+    table = jnp.stack((ln1_gain, ln1_bias, ln2_gain, ln2_bias), 1)
+    table = jnp.pad(table, ((0, 0), (0, lane_width - 4)))
     left = jnp.concatenate([w_qkv[:, : 2 * width], table], 1)
     right = jnp.concatenate([w_qkv[:, 2 * width :], w_out, jnp.zeros_like(table)], 1)
+    a_shard = jnp.stack([left, right])
+    g_shard = jnp.stack([w_gate_up[:, :ff], w_gate_up[:, ff:]])
+    if not on_chip_grid():
+        both = ("rows", "blk")
+        return (
+            lax.all_gather(a_shard, both, axis=1, tiled=True),
+            lax.all_gather(g_shard, both, axis=1, tiled=True),
+            lax.all_gather(w_down, both, axis=0, tiled=True),
+        )
     spare = ((0, 0), (0, 32 - rows), (0, 0))
-    a_shard = jnp.pad(jnp.stack([left, right]), spare)
-    ff = w_gate_up.shape[1] // 2
-    g_shard = jnp.pad(jnp.stack([w_gate_up[:, :ff], w_gate_up[:, ff:]]), spare)
-    a_full, g_full, d_full = gather_weights(a_shard, g_shard, w_down)
-    a_left, a_right = a_full.reshape(2, width, -1)
-    wqkv = jnp.concatenate([a_left[:, : 2 * width], a_right[:, :width]], 1)
-    wout = a_right[:, width : 2 * width]
-    wgu = jnp.concatenate([*g_full.reshape(2, width, ff)], 1)
-    columns = (a_left[:, 2 * width + i] for i in range(4))
-    return (wqkv, wout, wgu, d_full.reshape(-1, width), *columns)
-
-
-def summed_grads(grad_qkv, grad_out, grad_gate_up, grad_down, vectors, squares, count):
+    a_full, g_full, d_full = gather_weights(jnp.pad(a_shard, spare), jnp.pad(g_shard, spare), w_down)
+    return a_full.reshape(2, width, -1), g_full.reshape(2, width, ff), d_full.reshape(-1, width)
+
+
+def summed_grads(a_grad, g_grad, d_grad, small):
     both = ("rows", "blk")
-    width = grad_out.shape[1]
-    owners = lax.axis_size(both)
+    width = d_grad.shape[1]
     if not on_chip_grid():
-        parts = [
-            lax.psum_scatter(g, both, scatter_dimension=0, tiled=True)
-            for g in (grad_qkv, grad_out, grad_gate_up, grad_down)
-        ]
-        vectors = [lax.psum_scatter(v, both, scatter_dimension=0, tiled=True) for v in vectors]
-        return (parts, vectors, *lax.psum((squares, count), both))
-    low = jnp.bfloat16
-    left = grad_qkv[:, : 2 * width]
-    right = jnp.concatenate([grad_qkv[:, 2 * width :], grad_out], 1)
-    ff = grad_gate_up.shape[1] // 2
-    chips = lambda m: m.astype(low).reshape(16, -1, m.shape[1])
-    a_grad = jnp.stack([chips(left), chips(right)])
-    g_grad = jnp.stack([chips(grad_gate_up[:, :ff]), chips(grad_gate_up[:, ff:])])
-    d_grad = grad_down.astype(low).reshape(16, 2, -1, width)
-    flat = jnp.concatenate([*vectors, squares, count[None]])
-    small = jnp.pad(flat, (0, 32 * lane_width - flat.shape[0])).reshape(32, lane_width)
-    *parts, small = scatter_grads(a_grad, g_grad, d_grad, small)
-    flat = small.reshape(-1)
-    me = lax.axis_index("rows") * 2 + lax.axis_index("blk")
-    share = width // owners
-    mine = [lax.dynamic_slice_in_dim(flat, i * width + me * share, share) for i in range(4)]
-    return (parts, mine, flat[4 * width : 4 * width + 4], flat[4 * width + 4])
+        share = lambda g, axis: lax.psum_scatter(g.astype(jnp.float32), both, scatter_dimension=axis, tiled=True)
+        left, right = share(a_grad, 1)
+        gate, up = share(g_grad, 1)
+        cut = right.shape[1] - width
+        return (
+            jnp.concatenate([left, right[:, :cut]], 1), right[:, cut:],
+            jnp.concatenate([gate, up], 1), share(d_grad, 0), lax.psum(small, both),
+        )
+    split = lambda g: g.reshape(2, 16, rows_chip, g.shape[2])
+    return scatter_grads(split(a_grad), split(g_grad), d_grad.reshape(16, 2, -1, width), small)
+
+
+def body(
+    tokens, segments, w_qkv, w_out, ln1_gain, ln1_bias, w_gate_up, w_down, ln2_gain, ln2_bias, out_grad,
+):
+    inputs, labels = tokens[0], segments[0]
+    tok_rows, width = inputs.shape
+    low, wide = jnp.bfloat16, jnp.float32
+    both = ("rows", "blk")
+    first = lax.axis_index("blk") * tok_rows
+    span = key_spans(labels, first, tok_rows)
+    valid = (lax.dynamic_slice_in_dim(labels, first, tok_rows, 0) != labels.shape[0]).astype(wide)[:, None]
+    a_full, w_gu, w_dn = gathered_weights(
+        w_qkv, w_out, ln1_gain, ln1_bias, w_gate_up, w_down, ln2_gain, ln2_bias
+    )
+    vectors = jnp.pad(a_full[0, :, 2 * width : 2 * width + 4].astype(wide).T, ((0, 4), (0, 0)))
+    w_qk, w_v = a_full[0, :, : 2 * width], a_full[1, :, :width]
+    qk = jnp.dot(inputs, w_qk, preferred_element_type=wide).astype(low)
+    v = jnp.dot(inputs, w_v, preferred_element_type=wide).astype(low)
+    query = qk[:, :width]
+    kv = window(jnp.concatenate([qk[:, width:], v], 1), tok_rows)
+    keys, values = kv[:, :width], kv[:, width:]
+    attended, lse = attend(query, keys, values, span, HEADS)
+    output, d_resid_one, d_att, grad_out, g_grad, d_grad, small = ffn(
+        inputs, attended, a_full, vectors, valid, out_grad[0], w_gu, w_dn
+    )
+    dq, dk, dv = attend_back(query, keys, values, span, lse, attended, d_att, HEADS)
+    dkv = window_back(jnp.concatenate([dk, dv], 1), tok_rows)
+    d_qk = jnp.concatenate([dq, dkv[:, :width].astype(low)], 1)
+    d_v = dkv[:, width:].astype(low)
+    grad_qk = transposed_times(inputs, d_qk).astype(low)
+    grad_v = transposed_times(inputs, d_v).astype(low)
+    d_tokens = d_resid_one + times_transposed(d_qk, w_qk) + times_transposed(d_v, w_v)
+    a_grad = jnp.stack([grad_qk, jnp.concatenate([grad_v, grad_out], 1)])
+    *parts, small = summed_grads(a_grad, g_grad, d_grad, small)
+    share = width // lax.axis_size(both)
+    mine = lax.axis_index(both) * share
+    rows = lax.dynamic_slice_in_dim(small[:4], mine, share, 1)
+    stats = jnp.sqrt(jnp.sum(small[4:8], 1) / (small[8, 0] * width))
+    return (
+        output[None], d_tokens.astype(low)[None], parts[0], parts[1], rows[0], rows[1],
+        parts[2], parts[3], rows[2], rows[3], stats,
+    )
 
 
 def solution(mesh):

time: 537 us -> 338 us (0.63); the launches traced: 530 us -> 337 us
  matrix products: 185 us -> 12.3 us
  Pallas kernels: 197 us -> 282 us
  other arithmetic: 77.9 us -> 17.6 us
  local copies, waits for them, and re-layouts: 55.7 us -> 20.1 us
  starting transfers between devices: 11.6 us -> 1.04 us
    dot_general x46 -> x2, matrix products: 127 us -> 2.16 us  [the longest x1 1.38 us: body(): qk = jnp.dot(inputs, w_qk, preferred_element_type=wide).astype(low)]
    pallas_call x0 -> x3, Pallas kernels: none -> 84 us  [the longest x1 37.5 us: ffn(): pl.pallas_call(ffn_kernel, grid=(2 * tiles,), out_shape=(jax.ShapeDtypeSt...]
    convert_element_type x25 -> x2, other arithmetic: 31 us -> 1.42 us  [the longest x1 1.41 us: window_back(): jnp.where(first, lower, upper).astype(low)]
    dot_general x4 -> x2, matrix products: 32.7 us -> 7.82 us  [times_transposed(): lax.dot_general(left, right, (((1,), (1,)), ((), ())), preferred_element_...]
    dot_general x4 -> x2, matrix products: 25.1 us -> 2.28 us  [transposed_times(): lax.dot_general(left, right, (((0,), (0,)), ((), ())), preferred_element_...]
    slice x12 -> x4, local copies, waits for them, and re-layouts: 15.1 us -> 2.96 us  [the longest x1 1.7 us: body(): kv = window(jnp.concatenate([qk[:, width:], v], 1), tok_rows)]
    reduce_sum x13 -> x1, other arithmetic: 12.4 us -> 0.93 us  [body(): stats = jnp.sqrt(jnp.sum(small[4:8], 1) / (small[8, 0] * width))]
    another operation x9 -> x6, other arithmetic: 19.2 us -> 7.86 us  [the longest x1 8.39 us: summed_grads(): jnp.stack([chips(grad_gate_up[:, :ff]), chips(grad_gate_up[:, ff:])])]
  transfers between devices with their start and end apart: 4 -> 2, of which waited for: 0 -> 1; matrix products, arithmetic and copies ran while one was open for 8% -> 1% of each run, Pallas kernels for 0% -> 0%
where the time goes in v2:
time: 338 us; the launch traced here: 337 us
  Pallas kernels  282 us (83%)
  local copies, waits for them, and re-layouts  20.1 us (6%)
  other arithmetic  17.6 us (5%)
  matrix products  12.3 us (4%)
    pallas_call x1, Pallas kernels, scatter_grads(): pl.pallas_call(scatter_kernel, out_shape=(jax.ShapeDtypeStruct((24, 3 * w...  103 us
    pallas_call x1, Pallas kernels, gather_weights(): pl.pallas_call(gather_kernel, out_shape=(jax.ShapeDtypeStruct((2, 16, row...  94.1 us
    pallas_call x1, Pallas kernels, ffn(): pl.pallas_call(ffn_kernel, grid=(2 * tiles,), out_shape=(jax.ShapeDtypeSt...  37.5 us
    pallas_call x1, Pallas kernels, attend_back(): pl.pallas_call(lambda *refs: attend_back_kernel(heads, *refs), out_shape=...  24 us
    pallas_call x1, Pallas kernels, attend(): pl.pallas_call(lambda *refs: attend_kernel(heads, *refs), out_shape=(jax....  22.5 us
    unnamed x38, local copies, waits for them, and re-layouts  12.3 us
    dot_general x2, matrix products, times_transposed(): lax.dot_general(left, right, (((1,), (1,)), ((), ())), preferred_element_...  7.82 us
  transfers between devices with their start and end apart: 2, of which 1 were waited for; matrix products, arithmetic and copies ran while one was open for 1% of the time, Pallas kernels for 0%

profile of v2, /device:TPU:0, one launch (start us, length us, event | category | flops | bytes accessed | tf_op | source)
XLA Modules:
  0.0 337.3 jit_solution(16391621664419417546)
XLA Ops:
  0.7 0.9 slice.69
  1.5 0.9 slice.68
  2.4 0.7 pad_maximum_fusion.7
  3.1 0.1 copy.40
  3.2 1.0 slice_bitcast_fusion.7
  4.3 0.8 fusion.18
  5.1 94.1 %gather_weights.1 = (bf16[2,16,48,1664]{3,2,1,0:T(8,128)(2,1)S(1)}, bf16[2,16,48,3072]{3,2,1,0:T(8,128)(2,1)S(1)}, bf16[16,2,96,768]{3,2,1,0:T(8,128)(2,1)S(1)}) custom-call(bf16[2,32,1664]{2,1,0:T(8,128)(2,1)S(1)} %fusion.15.a_shard, bf16[2,32,3072]{2,1,0:T(8,128)(2,1)S(1)} %fusion.14.g_shard, bf16[96,768]{1,0:T(8,128)(2,1)S(1)} %copy-done.1), custom_call_target="tpu_custom_call" | custom-call | tf_op jit(solution)/shard_map/gather_weights/pallas_call | solution.py:281
  99.2 3.6 %copy-done.2 = bf16[2,16,48,3072]{3,2,1,0:T(8,128)(2,1)} copy-done((bf16[2,16,48,3072]{3,2,1,0:T(8,128)(2,1)}, bf16[2,16,48,3072]{3,2,1,0:T(8,128)(2,1)S(1)}, u32[]{:S(2)}) %copy-start.2) | copy-done | bytes 9437208
  102.8 0.8 fusion.6
  103.6 1.4 fusion
  105.0 1.7 fusion.26
  106.7 0.1 pad_maximum_fusion.3
  106.8 0.6 collective-permute-start
  107.5 0.9 copy.44.valid
  108.3 0.1 copy.49
  108.5 0.6 pad_convert_fusion.vectors
  109.1 2.1 convert_select_fusion.refs_3_
  111.2 2.0 broadcast_select_fusion
  113.2 1.9 pad_maximum_fusion.2
  115.0 22.5 %attend.1 = (bf16[512,768]{1,0:T(8,128)(2,1)}, f32[16,512]{1,0:T(8,128)}) custom-call(bf16[512,768]{1,0:T(8,128)(2,1)} %get-tuple-element.58.refs_0_, bf16[1024,768]{1,0:T(8,128)(2,1)} %get-tuple-element.54.refs_1_, bf16[1024,768]{1,0:T(8,128)(2,1)} %get-tuple-element.53.refs_2_, f32[1024,512]{1,0:T(8,128)} %convert_select_fusion.refs_3_), custom_call_target="tpu_custom_call" | custom-call | flops 1610612736 | bytes 6291456 | tf_op jit(solution)/shard_map/attend/pallas_call | solution.py:625
  137.5 37.5 %feed_forward.1 = (bf16[512,768]{1,0:T(8,128)(2,1)}, f32[512,768]{1,0:T(8,128)}, bf16[512,768]{1,0:T(8,128)(2,1)}, bf16[768,768]{1,0:T(8,128)(2,1)}, bf16[2,768,...) custom-call(bf16[512,768]{1,0:T(8,128)(2,1)} %bitcast.85, ...), custom_call_target="tpu_custom_call" | custom-call | flops 23555211264 | bytes 42467328 | tf_op jit(solution)/shard_map/feed_forward/pallas_call | solution.py:532
  175.0 24.0 %attend_back.1 = (bf16[512,768]{1,0:T(8,128)(2,1)}, f32[1024,768]{1,0:T(8,128)}, f32[1024,768]{1,0:T(8,128)}) custom-call(bf16[512,768]{1,0:T(8,128)(2,1)} %get-tuple-element.58.refs_0_, bf16[1024,768]{1,0:T(8,128)(2,1)} %get-tuple-element.54.refs_1_, bf16[1024,768]{1,0:T(8,128)(2,1)} %get-tuple-element.53.refs_2_, f32[1024,512]{1,0:T(8,128)} %convert_select_fusion.refs_3_, ...), custom_call_target="tpu_custom_call" | custom-call | flops 4026531840 | bytes 12582912 | tf_op jit(solution)/shard_map/attend_back/pallas_call | solution.py:697
  199.1 2.5 constant_dynamic-update-slice_fusion.1
  201.6 0.3 copy-done.5
  201.9 0.5 constant_dynamic-update-slice_fusion
  202.4 2.7 copy-done.4
  205.1 1.4 select_convert_fusion
  206.5 0.5 collective-permute-start.1
  206.9 3.2 collective-permute-done.1
  210.2 3.7 %add_convert_fusion = bf16[512,1536]{1,0:T(8,128)(2,1)S(1)} fusion(bf16[512,1536]{1,0:T(8,128)(2,1)S(1)} %collective-permute-done.1, f32[1024,1536]{1,0:T(8,128)} %copy-done.4, pred[]{:T(512)S(6)} %eq.27), kind=kLoop, calls=%fused_computation.4 | loop fusion | flops 3145728 | bytes 9437185 | tf_op jit(solution)/shard_map/convert.6
  213.9 0.1 slice.99
  213.9 0.8 fusion.5
  214.8 0.2 copy-done.15
  215.0 4.3 %fusion.3 = f32[512,768]{1,0:T(8,128)} fusion(bf16[2,768,1664]{2,1,0:T(8,128)(2,1)} %bitcast.68, bf16[512,768]{1,0:T(8,128)(2,1)S(1)} %slice.99, bf16[512,768]{1,0:T(8,128)(2,1)S(1)} %copy-done.15), kind=kOutput, calls=%fused_computation.14 | convolution fusion | flops 1211105280 | bytes 5505024 | tf_op jit(solution)/shard_map/dot_general | solution.py:17
  219.2 1.4 convolution_convert_fusion
  220.7 0.2 pad_maximum_fusion.1
  220.9 2.6 pad_maximum_fusion.a_grad
  223.5 103.4 %scatter_grads.1 = (f32[24,2304]{1,0:T(8,128)}, f32[24,768]{1,0:T(8,128)}, f32[24,6144]{1,0:T(8,128)}, f32[96,768]{1,0:T(8,128)}, f32[16,768]{1,0:T(8,128)}) custom-call(bf16[2,16,48,1536]{3,2,1,0:T(8,128)(2,1)} %pad_maximum_fusion.a_grad, bf16[2,16,48,3072]{3,2,1,0:T(8,128)(2,1)} %bitcast.72, bf16[16,2,96,768]{3,2,1,0:T(8,128)(2,1)} %bitcast.74, ...), custom_call_target="tpu_custom_call" | custom-call | tf_op jit(solution)/shard_map/scatter_grads/pallas_call | solution.py:386
  327.0 1.2 slice.89
  328.2 0.9 slice_reduce_fusion
  329.1 0.1 constant_dynamic-slice_fusion
  329.2 0.5 slice_bitcast_fusion.8
  329.7 3.6 %fusion.7 = bf16[1,512,768]{2,1,0:T(8,128)(2,1)} fusion(f32[512,768]{1,0:T(8,128)S(1)} %copy-done.6, f32[512,768]{1,0:T(8,128)} %fusion.3, bf16[2,768,1664]{2,1,0:T(8,128)(2,1)} %bitcast.69, bf16[512,1536]{1,0:T(8,128)(2,1)S(1)} %add_convert_fusion), kind=kOutput, calls=%fused_computation.26 | convolution fusion | flops 605159424 | bytes 5898240 | tf_op jit(solution)/shard_map/dot_general | solution.py:17
  333.9 0.5 divide_sqrt_fusion
  334.5 0.7 copy.55
  335.1 0.6 copy.56
  335.8 0.8 copy.57
  336.6 0.7 copy.58
  (37 shorter events, 0.2 us)
Async XLA Ops:
  0.6 4.5 %copy-start.1 = (bf16[96,768]{1,0:T(8,128)(2,1)S(1)}, bf16[96,768]{1,0:T(8,128)(2,1)}, u32[]{:S(2)}) copy-start(bf16[96,768]{1,0:T(8,128)(2,1)} %d_own.1) | copy-start | bytes 442372
  0.7 102.2 %copy-start.13 = (bf16[1,512,768]{2,1,0:T(8,128)(2,1)S(1)}, bf16[1,512,768]{2,1,0:T(8,128)(2,1)}, u32[]{:S(2)}) copy-start(bf16[1,512,768]{2,1,0:T(8,128)(2,1)} %param.11) | copy-start | bytes 2359300
  99.2 3.6 %copy-start.2 = (bf16[2,16,48,3072]{3,2,1,0:T(8,128)(2,1)}, bf16[2,16,48,3072]{3,2,1,0:T(8,128)(2,1)S(1)}, u32[]{:S(2)}) copy-start(bf16[2,16,48,3072]{3,2,1,0:T(8,128)(2,1)S(1)} %get-tuple-element.33) | copy-start | bytes 28311556
  102.8 2.2 copy-start.3
  102.8 4.6 %copy-start = (bf16[2,16,48,1664]{3,2,1,0:T(8,128)(2,1)}, bf16[2,16,48,1664]{3,2,1,0:T(8,128)(2,1)S(1)}, u32[]{:S(2)}) copy-start(bf16[2,16,48,1664]{3,2,1,0:T(8,128)(2,1)S(1)} %get-tuple-element.31) | copy-start | bytes 15335428
  106.7 0.7 copy-start.12
  106.8 4.4 %collective-permute-start = (bf16[512,1536]{1,0:T(8,128)(2,1)S(1)}, bf16[512,1536]{1,0:T(8,128)(2,1)}, u32[]{:S(2)}, u32[]{:S(2)}) collective-permute-start(bf16[512,1536]{1,0:T(8,128)(2,1)S(1)} %pad_maximum_fusion.3), channel_id=1, source_target_pairs={{0,1},{1,0},{2,3},{3,2},{4,5},{5,4},{6,7},{7,6},{8,9},{9,8},{10,11... | collective-permute-start | bytes 4718600 | tf_op jit(solution)/shard_map/ppermute | solution.py:724
  199.1 2.8 copy-start.5
  202.4 2.7 copy-start.4
  206.5 3.7 %collective-permute-start.1 = (bf16[512,1536]{1,0:T(8,128)(2,1)}, bf16[512,1536]{1,0:T(8,128)(2,1)S(1)}, u32[]{:S(2)}, u32[]{:S(2)}) collective-permute-start(bf16[512,1536]{1,0:T(8,128)(2,1)} %select_convert_fusion), channel_id=1, source_target_pairs={{0,1},{1,0},{2,3},{3,2},{4,5},{5,4},{6,7},{7,6},{8,9},{9,8},{10,11... | collective-permute-start | bytes 4718600 | tf_op jit(solution)/shard_map/ppermute | solution.py:738
  206.9 7.0 %copy-start.14 = (bf16[1,512,768]{2,1,0:T(8,128)(2,1)S(1)}, bf16[1,512,768]{2,1,0:T(8,128)(2,1)}, u32[]{:S(2)}) copy-start(bf16[1,512,768]{2,1,0:T(8,128)(2,1)} %param.11) | copy-start | bytes 2359300
  213.8 1.1 copy-start.15
  219.2 1.5 copy-start.7
  223.5 106.2 %copy-start.6 = (f32[512,768]{1,0:T(8,128)S(1)}, f32[512,768]{1,0:T(8,128)}, u32[]{:S(2)}) copy-start(f32[512,768]{1,0:T(8,128)} %get-tuple-element.36) | copy-start | bytes 4718596
  329.7 4.8 %copy-start.10 = (f32[24,2304]{1,0:T(8,128)S(1)}, f32[24,2304]{1,0:T(8,128)}, u32[]{:S(2)}) copy-start(f32[24,2304]{1,0:T(8,128)} %get-tuple-element.82) | copy-start | bytes 663556
  329.7 5.4 %copy-start.11 = (f32[24,768]{1,0:T(8,128)S(1)}, f32[24,768]{1,0:T(8,128)}, u32[]{:S(2)}) copy-start(f32[24,768]{1,0:T(8,128)} %get-tuple-element.83) | copy-start | bytes 221188
  329.7 6.1 %copy-start.8 = (f32[24,6144]{1,0:T(8,128)S(1)}, f32[24,6144]{1,0:T(8,128)}, u32[]{:S(2)}) copy-start(f32[24,6144]{1,0:T(8,128)} %get-tuple-element.86) | copy-start | bytes 1769476
  329.7 6.9 %copy-start.9 = (f32[96,768]{1,0:T(8,128)S(1)}, f32[96,768]{1,0:T(8,128)}, u32[]{:S(2)}) copy-start(f32[96,768]{1,0:T(8,128)} %get-tuple-element.87) | copy-start | bytes 884740

commit v3 on v2

--- a/solution.py
+++ b/solution.py
@@ -62,23 +62,22 @@
     def __init__(self, send, recv):
         self.send, self.recv, self.open = send, recv, []
 
-    def put(self, src, dst, slot, peer):
-        copy = pltpu.make_async_remote_copy(
+    def of(self, src, dst, slot, peer):
+        return pltpu.make_async_remote_copy(
             src_ref=src, dst_ref=dst, send_sem=self.send.at[slot], recv_sem=self.recv.at[slot],
             device_id=peer, device_id_type=MESH,
         )
-        copy.start()
-        self.open.append(copy)
+
+    def put(self, src, dst, slot, peer, like=None):
+        self.of(src, dst, slot, peer).start()
+        self.open.append((like or (lambda: dst), slot))
 
     def got(self, dst, slot, peer):
-        pltpu.make_async_remote_copy(
-            src_ref=dst, dst_ref=dst, send_sem=self.send.at[slot], recv_sem=self.recv.at[slot],
-            device_id=peer, device_id_type=MESH,
-        ).wait_recv()
-
-    def drain(self):
-        for copy in self.open:
-            copy.wait_send()
+        self.of(dst, dst, slot, peer).wait_recv()
+
+    def drain(self, peer):
+        for like, slot in self.open:
+            self.of(like(), like(), slot, peer).wait_send()
         self.open = []
 
 
@@ -93,23 +92,26 @@
     def block(self, k, j):
         return self.out(self.p.c, self.p.at(k, j))
 
+    def send(self, src, dst, slot, peer):
+        self.cp.put(src, dst, slot, peer, lambda: self.own)
+
     def push(self, src, k, j):
-        self.cp.put(src, self.block(k, j), self.slot("s", k, j), self.p.sib)
-
-    def own_z(self):
-        for k in (1, 2, 3):
-            self.cp.put(self.own, self.block(0, "o"), self.slot("z", k), self.p.zn[k])
-
-    def own_xy(self):
-        self.spread(self.own, 0)
+        self.send(src, self.block(k, j), self.slot("s", k, j), self.p.sib)
+
+    def to_z(self, k):
+        if k:
+            self.send(self.own, self.block(0, "o"), self.slot("z", k), self.p.zn[k])
 
     def spread(self, src, k):
         dst = self.block(k, "o")
-        self.cp.put(src, dst, self.slot("x", k), self.p.xn)
-        self.cp.put(src, dst, self.slot("y", k), self.p.yn)
+        self.send(src, dst, self.slot("x", k), self.p.xn)
+        self.send(src, dst, self.slot("y", k), self.p.yn)
         self.push(src, k, "o")
 
     def from_z(self, k):
+        if k == 0:
+            self.spread(self.own, 0)
+            return
         block = self.block(k, "o")
         self.cp.got(block, self.slot("z", k), self.p.zn[k])
         self.spread(block, k)
@@ -117,17 +119,27 @@
     def from_xy(self, k):
         x, y = self.block(k, "x"), self.block(k, "y")
         self.cp.got(x, self.slot("x", k), self.p.xn)
-        if k >= 2:
-            self.cp.put(x, x, self.slot("d", k), self.p.yn)
+        if k == 2:
+            self.send(x, x, self.slot("d", k), self.p.yn)
+        self.cp.got(y, self.slot("y", k), self.p.yn)
+        if k == 0:
+            self.send(y, y, self.slot("d", k), self.p.xn)
         self.push(x, k, "x")
-        self.cp.got(y, self.slot("y", k), self.p.yn)
-        if k < 2:
-            self.cp.put(y, y, self.slot("d", k), self.p.xn)
         self.push(y, k, "y")
+
+    def from_even(self, k):
+        if k % 2 == 0:
+            self.from_d(k)
+
+    def from_odd(self, k):
+        if k % 2:
+            self.from_d(k)
 
     def from_d(self, k):
         block = self.block(k, "d")
         self.cp.got(block, self.slot("d", k), self.p.xn)
+        if k % 2 == 0:
+            self.send(block, block, self.slot("d", k + 1), self.p.zn[1])
         self.push(block, k, "d")
 
     def from_sib(self):
@@ -137,73 +149,113 @@
                 self.cp.got(block, self.slot("s", k, j), self.p.sib)
 
 
-def low_add(left, right):
-    return left + right
-
-
 class Scatter:
-    def __init__(self, place, copies, base, local, grad, own, sib, rly, xin, yin, out, zin):
-        self.p, self.cp, self.base, self.local, self.grad = place, copies, base, local, grad
-        self.own, self.sib, self.rly, self.xin, self.yin, self.out, self.zin = own, sib, rly, xin, yin, out, zin
+    def __init__(self, place, copies, base, give, own, sib, rly, dia, xin, yin, zin, load=None):
+        self.p, self.cp, self.base, self.give, self.own, self.load = place, copies, base, give, own, load
+        self.sib, self.rly, self.dia, self.xin, self.yin, self.zin = sib, rly, dia, xin, yin, zin
 
     def slot(self, kind, k):
-        return self.base + {"s": 0, "r": 4, "x": 8, "y": 12, "z": 15}[kind] + k
-
-    def load(self, k):
-        four = pl.ds(self.p.plane(k) * 4, 4)
-        return pltpu.make_async_copy(self.grad(self.p.c, four), self.own.at[four], self.local.at[self.base + k])
+        return self.base + {"s": 0, "r": 4, "d": 5, "x": 8, "y": 12, "z": 15}[kind] + k
+
+    def four(self, k):
+        return pl.ds(self.p.plane(k) * 4, 4)
 
     def begin(self, k):
-        four = pl.ds(self.p.plane(k) * 4, 4)
-        self.cp.put(self.grad(1 - self.p.c, four), self.sib.at[four], self.slot("s", k), self.p.sib)
-        self.load(k).start()
+        four = self.four(k)
+        self.cp.put(self.give(four), self.sib.at[four], self.slot("s", k), self.p.sib, lambda: self.sib.at[pl.ds(0, 4)])
+        if self.load is not None:
+            self.load(four, self.base + k).start()
+
+    def to_x(self, own, k):
+        self.cp.put(own, self.xin.at[k], self.slot("x", k), self.p.xn, lambda: self.xin.at[k])
+
+    def to_y(self, own, k):
+        self.cp.put(own, self.yin.at[k], self.slot("y", k), self.p.yn, lambda: self.yin.at[k])
+
+    def both(self, k, j, *more):
+        at = self.p.at(k, j)
+        own = self.own(at)
+        total = own[...] + self.sib[at]
+        for ref in more:
+            total = total + ref[...]
+        own[...] = total
+        return own
 
     def pair(self, k):
-        p = self.p
-        four = pl.ds(p.plane(k) * 4, 4)
-        self.load(k).wait()
-        self.cp.got(self.sib.at[four], self.slot("s", k), p.sib)
-        d, x, y = p.at(k, "d"), p.at(k, "x"), p.at(k, "y")
-        self.own[d] = low_add(self.own[d], self.sib[d])
-        self.cp.put(self.own.at[d], self.rly.at[k], self.slot("r", k), p.xn if k < 2 else p.yn)
-        if k < 2:
-            self.own[x] = low_add(self.own[x], self.sib[x])
-            self.cp.put(self.own.at[x], self.xin.at[k], self.slot("x", k), p.xn)
+        four = self.four(k)
+        if self.load is not None:
+            self.load(four, self.base + k).wait()
+        self.cp.got(self.sib.at[four], self.slot("s", k), self.p.sib)
+        if k % 2:
+            i = k // 2
+            dia = lambda: self.dia.at[i]
+            self.cp.put(self.both(k, "d"), dia(), self.slot("d", 2 * i), self.p.zn[1], dia)
+        if k != 2:
+            self.to_x(self.both(k, "x"), k)
+        if k != 0:
+            self.to_y(self.both(k, "y"), k)
+
+    def diag(self, k):
+        if k % 2:
+            return
+        i = k // 2
+        self.cp.got(self.dia.at[i], self.slot("d", k), self.p.zn[1])
+        own = self.both(k, "d", self.dia.at[i])
+        peer = self.p.xn if k == 0 else self.p.yn
+        self.cp.put(own, self.rly.at[i], self.slot("r", k), peer, lambda: self.rly.at[i])
+
+    def relay(self, k):
+        if k % 2:
+            return
+        i = k // 2
+        self.cp.got(self.rly.at[i], self.slot("r", k), self.p.xn)
+        if k == 0:
+            self.to_y(self.both(k, "y", self.rly.at[i]), k)
         else:
-            self.own[y] = low_add(self.own[y], self.sib[y])
-            self.cp.put(self.own.at[y], self.yin.at[k], self.slot("y", k), p.yn)
-
-    def relay(self, k):
-        p = self.p
-        x, y = p.at(k, "x"), p.at(k, "y")
-        self.cp.got(self.rly.at[k], self.slot("r", k), p.xn)
-        if k < 2:
-            self.own[y] = low_add(low_add(self.own[y], self.sib[y]), self.rly[k])
-            self.cp.put(self.own.at[y], self.yin.at[k], self.slot("y", k), p.yn)
-        else:
-            self.own[x] = low_add(low_add(self.own[x], self.sib[x]), self.rly[k])
-            self.cp.put(self.own.at[x], self.xin.at[k], self.slot("x", k), p.xn)
+            self.to_x(self.both(k, "x", self.rly.at[i]), k)
 
     def plane(self, k):
         p = self.p
-        o = p.at(k, "o")
+        at = p.at(k, "o")
         self.cp.got(self.xin.at[k], self.slot("x", k), p.xn)
         self.cp.got(self.yin.at[k], self.slot("y", k), p.yn)
         wide = jnp.float32
-        total = (self.own[o].astype(wide) + self.sib[o].astype(wide)) + (
+        own = self.own(at)
+        total = (own[...].astype(wide) + self.sib[at].astype(wide)) + (
             self.xin[k].astype(wide) + self.yin[k].astype(wide)
         )
-        self.out[k] = total.astype(jnp.bfloat16)
+        own[...] = total.astype(jnp.bfloat16)
         if k:
-            self.cp.put(self.out.at[k], self.zin.at[k - 1], self.slot("z", k), p.zn[k])
+            self.cp.put(own, self.zin.at[k - 1], self.slot("z", k), p.zn[k], lambda: self.zin.at[k - 1])
 
     def total(self):
         for k in (1, 2, 3):
             self.cp.got(self.zin.at[k - 1], self.slot("z", k), self.p.zn[k])
         wide = jnp.float32
-        return (self.out[0].astype(wide) + self.zin[0].astype(wide)) + (
+        own = self.own(self.p.at(0, "o"))
+        return (own[...].astype(wide) + self.zin[0].astype(wide)) + (
             self.zin[1].astype(wide) + self.zin[2].astype(wide)
         )
+
+
+class Steps:
+    def __init__(self, items, stages):
+        self.items, self.stages = items, stages
+
+    def __call__(self, t):
+        for name, lag in self.stages:
+            if 0 <= t - lag < len(self.items):
+                matrix, planes = self.items[t - lag]
+                for k in planes:
+                    getattr(matrix, name)(k)
+
+    def count(self):
+        return len(self.items) + max(lag for _, lag in self.stages)
+
+
+gather_stages = (("to_z", -2), ("from_z", 0), ("from_xy", 1), ("from_even", 2), ("from_odd", 3))
+scatter_stages = (("begin", -2), ("pair", 0), ("diag", 1), ("relay", 2), ("plane", 3))
+near_far, far_near = ((0, 1), (2, 3)), ((3, 2), (1, 0))
 
 
 rows_chip = 48
@@ -218,15 +270,15 @@
     for i, (shard, other) in enumerate(((a_shard, a_pair), (g_shard, g_pair))):
         pairs.put(shard.at[1 - c], other, i, place.sib)
     copies = Copies(send, recv)
-    a_out = lambda half, r: a_full.at[half, r]
-    g_out = lambda half, r: g_full.at[half, r]
-    d_out = lambda half, r: d_full.at[r, half]
-    mats = [
-        Gather(place, copies, 0, a_own, a_out),
-        Gather(place, copies, gather_slots, g_own, g_out),
-        Gather(place, copies, 2 * gather_slots, d_own, d_out),
+    half_g = g_full.shape[3] // 2
+    outs = [
+        lambda half, r: a_full.at[half, r],
+        lambda half, r: g_full.at[half, r, :, :half_g],
+        lambda half, r: g_full.at[half, r, :, half_g:],
+        lambda half, r: d_full.at[r, half],
     ]
-    att, gat, dow = mats
+    owns = [a_own, g_own.at[:, :half_g], g_own.at[:, half_g:], d_own]
+    mats = [Gather(place, copies, i * gather_slots, own, out) for i, (own, out) in enumerate(zip(owns, outs))]
 
     def assemble(shard, other, own, i):
         pairs.got(other, i, place.sib)
@@ -239,40 +291,21 @@
 
     kept = [pltpu.make_async_copy(m.own, m.block(0, "o"), local.at[i]) for i, m in enumerate(mats)]
     assemble(a_shard, a_pair, a_own, 0)
-    att.own_z()
-    att.own_xy()
+    steps = Steps([(m, planes) for m in mats for planes in near_far], gather_stages)
+    steps(-2)
+    steps(-1)
     kept[0].start()
     assemble(g_shard, g_pair, g_own, 1)
-    gat.own_z()
-    dow.own_z()
-    kept[1].start()
-    kept[2].start()
-    for k in (1, 2, 3):
-        att.from_z(k)
-    for k in range(4):
-        att.from_xy(k)
-    gat.own_xy()
-    for k in (1, 2, 3):
-        gat.from_z(k)
-    for k in range(4):
-        att.from_d(k)
-    for k in range(4):
-        gat.from_xy(k)
-    dow.own_xy()
-    for k in (1, 2, 3):
-        dow.from_z(k)
-    for k in range(4):
-        gat.from_d(k)
-    for k in range(4):
-        dow.from_xy(k)
-    for k in range(4):
-        dow.from_d(k)
+    for copy in kept[1:]:
+        copy.start()
+    for t in range(steps.count()):
+        steps(t)
     for m in mats:
         m.from_sib()
     for copy in kept:
         copy.wait()
-    pairs.drain()
-    copies.drain()
+    pairs.drain(place.sib)
+    copies.drain(place.sib)
 
 
 def gather_weights(a_shard, g_shard, d_shard):
@@ -293,124 +326,15 @@
             pltpu.VMEM((rows_chip, half_a), low),
             pltpu.VMEM((rows_chip, half_g), low),
             pltpu.SemaphoreType.DMA((2, 2)),
-            pltpu.SemaphoreType.DMA((3 * gather_slots,)),
-            pltpu.SemaphoreType.DMA((3 * gather_slots,)),
-            pltpu.SemaphoreType.DMA((3,)),
+            pltpu.SemaphoreType.DMA((4 * gather_slots,)),
+            pltpu.SemaphoreType.DMA((4 * gather_slots,)),
+            pltpu.SemaphoreType.DMA((4,)),
         ],
         compiler_params=pltpu.CompilerParams(
             collective_id=0, has_side_effects=True, vmem_limit_bytes=32 * 2**20
         ),
         name="gather_weights",
     )(a_shard, g_shard, d_shard)
-
-
-def scatter_kernel(
-    a_grad, g_grad, d_grad, small, qkv_out, wout_out, gu_out, down_out, small_out, *scratch
-):
-    place = Place()
-    place.greet()
-    c = place.c
-    bufs, (a_sum, g_sum, a_fin, g_fin, small_buf, send, recv, local, fin_sem) = scratch[:21], scratch[21:]
-    copies = Copies(send, recv)
-    last = Copies(fin_sem.at[0], fin_sem.at[1])
-    a_at = lambda half, four: a_grad.at[half, four]
-    g_at = lambda half, four: g_grad.at[half, four]
-    d_at = lambda half, four: d_grad.at[four, half]
-    mats = [
-        Scatter(place, copies, i * scatter_slots, local, at, *bufs[7 * i : 7 * i + 7])
-        for i, at in enumerate((g_at, d_at, a_at))
-    ]
-    order = [(m, k) for m in mats for k in (3, 2, 1, 0)]
-    depth = 3
-    steps = ["begin", "pair", "relay", "plane"]
-    hops = ((place.sib, 0), (place.xn, 1), (place.yn, 2))
-
-    def exchange(i):
-        peer, slot = hops[i]
-        last.put(small_buf.at[i], small_buf.at[4 + i], slot, peer)
-
-    def combine(i):
-        peer, slot = hops[i]
-        last.got(small_buf.at[4 + i], slot, peer)
-        small_buf[i + 1] = small_buf[i] + small_buf[4 + i]
-
-    small_buf[0] = small[...]
-    exchange(0)
-    for t in range(len(order) + depth):
-        for s, name in enumerate(steps):
-            if 0 <= t - s < len(order):
-                m, k = order[t - s]
-                getattr(m, name)(k)
-        if 1 <= t <= 3:
-            combine(t - 1)
-            if t < 3:
-                exchange(t)
-            else:
-                for k in (1, 2, 3):
-                    last.put(small_buf.at[3], small_buf.at[6 + k], 2 + k, place.zn[k])
-    for k in (1, 2, 3):
-        last.got(small_buf.at[6 + k], 2 + k, place.zn[k])
-    small_out[...] = (small_buf[3] + small_buf[7]) + (small_buf[8] + small_buf[9])
-    gate, down, att = mats
-    down_out[...] = down.total()
-    g_sum[...] = gate.total()
-    mine, theirs = pl.ds(pl.multiple_of(24 * c, 8), 24), pl.ds(pl.multiple_of(24 - 24 * c, 8), 24)
-    last.put(g_sum.at[theirs], g_fin, 6, place.sib)
-    a_sum[...] = att.total()
-    last.put(a_sum.at[theirs], a_fin, 7, place.sib)
-    first = c == 0
-    last.got(g_fin, 6, place.sib)
-    last.got(a_fin, 7, place.sib)
-    half_g = g_fin.shape[1]
-    gu_out[:, :half_g] = jnp.where(first, g_sum[mine], g_fin[...])
-    gu_out[:, half_g:] = jnp.where(first, g_fin[...], g_sum[mine])
-    left = jnp.where(first, a_sum[mine], a_fin[...])
-    right = jnp.where(first, a_fin[...], a_sum[mine])
-    cut = qkv_out.shape[1] - left.shape[1]
-    qkv_out[:, : left.shape[1]] = left
-    qkv_out[:, left.shape[1] :] = right[:, :cut]
-    wout_out[...] = right[:, cut:]
-    copies.drain()
-    last.drain()
-
-
-def scatter_grads(a_grad, g_grad, d_grad, small):
-    low = jnp.bfloat16
-    bufs = []
-    for rows, half in ((rows_chip, g_grad.shape[-1]), d_grad.shape[2:], (rows_chip, a_grad.shape[-1])):
-        for count in (16, 16, 4, 4, 4, 4, 3):
-            bufs.append(pltpu.VMEM((count, rows, half), low))
-    half_a, half_g = a_grad.shape[-1], g_grad.shape[-1]
-    width = d_grad.shape[-1]
-    wide = jnp.float32
-    return pl.pallas_call(
-        scatter_kernel,
-        out_shape=(
-            jax.ShapeDtypeStruct((24, 3 * width), wide),
-            jax.ShapeDtypeStruct((24, width), wide),
-            jax.ShapeDtypeStruct((24, 2 * half_g), wide),
-            jax.ShapeDtypeStruct(d_grad.shape[2:], wide),
-            jax.ShapeDtypeStruct(small.shape, wide),
-        ),
-        in_specs=[pl.BlockSpec(memory_space=pl.ANY)] * 3 + [pl.BlockSpec(memory_space=pltpu.VMEM)],
-        out_specs=(pl.BlockSpec(memory_space=pltpu.VMEM),) * 5,
-        scratch_shapes=bufs
-        + [
-            pltpu.VMEM((rows_chip, half_a), wide),
-            pltpu.VMEM((rows_chip, half_g), wide),
-            pltpu.VMEM((24, half_a), wide),
-            pltpu.VMEM((24, half_g), wide),
-            pltpu.VMEM((10,) + small.shape, wide),
-            pltpu.SemaphoreType.DMA((3 * scatter_slots,)),
-            pltpu.SemaphoreType.DMA((3 * scatter_slots,)),
-            pltpu.SemaphoreType.DMA((3 * scatter_slots,)),
-            pltpu.SemaphoreType.DMA((2, 8)),
-        ],
-        compiler_params=pltpu.CompilerParams(
-            collective_id=1, has_side_effects=True, vmem_limit_bytes=60 * 2**20
-        ),
-        name="scatter_grads",
-    )(a_grad, g_grad, d_grad, small)
 
 
 def dot(left, right, dims=((1,), (0,))):
@@ -641,53 +565,55 @@
     )(q, k, v, span)
 
 
-def attend_back_kernel(heads, q, k, v, span, lse, att, d_att, dq, dk, dv, q_t, k_t, do_t, dq_t, delta, dk_sum, dv_sum):
+def attend_back_pair(pair, heads, q, k, v, span, lse, att, d_att, dq, dk_sum, dv_sum):
     low, wide = jnp.bfloat16, jnp.float32
     rows, width = q.shape
     lanes = lane_width
     depth = width // heads
     chunk = 256
     scale = depth**-0.5
-
-    q_t[...] = (q[...].astype(wide) * scale).T.astype(low)
-    k_t[...] = k[...].astype(wide).T.astype(low)
-    do_wide = d_att[...].astype(wide)
-    do_t[...] = do_wide.T.astype(low)
-    both_t = (do_wide * att[...].astype(wide)).T
-    delta[...] = jnp.sum(both_t.reshape(heads, depth, rows), 1)
-
+    at = pl.ds(pl.multiple_of(pair * lanes, lanes), lanes)
+    keys, values = k[:, at], v[:, at]
+    keys_t = keys.astype(wide).T.astype(low)
+    for c in range(rows // chunk):
+        here = pl.ds(c * chunk, chunk)
+        q_wide = q[here, at].astype(wide) * scale
+        do_here = d_att[here, at]
+        do_wide = do_here.astype(wide)
+        q_here = q_wide.astype(low)
+        q_t, do_t = q_wide.T.astype(low), do_wide.T.astype(low)
+        both_t = (do_wide * att[here, at].astype(wide)).T
+        dk_part, dv_part, dq_parts = None, None, []
+        for h in (0, 1):
+            head = 2 * pair + h
+            own = slice(h * depth, (h + 1) * depth)
+            slope = jnp.exp2(jnp.full((1, 1), -8.0 / heads, wide) * (head + 1).astype(wide))
+            delta = jnp.sum(both_t[own], 0, keepdims=True)
+            logits = dot(keys, half_of(q_t, 0, h)) - slope * span[:, here]
+            probs = jnp.exp(logits - lse[pl.ds(head, 1), here])
+            d_probs = dot(values, half_of(do_t, 0, h))
+            d_logits = (probs * (d_probs - delta)).astype(low)
+            dv_term = dot(probs.astype(low), half_of(do_here, 1, h))
+            dk_term = dot(d_logits, half_of(q_here, 1, h))
+            dv_part = dv_term if dv_part is None else dv_part + dv_term
+            dk_part = dk_term if dk_part is None else dk_part + dk_term
+            dq_parts.append(dot(keys_t[own], d_logits) * scale)
+        if c == 0:
+            dk_sum[...] = dk_part
+            dv_sum[...] = dv_part
+        else:
+            dk_sum[...] += dk_part
+            dv_sum[...] += dv_part
+        dq[here, at] = jnp.concatenate(dq_parts, 0).T.astype(low)
+
+
+def attend_back_kernel(heads, q, k, v, span, lse, att, d_att, dq, dk, dv, dk_sum, dv_sum):
     @pl.loop(0, heads // 2)
     def _(pair):
-        at = pl.ds(pl.multiple_of(pair * lanes, lanes), lanes)
-        keys, values = k[:, at], v[:, at]
-        for c in range(rows // chunk):
-            here = pl.ds(c * chunk, chunk)
-            q_here = (q[here, at].astype(wide) * scale).astype(low)
-            do_here = d_att[here, at]
-            dk_part, dv_part = None, None
-            for h in (0, 1):
-                head = 2 * pair + h
-                own = pl.ds(pl.multiple_of(pair * lanes + h * depth, depth), depth)
-                slope = jnp.exp2(jnp.full((1, 1), -8.0 / heads, jnp.float32) * (head + 1).astype(wide))
-                logits = dot(keys, half_of(q_t[at, here], 0, h)) - slope * span[:, here]
-                probs = jnp.exp(logits - lse[pl.ds(head, 1), here])
-                d_probs = dot(values, half_of(do_t[at, here], 0, h))
-                d_logits = (probs * (d_probs - delta[pl.ds(head, 1), here])).astype(low)
-                dv_term = dot(probs.astype(low), half_of(do_here, 1, h))
-                dk_term = dot(d_logits, half_of(q_here, 1, h))
-                dv_part = dv_term if dv_part is None else dv_part + dv_term
-                dk_part = dk_term if dk_part is None else dk_part + dk_term
-                dq_t[own, here] = dot(k_t[own, :], d_logits) * scale
-            if c == 0:
-                dk_sum[...] = dk_part
-                dv_sum[...] = dv_part
-            else:
-                dk_sum[...] += dk_part
-                dv_sum[...] += dv_part
-        dk[:, at] = dk_sum[...].astype(dk.dtype)
-        dv[:, at] = dv_sum[...].astype(dv.dtype)
-
-    dq[...] = dq_t[...].T.astype(low)
+        attend_back_pair(pair, heads, q, k, v, span, lse, att, d_att, dq, dk_sum, dv_sum)
+        at = pl.ds(pl.multiple_of(pair * lane_width, lane_width), lane_width)
+        dk[:, at] = dk_sum[...]
+        dv[:, at] = dv_sum[...]
 
 
 def attend_back(q, k, v, span, lse, att, d_att, heads):
@@ -704,11 +630,6 @@
         in_specs=[pl.BlockSpec(memory_space=pltpu.VMEM)] * 7,
         out_specs=(pl.BlockSpec(memory_space=pltpu.VMEM),) * 3,
         scratch_shapes=[
-            pltpu.VMEM((width, rows), low),
-            pltpu.VMEM((width, keys), low),
-            pltpu.VMEM((width, rows), low),
-            pltpu.VMEM((width, rows), wide),
-            pltpu.VMEM((heads, rows), wide),
             pltpu.VMEM((keys, lane_width), wide),
             pltpu.VMEM((keys, lane_width), wide),
         ],
@@ -716,6 +637,233 @@
         cost_estimate=pl.CostEstimate(flops=10 * rows * keys * width, bytes_accessed=16 * keys * width, transcendentals=heads * rows * keys),
         name="attend_back",
     )(q, k, v, span, lse, att, d_att)
+
+
+def back_kernel(
+    heads, tokens, q, k, v, span, lse, att, d_att, d_resid_one, grad_out, a_full, g_grad, d_grad, small,
+    d_tokens, qkv_out, wout_out, gu_out, down_out, small_out, *scratch,
+):
+    place = Place()
+    place.greet()
+    c = place.c
+    low, wide = jnp.bfloat16, jnp.float32
+    tok_rows, width = tokens.shape
+    pairs = heads // 2
+    bufs, rest = scratch[:27], scratch[27:]
+    a_grad, dq, dkv_own, dkv_out, dkv_in, g_sum, a_sum, g_fin, a_fin, small_buf, send, recv, local, pair_sem, fin_sem, in_sem = rest
+    copies = Copies(send, recv)
+    last = Copies(fin_sem.at[0], fin_sem.at[1])
+    half_g = g_grad.shape[3] // 2
+
+    def scatter(i, source, own, sib, *more):
+        return Scatter(
+            place, copies, i * scatter_slots, lambda four: source(1 - c, four), lambda at: own.at[at], sib, *more,
+            load=lambda four, slot: pltpu.make_async_copy(source(c, four), own.at[four], local.at[slot]),
+        )
+
+    down = scatter(0, lambda half, four: d_grad.at[four, half], *bufs[:7])
+    gate = scatter(1, lambda half, four: g_grad.at[half, four, :, :half_g], *bufs[7:14])
+    rest = scatter(2, lambda half, four: g_grad.at[half, four, :, half_g:], *bufs[14:21])
+    proj = Scatter(
+        place, copies, 3 * scatter_slots, lambda four: a_grad.at[1 - c, four], lambda at: a_grad.at[c, at], *bufs[21:]
+    )
+    chunks = Steps([(m, planes) for m in (down, gate, rest, proj) for planes in far_near], scatter_stages)
+    hops = ((place.sib, 0), (place.xn, 1), (place.yn, 2))
+
+    def exchange(i):
+        peer, slot = hops[i]
+        last.put(small_buf.at[i], small_buf.at[4 + i], slot, peer, lambda: small_buf.at[4 + i])
+
+    def combine(i):
+        peer, slot = hops[i]
+        last.got(small_buf.at[4 + i], slot, peer)
+        small_buf[i + 1] = small_buf[i] + small_buf[4 + i]
+
+    def spread():
+        for z in (1, 2, 3):
+            last.put(small_buf.at[3], small_buf.at[6 + z], 2 + z, place.zn[z], lambda z=z: small_buf.at[6 + z])
+
+    chunks(-2)
+    chunks(-1)
+    small_buf[0] = small[...]
+    exchange(0)
+
+    def steps(pair):
+        for i in range(3):
+
+            @pl.when(pair == 2 * i + 1)
+            def _(i=i):
+                chunks(i + 1)
+                combine(i)
+                if i < 2:
+                    exchange(i + 1)
+                else:
+                    spread()
+
+    half = lambda side: pl.ds(pl.multiple_of(side * tok_rows, tok_rows), tok_rows)
+
+    def send_dkv(pair):
+        return pltpu.make_async_remote_copy(
+            src_ref=dkv_out.at[pair], dst_ref=dkv_in.at[pair], send_sem=pair_sem.at[0, pair],
+            recv_sem=pair_sem.at[1, pair], device_id=place.sib, device_id_type=MESH,
+        )
+
+    def attention(q_v, k_v, v_v, span_v, att_v, datt_v, dk_sum, dv_sum):
+        loads = [
+            pltpu.make_async_copy(src, dst, in_sem.at[i])
+            for i, (src, dst) in enumerate(
+                ((q, q_v), (k, k_v), (v, v_v), (span, span_v), (att, att_v), (d_att, datt_v))
+            )
+        ]
+        for copy in loads:
+            copy.start()
+        chunks(0)
+        for copy in loads:
+            copy.wait()
+
+        @pl.loop(0, pairs)
+        def _(pair):
+            attend_back_pair(
+                pair, heads, q_v, k_v, v_v, span_v, lse, att_v, datt_v, dq, dk_sum, dv_sum
+            )
+            for i, part in enumerate((dk_sum, dv_sum)):
+                dkv_own[pair, i] = part[half(c), :]
+                dkv_out[pair, i] = part[half(1 - c), :].astype(low)
+            send_dkv(pair).start()
+            steps(pair)
+
+    block = lambda *shape: pltpu.VMEM(shape, low)
+    key_rows = k.shape[0]
+    pl.run_scoped(
+        attention, block(*q.shape), block(*k.shape), block(*v.shape), pltpu.VMEM(span.shape, wide),
+        block(*att.shape), block(*d_att.shape), pltpu.VMEM((key_rows, lane_width), wide),
+        pltpu.VMEM((key_rows, lane_width), wide),
+    )
+
+    def finish(w_left, w_right, resid, x_t, d_k, d_v):
+        loads = [
+            pltpu.make_async_copy(a_full.at[0, :, : 2 * width], w_left, in_sem.at[0]),
+            pltpu.make_async_copy(a_full.at[1, :, :width], w_right, in_sem.at[1]),
+            pltpu.make_async_copy(d_resid_one, resid, in_sem.at[2]),
+            pltpu.make_async_copy(grad_out, a_grad.at[1, :, :, width:], in_sem.at[3]),
+        ]
+        for copy in loads:
+            copy.start()
+        x_t[...] = tokens[...].astype(wide).T.astype(low)
+        for pair in range(pairs):
+            send_dkv(pair).wait_recv()
+            at = slice(pair * lane_width, (pair + 1) * lane_width)
+            d_k[:, at] = (dkv_own[pair, 0] + dkv_in[pair, 0].astype(wide)).astype(low)
+            d_v[:, at] = (dkv_own[pair, 1] + dkv_in[pair, 1].astype(wide)).astype(low)
+        tile = width // 2
+        for side, at, src in ((0, 0, dq), (0, width, d_k), (1, 0, d_v)):
+            for part in range(2):
+                cols = slice(part * tile, (part + 1) * tile)
+                term = dot(x_t[...], src[:, cols]).astype(low)
+                a_grad[side, :, :, at + part * tile : at + (part + 1) * tile] = term.reshape(16, rows_chip, tile)
+        loads[3].wait()
+        chunks(4)
+        for copy in loads[:3]:
+            copy.wait()
+        total = resid[...] + dot(dq[...], w_left[:, :width], ((1,), (1,)))
+        chunks(5)
+        total += dot(d_k[...], w_left[:, width:], ((1,), (1,))) + dot(d_v[...], w_right[...], ((1,), (1,)))
+        d_tokens[...] = total.astype(low)
+
+    pl.run_scoped(
+        finish, block(width, 2 * width), block(width, width), pltpu.VMEM((tok_rows, width), wide),
+        block(width, tok_rows), block(tok_rows, width), block(tok_rows, width),
+    )
+    for z in (1, 2, 3):
+        last.got(small_buf.at[6 + z], 2 + z, place.zn[z])
+    small_out[...] = (small_buf[3] + small_buf[7]) + (small_buf[8] + small_buf[9])
+    mine, theirs = pl.ds(pl.multiple_of(24 * c, 8), 24), pl.ds(pl.multiple_of(24 - 24 * c, 8), 24)
+    chunks(6)
+    down_out[...] = down.total()
+    chunks(7)
+    g_sum[0] = gate.total()
+    last.put(g_sum.at[0, theirs], g_fin.at[0], 6, place.sib, lambda: g_fin.at[0])
+    chunks(8)
+    chunks(9)
+    g_sum[1] = rest.total()
+    last.put(g_sum.at[1, theirs], g_fin.at[1], 8, place.sib, lambda: g_fin.at[1])
+    chunks(10)
+    first = c == 0
+    for i, slot in ((0, 6), (1, 8)):
+        last.got(g_fin.at[i], slot, place.sib)
+        own, other = g_sum[i, mine], g_fin[i]
+        gu_out[:, i * half_g : (i + 1) * half_g] = jnp.where(first, own, other)
+        gu_out[:, (i + 2) * half_g : (i + 3) * half_g] = jnp.where(first, other, own)
+    a_sum[...] = proj.total()
+    last.put(a_sum.at[theirs], a_fin, 7, place.sib, lambda: a_fin)
+    last.got(a_fin, 7, place.sib)
+    left = jnp.where(first, a_sum[mine], a_fin[...])
+    right = jnp.where(first, a_fin[...], a_sum[mine])
+    qkv_out[:, : 2 * width] = left
+    qkv_out[:, 2 * width :] = right[:, :width]
+    wout_out[...] = right[:, width:]
+
+    @pl.loop(0, pairs)
+    def _(pair):
+        send_dkv(pair).wait_send()
+
+    copies.drain(place.sib)
+    last.drain(place.sib)
+
+
+def back(heads, tokens, q, k, v, span, lse, att, d_att, d_resid_one, grad_out, a_full, g_grad, d_grad, small):
+    low, wide = jnp.bfloat16, jnp.float32
+    tok_rows, width = tokens.shape
+    half_g, half_a = g_grad.shape[-1], 2 * width
+    pairs = heads // 2
+    d_rows = d_grad.shape[2]
+    bufs = []
+    shapes = ((d_rows, width), (rows_chip, half_g // 2), (rows_chip, half_g // 2), (rows_chip, half_a))
+    for i, (rows, half) in enumerate(shapes):
+        counts = (16, 16, 2, 2, 4, 4, 3)[i == 3 :]
+        bufs += [pltpu.VMEM((count, rows, half), low) for count in counts]
+    vmem, hbm = pl.BlockSpec(memory_space=pltpu.VMEM), pl.BlockSpec(memory_space=pl.ANY)
+    keys = k.shape[0]
+    dma = lambda *shape: pltpu.SemaphoreType.DMA(shape)
+    return pl.pallas_call(
+        lambda *refs: back_kernel(heads, *refs),
+        out_shape=(
+            jax.ShapeDtypeStruct((tok_rows, width), low),
+            jax.ShapeDtypeStruct((24, 3 * width), wide),
+            jax.ShapeDtypeStruct((24, width), wide),
+            jax.ShapeDtypeStruct((24, 2 * half_g), wide),
+            jax.ShapeDtypeStruct((d_rows, width), wide),
+            jax.ShapeDtypeStruct(small.shape, wide),
+        ),
+        in_specs=[vmem, hbm, hbm, hbm, hbm, vmem] + [hbm] * 7 + [vmem],
+        out_specs=(vmem,) * 6,
+        scratch_shapes=bufs
+        + [
+            pltpu.VMEM((2, 16, rows_chip, half_a), low),
+            pltpu.VMEM((tok_rows, width), low),
+            pltpu.VMEM((pairs, 2, tok_rows, lane_width), wide),
+            pltpu.VMEM((pairs, 2, tok_rows, lane_width), low),
+            pltpu.VMEM((pairs, 2, tok_rows, lane_width), low),
+            pltpu.VMEM((2, rows_chip, half_g // 2), wide),
+            pltpu.VMEM((rows_chip, half_a), wide),
+            pltpu.VMEM((2, 24, half_g // 2), wide),
+            pltpu.VMEM((24, half_a), wide),
+            pltpu.VMEM((10,) + small.shape, wide),
+            dma(4 * scatter_slots),
+            dma(4 * scatter_slots),
+            dma(4 * scatter_slots),
+            dma(2, pairs),
+            dma(2, 9),
+            dma(6),
+        ],
+        compiler_params=pltpu.CompilerParams(
+            collective_id=1, has_side_effects=True, vmem_limit_bytes=62 * 2**20
+        ),
+        cost_estimate=pl.CostEstimate(
+            flops=10 * tok_rows * keys * width, bytes_accessed=40 * width * width, transcendentals=heads * tok_rows * keys
+        ),
+        name="attention_back_and_sums",
+    )(tokens, q, k, v, span, lse, att, d_att, d_resid_one, grad_out, a_full, g_grad, d_grad, small)
 
 
 def window(cells, width):
@@ -782,20 +930,29 @@
     return a_full.reshape(2, width, -1), g_full.reshape(2, width, ff), d_full.reshape(-1, width)
 
 
-def summed_grads(a_grad, g_grad, d_grad, small):
+def back_and_sums(heads, tokens, q, k, v, span, lse, att, d_att, d_resid_one, grad_out, a_full, g_grad, d_grad, small):
     both = ("rows", "blk")
-    width = d_grad.shape[1]
-    if not on_chip_grid():
-        share = lambda g, axis: lax.psum_scatter(g.astype(jnp.float32), both, scatter_dimension=axis, tiled=True)
-        left, right = share(a_grad, 1)
-        gate, up = share(g_grad, 1)
-        cut = right.shape[1] - width
-        return (
-            jnp.concatenate([left, right[:, :cut]], 1), right[:, cut:],
-            jnp.concatenate([gate, up], 1), share(d_grad, 0), lax.psum(small, both),
+    tok_rows, width = tokens.shape
+    if on_chip_grid():
+        split = lambda g: g.reshape(2, 16, rows_chip, g.shape[2])
+        return back(
+            heads, tokens, q, k, v, span, lse, att, d_att, d_resid_one, grad_out.reshape(16, rows_chip, width),
+            a_full, split(g_grad), d_grad.reshape(16, 2, -1, width), small,
         )
-    split = lambda g: g.reshape(2, 16, rows_chip, g.shape[2])
-    return scatter_grads(split(a_grad), split(g_grad), d_grad.reshape(16, 2, -1, width), small)
+    low = jnp.bfloat16
+    dq, dk, dv = attend_back(q, k, v, span, lse, att, d_att, heads)
+    dkv = window_back(jnp.concatenate([dk, dv], 1), tok_rows)
+    d_qk = jnp.concatenate([dq, dkv[:, :width].astype(low)], 1)
+    d_v = dkv[:, width:].astype(low)
+    grad_qkv = transposed_times(tokens, jnp.concatenate([d_qk, d_v], 1))
+    d_tokens = d_resid_one + times_transposed(d_qk, a_full[0, :, : 2 * width])
+    d_tokens = d_tokens + times_transposed(d_v, a_full[1, :, :width])
+    share = lambda g, axis: lax.psum_scatter(g.astype(jnp.float32), both, scatter_dimension=axis, tiled=True)
+    gate, up = share(g_grad, 1)
+    return (
+        d_tokens.astype(low), share(grad_qkv, 0), share(grad_out, 0), jnp.concatenate([gate, up], 1),
+        share(d_grad, 0), lax.psum(small, both),
+    )
 
 
 def body(
@@ -822,21 +979,15 @@
     output, d_resid_one, d_att, grad_out, g_grad, d_grad, small = ffn(
         inputs, attended, a_full, vectors, valid, out_grad[0], w_gu, w_dn
     )
-    dq, dk, dv = attend_back(query, keys, values, span, lse, attended, d_att, HEADS)
-    dkv = window_back(jnp.concatenate([dk, dv], 1), tok_rows)
-    d_qk = jnp.concatenate([dq, dkv[:, :width].astype(low)], 1)
-    d_v = dkv[:, width:].astype(low)
-    grad_qk = transposed_times(inputs, d_qk).astype(low)
-    grad_v = transposed_times(inputs, d_v).astype(low)
-    d_tokens = d_resid_one + times_transposed(d_qk, w_qk) + times_transposed(d_v, w_v)
-    a_grad = jnp.stack([grad_qk, jnp.concatenate([grad_v, grad_out], 1)])
-    *parts, small = summed_grads(a_grad, g_grad, d_grad, small)
+    d_tokens, *parts, small = back_and_sums(
+        HEADS, inputs, query, keys, values, span, lse, attended, d_att, d_resid_one, grad_out, a_full, g_grad, d_grad, small
+    )
     share = width // lax.axis_size(both)
     mine = lax.axis_index(both) * share
     rows = lax.dynamic_slice_in_dim(small[:4], mine, share, 1)
     stats = jnp.sqrt(jnp.sum(small[4:8], 1) / (small[8, 0] * width))
     return (
-        output[None], d_tokens.astype(low)[None], parts[0], parts[1], rows[0], rows[1],
+        output[None], d_tokens[None], parts[0], parts[1], rows[0], rows[1],
         parts[2], parts[3], rows[2], rows[3], stats,
     )
 

time: 338 us -> 276 us (0.82)
  Pallas kernels: 282 us -> 242 us
  matrix products: 12.3 us -> 2.16 us
  other arithmetic: 17.6 us -> 9.22 us
    pallas_call x2 -> x1, Pallas kernels: 127 us -> 92.8 us  [back(): pl.pallas_call(lambda *refs: back_kernel(heads, *refs), out_shape=(jax.Sh...]
    dot_general x4 -> x0, matrix products: 10.1 us -> none  [the longest x2 7.82 us: times_transposed(): lax.dot_general(left, right, (((1,), (1,)), ((), ())), preferred_element_...]
    another operation x2 -> x0, other arithmetic: 6.31 us -> none
    pallas_call x1, Pallas kernels: 94.1 us -> 89.4 us  [gather_weights(): pl.pallas_call(gather_kernel, out_shape=(jax.ShapeDtypeStruct((2, 16, row...]
    unnamed x38 -> x23, local copies, waits for them, and re-layouts: 12.3 us -> 11 us
  transfers between devices with their start and end apart: 2 -> 1, of which waited for: 1 -> 0; matrix products, arithmetic and copies ran while one was open for 1% -> 2% of each run, Pallas kernels for 0% -> 0%
where the time goes in v3:
time: 276 us; the launch traced here: 275 us
  Pallas kernels  242 us (88%)
  local copies, waits for them, and re-layouts  19.3 us (7%)
  other arithmetic  9.22 us (3%)
    pallas_call x1, Pallas kernels, back(): pl.pallas_call(lambda *refs: back_kernel(heads, *refs), out_shape=(jax.Sh...  92.8 us
    pallas_call x1, Pallas kernels, gather_weights(): pl.pallas_call(gather_kernel, out_shape=(jax.ShapeDtypeStruct((2, 16, row...  89.4 us
    pallas_call x1, Pallas kernels, ffn(): pl.pallas_call(ffn_kernel, grid=(2 * tiles,), out_shape=(jax.ShapeDtypeSt...  37.5 us
    pallas_call x1, Pallas kernels, attend(): pl.pallas_call(lambda *refs: attend_kernel(heads, *refs), out_shape=(jax....  22.5 us
    unnamed x23, local copies, waits for them, and re-layouts  11 us
  transfers between devices with their start and end apart: 1, of which 0 were waited for; matrix products, arithmetic and copies ran while one was open for 2% of the time, Pallas kernels for 0%

profile of v3, /device:TPU:0, one launch (start us, length us, event | category | flops | bytes accessed | tf_op | source)
XLA Modules:
  0.0 274.9 jit_solution(14251970400827554716)
XLA Ops:
  0.6 0.0 copy-start.1
  0.7 0.0 copy-start.4
  0.7 0.9 slice.55
  1.5 0.9 slice.54
  2.4 0.7 pad_maximum_fusion.2
  3.1 0.1 copy.42
  3.2 1.0 slice_bitcast_fusion.6
  4.3 0.8 fusion.13
  5.1 0.0 copy-done.1
  5.1 89.4 %gather_weights.1 = (bf16[2,16,48,1664]{3,2,1,0:T(8,128)(2,1)S(1)}, bf16[2,16,48,3072]{3,2,1,0:T(8,128)(2,1)S(1)}, bf16[16,2,96,768]{3,2,1,0:T(8,128)(2,1)S(1)}) custom-call(bf16[2,32,1664]{2,1,0:T(8,128)(2,1)S(1)} %fusion.10.a_shard, bf16[2,32,3072]{2,1,0:T(8,128)(2,1)S(1)} %fusion.9.g_shard, bf16[96,768]{1,0:T(8,128)(2,1)S(1)} %copy-done.1), custom_call_target="tpu_custom_call" | custom-call | tf_op jit(solution)/shard_map/gather_weights/pallas_call | solution.py:314
  94.5 0.0 copy-start.2
  94.5 3.7 %copy-done.2 = bf16[2,16,48,3072]{3,2,1,0:T(8,128)(2,1)} copy-done((bf16[2,16,48,3072]{3,2,1,0:T(8,128)(2,1)}, bf16[2,16,48,3072]{3,2,1,0:T(8,128)(2,1)S(1)}, u32[]{:S(2)}) %copy-start.2) | copy-done | bytes 9437208
  98.2 0.0 copy-start
  98.2 0.0 copy-done.4
  98.2 0.8 fusion.4
  99.0 1.4 fusion
  100.4 0.1 copy-done
  100.5 1.4 copy-done.3
  101.8 1.0 fusion.17
  102.8 0.1 pad_maximum_fusion.1
  102.9 0.6 collective-permute-start
  103.6 0.0 copy-done.8
  103.6 0.9 copy.46.valid
  104.4 0.9 slice_bitcast_fusion.4
  105.4 0.7 copy.45.vectors
  106.2 2.2 convert_select_fusion.refs_3_.refs_4_
  108.3 0.0 collective-permute-done
  108.3 2.0 broadcast_select_fusion
  110.3 1.9 pad_maximum_fusion
  112.2 22.5 %attend.1 = (bf16[512,768]{1,0:T(8,128)(2,1)}, f32[16,512]{1,0:T(8,128)}) custom-call(bf16[512,768]{1,0:T(8,128)(2,1)} %get-tuple-element.54.refs_0_.refs_1_, bf16[1024,768]{1,0:T(8,128)(2,1)} %get-tuple-element.50.refs_1_.refs_2_, bf16[1024,768]{1,0:T(8,128)(2,1)} %get-tuple-element.49.refs_2_.refs_3_, f32[1024,512]{1,0:T(8,128)} %convert_select_fusion.refs_3_.refs_4_), custom_call_target="tpu_custom_call" | custom-call | flops 1610612736 | bytes 6291456 | tf_op jit(solution)/shard_map/attend/pallas_call | solution.py:549
  134.8 37.5 %feed_forward.1 = (bf16[512,768]{1,0:T(8,128)(2,1)}, f32[512,768]{1,0:T(8,128)}, bf16[512,768]{1,0:T(8,128)(2,1)}, bf16[768,768]{1,0:T(8,128)(2,1)}, bf16[2,768,...) custom-call(bf16[512,768]{1,0:T(8,128)(2,1)} %bitcast.64, ...), custom_call_target="tpu_custom_call" | custom-call | flops 23555211264 | bytes 42467328 | tf_op jit(solution)/shard_map/feed_forward/pallas_call | solution.py:456
  172.2 92.8 %attention_back_and_sums.1 = (bf16[512,768]{1,0:T(8,128)(2,1)}, f32[24,2304]{1,0:T(8,128)}, f32[24,768]{1,0:T(8,128)}, f32[24,6144]{1,0:T(8,128)}, f32[96,768]{1,0:T(8,128)}, /*index=5*/f32[16,768]{1,0:T(8,128)}) custom-call(bf16[512,768]{1,0:T(8,128)(2,1)} %bitcast.65, bf16[512,768]{1,0:T(8,128)(2,1)} %get-tuple-element.54.refs_0_.refs_1_, ...), custom_call_target="tpu_custom_call" | custom-call | flops 4026531840 | bytes 23592960 | tf_op jit(solution)/shard_map/attention_back_and_sums/pallas_call | solution.py:828
  265.0 0.0 copy-start.7
  265.0 0.0 copy-start.5
  265.0 0.0 copy-start.6
  265.0 1.3 slice.71
  266.3 0.9 slice_reduce_fusion
  267.2 0.1 constant_dynamic-slice_fusion
  267.3 0.5 slice_bitcast_fusion.7
  268.5 0.5 divide_sqrt_fusion
  269.0 2.1 copy.54
  271.1 1.6 copy.55
  272.7 0.0 copy-done.7
  272.7 0.6 copy.56
  273.4 0.0 copy-done.5
  273.4 0.8 copy.57
  274.2 0.0 copy-done.6
  274.2 0.7 copy.58
  (10 shorter events, 0.1 us)
Async XLA Ops:
  0.6 4.5 %copy-start.1 = (bf16[96,768]{1,0:T(8,128)(2,1)S(1)}, bf16[96,768]{1,0:T(8,128)(2,1)}, u32[]{:S(2)}) copy-start(bf16[96,768]{1,0:T(8,128)(2,1)} %d_own.1) | copy-start | bytes 442372
  0.7 97.5 %copy-start.4 = (bf16[1,512,768]{2,1,0:T(8,128)(2,1)S(1)}, bf16[1,512,768]{2,1,0:T(8,128)(2,1)}, u32[]{:S(2)}) copy-start(bf16[1,512,768]{2,1,0:T(8,128)(2,1)} %param.11) | copy-start | bytes 2359300
  94.5 3.7 %copy-start.2 = (bf16[2,16,48,3072]{3,2,1,0:T(8,128)(2,1)}, bf16[2,16,48,3072]{3,2,1,0:T(8,128)(2,1)S(1)}, u32[]{:S(2)}) copy-start(bf16[2,16,48,3072]{3,2,1,0:T(8,128)(2,1)S(1)} %get-tuple-element.31) | copy-start | bytes 28311556
  98.2 2.3 copy-start
  98.2 3.6 %copy-start.3 = (bf16[16,2,96,768]{3,2,1,0:T(8,128)(2,1)}, bf16[16,2,96,768]{3,2,1,0:T(8,128)(2,1)S(1)}, u32[]{:S(2)}) copy-start(bf16[16,2,96,768]{3,2,1,0:T(8,128)(2,1)S(1)} %get-tuple-element.32) | copy-start | bytes 14155780
  102.8 0.8 copy-start.8
  102.9 5.4 %collective-permute-start = (bf16[512,1536]{1,0:T(8,128)(2,1)S(1)}, bf16[512,1536]{1,0:T(8,128)(2,1)}, u32[]{:S(2)}, u32[]{:S(2)}) collective-permute-start(bf16[512,1536]{1,0:T(8,128)(2,1)S(1)} %pad_maximum_fusion.1), channel_id=1, source_target_pairs={{0,1},{1,0},{2,3},{3,2},{4,5},{5,4},{6,7},{7,6},{8,9},{9,8},{10,11... | collective-permute-start | bytes 4718600 | tf_op jit(solution)/shard_map/ppermute | solution.py:872
  265.0 7.7 %copy-start.7 = (f32[24,768]{1,0:T(8,128)S(1)}, f32[24,768]{1,0:T(8,128)}, u32[]{:S(2)}) copy-start(f32[24,768]{1,0:T(8,128)} %get-tuple-element.79) | copy-start | bytes 221188
  265.0 8.3 %copy-start.5 = (f32[24,6144]{1,0:T(8,128)S(1)}, f32[24,6144]{1,0:T(8,128)}, u32[]{:S(2)}) copy-start(f32[24,6144]{1,0:T(8,128)} %get-tuple-element.82) | copy-start | bytes 1769476
  265.0 9.1 %copy-start.6 = (f32[96,768]{1,0:T(8,128)S(1)}, f32[96,768]{1,0:T(8,128)}, u32[]{:S(2)}) copy-start(f32[96,768]{1,0:T(8,128)} %get-tuple-element.83) | copy-start | bytes 884740

commit v4 on v3

--- a/solution.py
+++ b/solution.py
@@ -82,8 +82,8 @@
 
 
 class Gather:
-    def __init__(self, place, copies, base, own, out):
-        self.p, self.cp, self.base, self.own, self.out = place, copies, base, own, out
+    def __init__(self, place, copies, base, out):
+        self.p, self.cp, self.base, self.out = place, copies, base, out
 
     def slot(self, kind, k, j="o"):
         start = {"z": -1, "x": 3, "y": 7, "d": 11, "s": 15}[kind]
@@ -93,14 +93,14 @@
         return self.out(self.p.c, self.p.at(k, j))
 
     def send(self, src, dst, slot, peer):
-        self.cp.put(src, dst, slot, peer, lambda: self.own)
+        self.cp.put(src, dst, slot, peer, lambda: self.out(0, 0))
 
     def push(self, src, k, j):
         self.send(src, self.block(k, j), self.slot("s", k, j), self.p.sib)
 
     def to_z(self, k):
         if k:
-            self.send(self.own, self.block(0, "o"), self.slot("z", k), self.p.zn[k])
+            self.send(self.block(0, "o"), self.block(0, "o"), self.slot("z", k), self.p.zn[k])
 
     def spread(self, src, k):
         dst = self.block(k, "o")
@@ -110,7 +110,7 @@
 
     def from_z(self, k):
         if k == 0:
-            self.spread(self.own, 0)
+            self.spread(self.block(0, "o"), 0)
             return
         block = self.block(k, "o")
         self.cp.got(block, self.slot("z", k), self.p.zn[k])
@@ -150,8 +150,8 @@
 
 
 class Scatter:
-    def __init__(self, place, copies, base, give, own, sib, rly, dia, xin, yin, zin, load=None):
-        self.p, self.cp, self.base, self.give, self.own, self.load = place, copies, base, give, own, load
+    def __init__(self, place, copies, gives, base, give, own, sib, rly, dia, xin, yin, zin):
+        self.p, self.cp, self.gives, self.base, self.give, self.own = place, copies, gives, base, give, own
         self.sib, self.rly, self.dia, self.xin, self.yin, self.zin = sib, rly, dia, xin, yin, zin
 
     def slot(self, kind, k):
@@ -162,9 +162,7 @@
 
     def begin(self, k):
         four = self.four(k)
-        self.cp.put(self.give(four), self.sib.at[four], self.slot("s", k), self.p.sib, lambda: self.sib.at[pl.ds(0, 4)])
-        if self.load is not None:
-            self.load(four, self.base + k).start()
+        self.gives.put(self.give(four), self.sib.at[four], self.slot("s", k), self.p.sib, lambda: self.sib.at[pl.ds(0, 4)])
 
     def to_x(self, own, k):
         self.cp.put(own, self.xin.at[k], self.slot("x", k), self.p.xn, lambda: self.xin.at[k])
@@ -183,8 +181,6 @@
 
     def pair(self, k):
         four = self.four(k)
-        if self.load is not None:
-            self.load(four, self.base + k).wait()
         self.cp.got(self.sib.at[four], self.slot("s", k), self.p.sib)
         if k % 2:
             i = k // 2
@@ -254,87 +250,12 @@
 
 
 gather_stages = (("to_z", -2), ("from_z", 0), ("from_xy", 1), ("from_even", 2), ("from_odd", 3))
-scatter_stages = (("begin", -2), ("pair", 0), ("diag", 1), ("relay", 2), ("plane", 3))
+scatter_stages = (("pair", 0), ("diag", 1), ("relay", 2), ("plane", 3))
 near_far, far_near = ((0, 1), (2, 3)), ((3, 2), (1, 0))
 
 
 rows_chip = 48
 gather_slots, scatter_slots = 31, 19
-
-
-def gather_kernel(a_shard, g_shard, d_own, a_full, g_full, d_full, a_pair, g_pair, a_own, g_own, pair_sem, send, recv, local):
-    place = Place()
-    place.greet()
-    c = place.c
-    pairs = Copies(pair_sem.at[0], pair_sem.at[1])
-    for i, (shard, other) in enumerate(((a_shard, a_pair), (g_shard, g_pair))):
-        pairs.put(shard.at[1 - c], other, i, place.sib)
-    copies = Copies(send, recv)
-    half_g = g_full.shape[3] // 2
-    outs = [
-        lambda half, r: a_full.at[half, r],
-        lambda half, r: g_full.at[half, r, :, :half_g],
-        lambda half, r: g_full.at[half, r, :, half_g:],
-        lambda half, r: d_full.at[r, half],
-    ]
-    owns = [a_own, g_own.at[:, :half_g], g_own.at[:, half_g:], d_own]
-    mats = [Gather(place, copies, i * gather_slots, own, out) for i, (own, out) in enumerate(zip(owns, outs))]
-
-    def assemble(shard, other, own, i):
-        pairs.got(other, i, place.sib)
-        mine = shard[c, :24, :].astype(jnp.float32)
-        theirs = other[:24, :].astype(jnp.float32)
-        first = c == 0
-        top = jnp.where(first, mine, theirs)
-        low = jnp.where(first, theirs, mine)
-        own[...] = jnp.concatenate([top, low], 0).astype(jnp.bfloat16)
-
-    kept = [pltpu.make_async_copy(m.own, m.block(0, "o"), local.at[i]) for i, m in enumerate(mats)]
-    assemble(a_shard, a_pair, a_own, 0)
-    steps = Steps([(m, planes) for m in mats for planes in near_far], gather_stages)
-    steps(-2)
-    steps(-1)
-    kept[0].start()
-    assemble(g_shard, g_pair, g_own, 1)
-    for copy in kept[1:]:
-        copy.start()
-    for t in range(steps.count()):
-        steps(t)
-    for m in mats:
-        m.from_sib()
-    for copy in kept:
-        copy.wait()
-    pairs.drain(place.sib)
-    copies.drain(place.sib)
-
-
-def gather_weights(a_shard, g_shard, d_shard):
-    half_a, half_g = a_shard.shape[-1], g_shard.shape[-1]
-    low = jnp.bfloat16
-    return pl.pallas_call(
-        gather_kernel,
-        out_shape=(
-            jax.ShapeDtypeStruct((2, 16, rows_chip, half_a), low),
-            jax.ShapeDtypeStruct((2, 16, rows_chip, half_g), low),
-            jax.ShapeDtypeStruct((16, 2) + d_shard.shape, low),
-        ),
-        in_specs=[pl.BlockSpec(memory_space=pltpu.VMEM)] * 3,
-        out_specs=(pl.BlockSpec(memory_space=pl.ANY),) * 3,
-        scratch_shapes=[
-            pltpu.VMEM(a_shard.shape[1:], low),
-            pltpu.VMEM(g_shard.shape[1:], low),
-            pltpu.VMEM((rows_chip, half_a), low),
-            pltpu.VMEM((rows_chip, half_g), low),
-            pltpu.SemaphoreType.DMA((2, 2)),
-            pltpu.SemaphoreType.DMA((4 * gather_slots,)),
-            pltpu.SemaphoreType.DMA((4 * gather_slots,)),
-            pltpu.SemaphoreType.DMA((4,)),
-        ],
-        compiler_params=pltpu.CompilerParams(
-            collective_id=0, has_side_effects=True, vmem_limit_bytes=32 * 2**20
-        ),
-        name="gather_weights",
-    )(a_shard, g_shard, d_shard)
 
 
 def dot(left, right, dims=((1,), (0,))):
@@ -512,34 +433,10 @@
     return jnp.where(keep, block, jnp.zeros_like(block))
 
 
-def attend_kernel(heads, q, k, v, span, attended, lse, out_t, q_t, v_t):
-    low = jnp.bfloat16
-    rows, width = q.shape
-    lanes = lane_width
-    depth = width // heads
-    chunk = 256
-
-    q_t[...] = (q[...].astype(jnp.float32) * depth**-0.5).T.astype(low)
-    v_t[...] = v[...].astype(jnp.float32).T.astype(low)
-
+def attend_kernel(heads, q, k, v, span, attended, lse):
     @pl.loop(0, heads // 2)
     def _(pair):
-        at = pl.ds(pl.multiple_of(pair * lanes, lanes), lanes)
-        keys = k[:, at]
-        for h in (0, 1):
-            slope = jnp.exp2(jnp.full((1, 1), -8.0 / heads, jnp.float32) * (2 * pair + h + 1).astype(jnp.float32))
-            values_t = v_t[pl.ds(pl.multiple_of(pair * lanes + h * depth, depth), depth), :]
-            for c in range(rows // chunk):
-                here = pl.ds(c * chunk, chunk)
-                logits = dot(keys, half_of(q_t[at, here], 0, h)) - slope * span[:, here]
-                top = jnp.max(logits, 0, keepdims=True)
-                weights = jnp.exp(logits - top)
-                norm = jnp.sum(weights, 0, keepdims=True)
-                lse[pl.ds(2 * pair + h, 1), here] = top + jnp.log(norm)
-                mixed = dot(values_t, weights.astype(low))
-                out_t[pl.ds(pl.multiple_of(pair * lanes + h * depth, depth), depth), here] = mixed / norm
-
-    attended[...] = out_t[...].T.astype(low)
+        attend_pair(pair, heads, q, k, v, span, lse, attended)
 
 
 def attend(q, k, v, span, heads):
@@ -554,11 +451,6 @@
         ),
         in_specs=[pl.BlockSpec(memory_space=pltpu.VMEM)] * 4,
         out_specs=(pl.BlockSpec(memory_space=pltpu.VMEM),) * 2,
-        scratch_shapes=[
-            pltpu.VMEM((width, rows), wide),
-            pltpu.VMEM((width, rows), low),
-            pltpu.VMEM((width, keys), low),
-        ],
         compiler_params=pltpu.CompilerParams(vmem_limit_bytes=60 * 2**20),
         cost_estimate=pl.CostEstimate(flops=4 * rows * keys * width, bytes_accessed=8 * keys * width, transcendentals=heads * rows * keys),
         name="attend",
@@ -577,7 +469,7 @@
     keys_t = keys.astype(wide).T.astype(low)
     for c in range(rows // chunk):
         here = pl.ds(c * chunk, chunk)
-        q_wide = q[here, at].astype(wide) * scale
+        q_wide = q[here, at].astype(wide)
         do_here = d_att[here, at]
         do_wide = do_here.astype(wide)
         q_here = q_wide.astype(low)
@@ -639,35 +531,268 @@
     )(q, k, v, span, lse, att, d_att)
 
 
-def back_kernel(
-    heads, tokens, q, k, v, span, lse, att, d_att, d_resid_one, grad_out, a_full, g_grad, d_grad, small,
-    d_tokens, qkv_out, wout_out, gu_out, down_out, small_out, *scratch,
+def attend_pair(pair, heads, q, k, v, span, lse, attended):
+    low, wide = jnp.bfloat16, jnp.float32
+    rows, width = q.shape
+    lanes = lane_width
+    depth = width // heads
+    chunk = 256
+    at = pl.ds(pl.multiple_of(pair * lanes, lanes), lanes)
+    keys = k[:, at]
+    values_t = v[:, at].astype(wide).T.astype(low)
+    for c in range(rows // chunk):
+        here = pl.ds(c * chunk, chunk)
+        q_t = q[here, at].astype(wide).T.astype(low)
+        parts = []
+        for h in (0, 1):
+            head = 2 * pair + h
+            slope = jnp.exp2(jnp.full((1, 1), -8.0 / heads, wide) * (head + 1).astype(wide))
+            logits = dot(keys, half_of(q_t, 0, h)) - slope * span[:, here]
+            top = jnp.max(logits, 0, keepdims=True)
+            weights = jnp.exp(logits - top)
+            norm = jnp.sum(weights, 0, keepdims=True)
+            lse[pl.ds(head, 1), here] = top + jnp.log(norm)
+            parts.append(dot(values_t[h * depth : (h + 1) * depth], weights.astype(low)) / norm)
+        attended[here, at] = jnp.concatenate(parts, 0).T.astype(low)
+
+
+def fore_kernel(
+    heads, tokens, a_shard, g_shard, d_shard, valid, span, out_grad,
+    a_full, g_full, d_full, q_out, k_out, v_out, att_out, hid_t_out, norm_out, inv_out, gate_out, up_out, act_out,
+    output_out, d_hid_out, d_branch_out, lse, vectors, small,
+    w_a, w_g, w_d, a_pair, g_pair, q, k, v, att, span_v, grad_v, hid, hid_low, hid_t, norm_one, inv_one,
+    slope_gate, slope_up, act, output, d_hid, d_branch, pair_sem, send, recv, in_sem, out_sem,
 ):
     place = Place()
     place.greet()
     c = place.c
     low, wide = jnp.bfloat16, jnp.float32
     tok_rows, width = tokens.shape
+    ff = w_g.shape[3]
+    half_g = ff // 2
+    pairs = heads // 2
+    loads = [pltpu.make_async_copy(src, dst, in_sem.at[i]) for i, (src, dst) in enumerate(((span, span_v), (out_grad, grad_v)))]
+    for copy in loads:
+        copy.start()
+    swaps = Copies(pair_sem.at[0], pair_sem.at[1])
+    for i, (shard, other) in enumerate(((a_shard, a_pair), (g_shard, g_pair))):
+        swaps.put(shard.at[1 - c], other, i, place.sib)
+    copies = Copies(send, recv)
+    outs = [
+        lambda half, r: w_a.at[half, r],
+        lambda half, r: w_g.at[half, r, :, :half_g],
+        lambda half, r: w_g.at[half, r, :, half_g:],
+        lambda half, r: w_d.at[r, half],
+    ]
+    mats = [Gather(place, copies, i * gather_slots, out) for i, out in enumerate(outs)]
+    steps = Steps([(m, planes) for m in mats for planes in near_far], gather_stages)
+    me = place.at(0, "o")
+
+    def assemble(shard, other, full, i):
+        swaps.got(other, i, place.sib)
+        mine = shard[c, :24, :].astype(wide)
+        theirs = other[:24, :].astype(wide)
+        first = c == 0
+        top = jnp.where(first, mine, theirs)
+        rest = jnp.where(first, theirs, mine)
+        full[c, me] = jnp.concatenate([top, rest], 0).astype(low)
+
+    assemble(a_shard, a_pair, w_a, 0)
+    steps(-2)
+    steps(-1)
+    assemble(g_shard, g_pair, w_g, 1)
+    w_d[me, c] = d_shard[...]
+    for t in range(5):
+        steps(t)
+    mats[0].from_sib()
+    saved = []
+
+    def save(src, dst):
+        copy = pltpu.make_async_copy(src, dst, out_sem.at[len(saved)])
+        copy.start()
+        saved.append((src, dst))
+
+    save(w_a, a_full)
+    part = lambda half, at, size: w_a[half, :, :, at : at + size].reshape(width, size)
+    vectors[...] = part(0, 2 * width, lane_width).astype(wide).T[:8]
+    x = tokens[...]
+    half = pl.ds(pl.multiple_of(c * tok_rows, tok_rows), tok_rows)
+    k[half, :] = dot(x, part(0, width, width)).astype(low)
+    swaps.put(k.at[half], k.at[half], 2, place.sib, lambda: k.at[pl.ds(0, tok_rows)])
+    v[half, :] = dot(x, part(1, 0, width)).astype(low)
+    swaps.put(v.at[half], v.at[half], 3, place.sib, lambda: v.at[pl.ds(0, tok_rows)])
+    depth = width // heads
+    q[...] = dot(x, part(0, 0, width)).astype(low) * depth**-0.5
+    steps(5)
+    other = pl.ds(pl.multiple_of((1 - c) * tok_rows, tok_rows), tok_rows)
+    swaps.got(k.at[other], 2, place.sib)
+    swaps.got(v.at[other], 3, place.sib)
+    save(q, q_out)
+    save(k, k_out)
+    save(v, v_out)
+    loads[0].wait()
+
+    @pl.loop(0, pairs)
+    def _(pair):
+        attend_pair(pair, heads, q, k, v, span_v, lse, att)
+        for i in range(3):
+
+            @pl.when(pair == 2 * i + 1)
+            def _(i=i):
+                steps(6 + i)
+
+    save(att, att_out)
+    branch = dot(att[...], part(1, width, width))
+    toks = x.astype(wide)
+    norm, inverse = normalized(toks + branch)
+    norm_one[...] = norm
+    inv_one[...] = jnp.broadcast_to(inverse, inv_one.shape)
+    hidden = norm * vectors[0:1, :] + vectors[1:2, :]
+    hid[...] = hidden
+    hid_low[...] = hidden.astype(low)
+    hid_t[...] = hidden.T.astype(low)
+    save(hid_t, hid_t_out)
+    save(norm_one, norm_out)
+    save(inv_one, inv_out)
+    mask = valid[...]
+    small[0:4, :] = jnp.zeros((4, width), wide)
+    small[4:5, :] = column_sum(mask * toks * toks)
+    small[5:6, :] = column_sum(mask * branch * branch)
+    small[6:7, :] = column_sum(mask * hidden * hidden)
+    small[8:16, :] = jnp.zeros((8, width), wide)
+    small[8:9, :] = jnp.broadcast_to(jnp.sum(mask, 0, keepdims=True), (1, width))
+    tile = 512
+
+    def glu(j):
+        cols = pl.ds(pl.multiple_of(j * tile, tile), tile)
+        h = hid_low[...]
+        gate = dot(h, w_g[0, :, :, cols].reshape(width, tile))
+        up = dot(h, w_g[1, :, :, cols].reshape(width, tile))
+        cdf = 0.5 + 0.5 * lax.erf(gate * 0.7071067811865476)
+        mixed = gate * cdf
+        density = 0.3989422804014327 * jnp.exp(-0.5 * gate * gate)
+        slope_up[:, cols] = mixed.astype(low)
+        slope_gate[:, cols] = (up * (cdf + gate * density)).astype(low)
+        act[:, cols] = (mixed * up).astype(low)
+
+    mats[1].from_sib()
+
+    @pl.loop(0, half_g // tile)
+    def _(j):
+        glu(j)
+
+    steps(9)
+    mats[2].from_sib()
+    save(w_g, g_full)
+
+    @pl.loop(half_g // tile, ff // tile)
+    def _(j):
+        glu(j)
+
+    save(slope_gate, gate_out)
+    save(slope_up, up_out)
+    save(act, act_out)
+    steps(10)
+    mats[3].from_sib()
+    save(w_d, d_full)
+    d_hid[...] = jnp.zeros_like(d_hid)
+    chips = 4
+    deep = 2 * chips * w_d.shape[2]
+
+    @pl.loop(0, 16 // chips)
+    def _(j):
+        cols = pl.ds(pl.multiple_of(j * deep, deep), deep)
+        d_hid[...] += dot(act[:, cols], w_d[pl.ds(j * chips, chips)].reshape(deep, width))
+
+    branch = d_hid[...]
+    small[7:8, :] = column_sum(mask * branch * branch)
+    norm, inverse = normalized(hid[...] + branch)
+    gain = vectors[2:3, :]
+    output[...] = (norm * gain + vectors[3:4, :]).astype(low)
+    save(output, output_out)
+    loads[1].wait()
+    grad = grad_v[...].astype(wide)
+    small[2:3, :] = column_sum(grad * norm)
+    small[3:4, :] = column_sum(grad)
+    back = norm_back(grad, gain, norm, inverse)
+    d_hid[...] = back
+    d_branch[...] = back.astype(low)
+    save(d_hid, d_hid_out)
+    save(d_branch, d_branch_out)
+    for i, (src, dst) in enumerate(saved):
+        pltpu.make_async_copy(src, dst, out_sem.at[i]).wait()
+    swaps.drain(place.sib)
+    copies.drain(place.sib)
+
+
+def fore(heads, tokens, a_shard, g_shard, d_shard, valid, span, out_grad):
+    low, wide = jnp.bfloat16, jnp.float32
+    rows, width = tokens.shape
+    half_a, ff = a_shard.shape[-1], g_shard.shape[-1]
+    keys = span.shape[0]
+    vmem, hbm = pl.BlockSpec(memory_space=pltpu.VMEM), pl.BlockSpec(memory_space=pl.ANY)
+    dma = lambda *shape: pltpu.SemaphoreType.DMA(shape)
+    shape = jax.ShapeDtypeStruct
+    w_a, w_g, w_d = (2, 16, rows_chip, half_a), (2, 16, rows_chip, ff), (16, 2) + d_shard.shape
+    stored = [
+        (w_a, low), (w_g, low), (w_d, low), ((rows, width), low), ((keys, width), low), ((keys, width), low),
+        ((rows, width), low), ((width, rows), low), ((rows, width), wide), ((rows, lane_width), wide),
+        ((rows, ff), low), ((rows, ff), low), ((rows, ff), low), ((rows, width), low), ((rows, width), wide),
+        ((rows, width), low),
+    ]
+    block = lambda *dims: pltpu.VMEM(dims, low)
+    block_wide = lambda *dims: pltpu.VMEM(dims, wide)
+    return pl.pallas_call(
+        lambda *refs: fore_kernel(heads, *refs),
+        out_shape=tuple(shape(dims, kind) for dims, kind in stored)
+        + (shape((16, rows), wide), shape((8, width), wide), shape((16, width), wide)),
+        in_specs=[vmem] * 5 + [hbm] * 2,
+        out_specs=(hbm,) * len(stored) + (vmem,) * 3,
+        scratch_shapes=[
+            block(*w_a), block(*w_g), block(*w_d), block(*a_shard.shape[1:]), block(*g_shard.shape[1:]),
+            block(rows, width), block(keys, width), block(keys, width), block(rows, width),
+            block_wide(keys, rows), block(rows, width), block_wide(rows, width), block(rows, width),
+            block(width, rows), block_wide(rows, width), block_wide(rows, lane_width),
+            block(rows, ff), block(rows, ff), block(rows, ff), block(rows, width), block_wide(rows, width),
+            block(rows, width), dma(2, 4), dma(4 * gather_slots), dma(4 * gather_slots), dma(2), dma(len(stored)),
+        ],
+        compiler_params=pltpu.CompilerParams(
+            collective_id=0, has_side_effects=True, vmem_limit_bytes=62 * 2**20
+        ),
+        name="gather_and_forward",
+    )(tokens, a_shard, g_shard, d_shard, valid, span, out_grad)
+
+
+def back_kernel(
+    heads, tokens, q, k, v, span, att, hid_t, norm, inv, gate, up, act, d_hid, d_branch, a_full, g_full, d_full,
+    lse, vectors, small, d_tokens, qkv_out, wout_out, gu_out, down_out, small_out, *scratch,
+):
+    place = Place()
+    place.greet()
+    c = place.c
+    first = c == 0
+    low, wide = jnp.bfloat16, jnp.float32
+    tok_rows, width = tokens.shape
+    ff = gate.shape[1]
     pairs = heads // 2
     bufs, rest = scratch[:27], scratch[27:]
-    a_grad, dq, dkv_own, dkv_out, dkv_in, g_sum, a_sum, g_fin, a_fin, small_buf, send, recv, local, pair_sem, fin_sem, in_sem = rest
+    a_grad, dkv_in, resid, d_att, g_sum, a_sum, g_fin, a_fin, small_buf, send, recv, pair_sem, fin_sem, in_sem, tile_sem = rest
     copies = Copies(send, recv)
+    gives = Copies(send, recv)
     last = Copies(fin_sem.at[0], fin_sem.at[1])
-    half_g = g_grad.shape[3] // 2
-
-    def scatter(i, source, own, sib, *more):
-        return Scatter(
-            place, copies, i * scatter_slots, lambda four: source(1 - c, four), lambda at: own.at[at], sib, *more,
-            load=lambda four, slot: pltpu.make_async_copy(source(c, four), own.at[four], local.at[slot]),
-        )
-
-    down = scatter(0, lambda half, four: d_grad.at[four, half], *bufs[:7])
-    gate = scatter(1, lambda half, four: g_grad.at[half, four, :, :half_g], *bufs[7:14])
-    rest = scatter(2, lambda half, four: g_grad.at[half, four, :, half_g:], *bufs[14:21])
+    half_g = ff // 2
+
+    def scatter(i, own, *more):
+        give = lambda four: None
+        return Scatter(place, copies, gives, i * scatter_slots, give, lambda at: own.at[at], *more)
+
+    down, left, right = (scatter(i, *bufs[7 * i : 7 * i + 7]) for i in range(3))
     proj = Scatter(
-        place, copies, 3 * scatter_slots, lambda four: a_grad.at[1 - c, four], lambda at: a_grad.at[c, at], *bufs[21:]
+        place, copies, copies, 3 * scatter_slots, lambda four: a_grad.at[1 - c, four],
+        lambda at: a_grad.at[c, at], *bufs[21:],
     )
-    chunks = Steps([(m, planes) for m in (down, gate, rest, proj) for planes in far_near], scatter_stages)
+    chunks = Steps([(m, planes) for m in (down, left, right, proj) for planes in far_near], scatter_stages)
+    planes = (3, 2, 1, 0)
     hops = ((place.sib, 0), (place.xn, 1), (place.yn, 2))
 
     def exchange(i):
@@ -683,112 +808,215 @@
         for z in (1, 2, 3):
             last.put(small_buf.at[3], small_buf.at[6 + z], 2 + z, place.zn[z], lambda z=z: small_buf.at[6 + z])
 
-    chunks(-2)
-    chunks(-1)
-    small_buf[0] = small[...]
-    exchange(0)
-
-    def steps(pair):
-        for i in range(3):
-
-            @pl.when(pair == 2 * i + 1)
-            def _(i=i):
-                chunks(i + 1)
-                combine(i)
-                if i < 2:
-                    exchange(i + 1)
-                else:
-                    spread()
+    tile = 256
+
+    def feed_forward(give_d, give_g, act_v, db, ht, w_gu, w_dn, gate_v, up_v, att_v, norm_v, inv_v, w_out):
+        down.give = lambda four: give_d.at[four]
+        left.give = right.give = lambda four: give_g.at[four]
+        load = lambda i, src, dst: pltpu.make_async_copy(src, dst, in_sem.at[i])
+        loads = [
+            load(0, d_branch, db), load(1, hid_t, ht), load(2, d_hid, resid), load(3, att, att_v),
+            load(4, norm, norm_v), load(5, inv, inv_v), load(6, a_full.at[1, :, :, width : 2 * width], w_out),
+        ]
+
+        def act_load(i, z):
+            cols = pl.ds(pl.multiple_of(place.plane(z) * width, width), width)
+            return load(7 + i % 2, act.at[:, cols], act_v.at[i % 2])
+
+        def fetch(j):
+            slot = j % 2
+            cols = pl.ds(pl.multiple_of(j * tile, tile), tile)
+            return [
+                pltpu.make_async_copy(g_full.at[:, :, :, cols], w_gu.at[slot], tile_sem.at[0, slot]),
+                pltpu.make_async_copy(d_full.at[cols], w_dn.at[slot], tile_sem.at[1, slot]),
+                pltpu.make_async_copy(gate.at[:, cols], gate_v.at[slot], tile_sem.at[2, slot]),
+                pltpu.make_async_copy(up.at[:, cols], up_v.at[slot], tile_sem.at[3, slot]),
+            ]
+
+        loads[0].start()
+        act_load(0, planes[0]).start()
+        act_load(1, planes[1]).start()
+        for copy in loads[1:] + fetch(0):
+            copy.start()
+        loads[0].wait()
+        own_d = bufs[0]
+        for i, z in enumerate(planes):
+            act_load(i, z).wait()
+            term = dot(act_v[i % 2].T, db[...]).astype(low).reshape(4, 2, d_shard_rows(width, ff), width)
+            if i < 2:
+                act_load(i + 2, planes[i + 2]).start()
+            four = pl.ds(place.plane(z) * 4, 4)
+            own_d[four] = jnp.where(first, term[:, 0], term[:, 1])
+            give_d[four] = jnp.where(first, term[:, 1], term[:, 0])
+            down.begin(z)
+        chunks(0)
+        for copy in loads[1:3]:
+            copy.wait()
+
+        def tiles(begin, own_g):
+            @pl.loop(begin, begin + half_g // tile)
+            def _(j):
+                slot = j % 2
+                for copy in fetch(j):
+                    copy.wait()
+
+                @pl.when(j + 1 < ff // tile)
+                def _():
+                    for copy in fetch(j + 1):
+                        copy.start()
+
+                d_act = dot(db[...], w_dn[slot], ((1,), (1,)))
+                d_gate = (d_act * gate_v[slot].astype(wide)).astype(low)
+                d_up = (d_act * up_v[slot].astype(wide)).astype(low)
+                resid[...] += dot(d_gate, w_gu[slot, 0].reshape(width, tile), ((1,), (1,))) + dot(
+                    d_up, w_gu[slot, 1].reshape(width, tile), ((1,), (1,))
+                )
+                cols = pl.ds(pl.multiple_of((j - begin) * tile, tile), tile)
+                mine = dot(ht[...], jnp.where(first, d_gate, d_up)).astype(low)
+                own_g[:, :, cols] = mine.reshape(16, rows_chip, tile)
+                other = dot(ht[...], jnp.where(first, d_up, d_gate)).astype(low)
+                give_g[:, :, cols] = other.reshape(16, rows_chip, tile)
+
+        tiles(0, bufs[7])
+        for z in planes:
+            left.begin(z)
+        chunks(1)
+        gives.drain(place.sib)
+        tiles(half_g // tile, bufs[14])
+        for z in planes:
+            right.begin(z)
+        chunks(2)
+        for copy in loads[3:]:
+            copy.wait()
+        grad = resid[...]
+        unit = norm_v[...]
+        small_buf[0] = small[...]
+        small_buf[0, 0:1, :] = column_sum(grad * unit)
+        small_buf[0, 1:2, :] = column_sum(grad)
+        exchange(0)
+        back = norm_back(grad, vectors[0:1, :], unit, inv_v[:, 0:1])
+        resid[...] = back
+        d_one = back.astype(low)
+        d_att[...] = dot(d_one, w_out[...].reshape(width, width), ((1,), (1,))).astype(low)
+        a_grad[1, :, :, width:] = dot(att_v[...].T, d_one).astype(low).reshape(16, rows_chip, width)
+        gives.drain(place.sib)
+
+    block = lambda *dims: pltpu.VMEM(dims, low)
+    block_wide = lambda *dims: pltpu.VMEM(dims, wide)
+    pl.run_scoped(
+        feed_forward, block(*bufs[0].shape), block(*bufs[7].shape), block(2, tok_rows, width),
+        block(tok_rows, width), block(width, tok_rows), block(2, 2, 16, rows_chip, tile), block(2, tile, width),
+        block(2, tok_rows, tile), block(2, tok_rows, tile), block(tok_rows, width), block_wide(tok_rows, width),
+        block_wide(tok_rows, lane_width), block(16, rows_chip, width),
+    )
 
     half = lambda side: pl.ds(pl.multiple_of(side * tok_rows, tok_rows), tok_rows)
 
-    def send_dkv(pair):
-        return pltpu.make_async_remote_copy(
-            src_ref=dkv_out.at[pair], dst_ref=dkv_in.at[pair], send_sem=pair_sem.at[0, pair],
-            recv_sem=pair_sem.at[1, pair], device_id=place.sib, device_id_type=MESH,
+    def attention_part(dq, dkv_own, dkv_out):
+        def send_dkv(pair):
+            return pltpu.make_async_remote_copy(
+                src_ref=dkv_out.at[pair], dst_ref=dkv_in.at[pair], send_sem=pair_sem.at[0, pair],
+                recv_sem=pair_sem.at[1, pair], device_id=place.sib, device_id_type=MESH,
+            )
+
+        def attention(q_v, k_v, v_v, span_v, att_v, dk_sum, dv_sum):
+            loads = [
+                pltpu.make_async_copy(src, dst, in_sem.at[i])
+                for i, (src, dst) in enumerate(((q, q_v), (k, k_v), (v, v_v), (span, span_v), (att, att_v)))
+            ]
+            for copy in loads:
+                copy.start()
+            for copy in loads:
+                copy.wait()
+
+            @pl.loop(0, pairs)
+            def _(pair):
+                attend_back_pair(pair, heads, q_v, k_v, v_v, span_v, lse, att_v, d_att, dq, dk_sum, dv_sum)
+                for i, part in enumerate((dk_sum, dv_sum)):
+                    dkv_own[pair, i] = part[half(c), :]
+                    dkv_out[pair, i] = part[half(1 - c), :].astype(low)
+                send_dkv(pair).start()
+                for i in range(3):
+
+                    @pl.when(pair == 2 * i)
+                    def _(i=i):
+                        chunks(3 + i)
+                        combine(i)
+                        if i < 2:
+                            exchange(i + 1)
+                        else:
+                            spread()
+
+        key_rows = k.shape[0]
+        pl.run_scoped(
+            attention, block(*q.shape), block(*k.shape), block(*v.shape), block_wide(*span.shape), block(*att.shape),
+            block_wide(key_rows, lane_width), block_wide(key_rows, lane_width),
         )
 
-    def attention(q_v, k_v, v_v, span_v, att_v, datt_v, dk_sum, dv_sum):
-        loads = [
-            pltpu.make_async_copy(src, dst, in_sem.at[i])
-            for i, (src, dst) in enumerate(
-                ((q, q_v), (k, k_v), (v, v_v), (span, span_v), (att, att_v), (d_att, datt_v))
-            )
-        ]
-        for copy in loads:
-            copy.start()
-        chunks(0)
-        for copy in loads:
-            copy.wait()
+        def finish(w_left, w_right, x, d_k, d_v):
+            loads = [
+                pltpu.make_async_copy(src, dst, in_sem.at[i])
+                for i, (src, dst) in enumerate(
+                    (
+                        (tokens, x),
+                        (a_full.at[0, :, :, : 2 * width], w_left),
+                        (a_full.at[1, :, :, :width], w_right),
+                    )
+                )
+            ]
+            for copy in loads:
+                copy.start()
+            for pair in range(pairs):
+                send_dkv(pair).wait_recv()
+                at = slice(pair * lane_width, (pair + 1) * lane_width)
+                d_k[:, at] = (dkv_own[pair, 0] + dkv_in[pair, 0].astype(wide)).astype(low)
+                d_v[:, at] = (dkv_own[pair, 1] + dkv_in[pair, 1].astype(wide)).astype(low)
+            loads[0].wait()
+            x_t = x[...].T
+            size = width // 2
+            for side, at, src in ((0, 0, dq), (0, width, d_k), (1, 0, d_v)):
+                for part in range(2):
+                    term = dot(x_t, src[:, part * size : (part + 1) * size]).astype(low)
+                    here = at + part * size
+                    a_grad[side, :, :, here : here + size] = term.reshape(16, rows_chip, size)
+            for z in planes:
+                proj.begin(z)
+            for copy in loads[1:]:
+                copy.wait()
+            w_q = w_left[:, :, :width].reshape(width, width)
+            total = resid[...] + dot(dq[...], w_q, ((1,), (1,)))
+            chunks(6)
+            w_k = w_left[:, :, width:].reshape(width, width)
+            total += dot(d_k[...], w_k, ((1,), (1,)))
+            total += dot(d_v[...], w_right[...].reshape(width, width), ((1,), (1,)))
+            d_tokens[...] = total.astype(low)
+
+        pl.run_scoped(
+            finish, block(16, rows_chip, 2 * width), block(16, rows_chip, width), block(tok_rows, width),
+            block(tok_rows, width), block(tok_rows, width),
+        )
 
         @pl.loop(0, pairs)
         def _(pair):
-            attend_back_pair(
-                pair, heads, q_v, k_v, v_v, span_v, lse, att_v, datt_v, dq, dk_sum, dv_sum
-            )
-            for i, part in enumerate((dk_sum, dv_sum)):
-                dkv_own[pair, i] = part[half(c), :]
-                dkv_out[pair, i] = part[half(1 - c), :].astype(low)
-            send_dkv(pair).start()
-            steps(pair)
-
-    block = lambda *shape: pltpu.VMEM(shape, low)
-    key_rows = k.shape[0]
+            send_dkv(pair).wait_send()
+
     pl.run_scoped(
-        attention, block(*q.shape), block(*k.shape), block(*v.shape), pltpu.VMEM(span.shape, wide),
-        block(*att.shape), block(*d_att.shape), pltpu.VMEM((key_rows, lane_width), wide),
-        pltpu.VMEM((key_rows, lane_width), wide),
-    )
-
-    def finish(w_left, w_right, resid, x_t, d_k, d_v):
-        loads = [
-            pltpu.make_async_copy(a_full.at[0, :, : 2 * width], w_left, in_sem.at[0]),
-            pltpu.make_async_copy(a_full.at[1, :, :width], w_right, in_sem.at[1]),
-            pltpu.make_async_copy(d_resid_one, resid, in_sem.at[2]),
-            pltpu.make_async_copy(grad_out, a_grad.at[1, :, :, width:], in_sem.at[3]),
-        ]
-        for copy in loads:
-            copy.start()
-        x_t[...] = tokens[...].astype(wide).T.astype(low)
-        for pair in range(pairs):
-            send_dkv(pair).wait_recv()
-            at = slice(pair * lane_width, (pair + 1) * lane_width)
-            d_k[:, at] = (dkv_own[pair, 0] + dkv_in[pair, 0].astype(wide)).astype(low)
-            d_v[:, at] = (dkv_own[pair, 1] + dkv_in[pair, 1].astype(wide)).astype(low)
-        tile = width // 2
-        for side, at, src in ((0, 0, dq), (0, width, d_k), (1, 0, d_v)):
-            for part in range(2):
-                cols = slice(part * tile, (part + 1) * tile)
-                term = dot(x_t[...], src[:, cols]).astype(low)
-                a_grad[side, :, :, at + part * tile : at + (part + 1) * tile] = term.reshape(16, rows_chip, tile)
-        loads[3].wait()
-        chunks(4)
-        for copy in loads[:3]:
-            copy.wait()
-        total = resid[...] + dot(dq[...], w_left[:, :width], ((1,), (1,)))
-        chunks(5)
-        total += dot(d_k[...], w_left[:, width:], ((1,), (1,))) + dot(d_v[...], w_right[...], ((1,), (1,)))
-        d_tokens[...] = total.astype(low)
-
-    pl.run_scoped(
-        finish, block(width, 2 * width), block(width, width), pltpu.VMEM((tok_rows, width), wide),
-        block(width, tok_rows), block(tok_rows, width), block(tok_rows, width),
+        attention_part, block(tok_rows, width), block_wide(pairs, 2, tok_rows, lane_width),
+        block(pairs, 2, tok_rows, lane_width),
     )
     for z in (1, 2, 3):
         last.got(small_buf.at[6 + z], 2 + z, place.zn[z])
     small_out[...] = (small_buf[3] + small_buf[7]) + (small_buf[8] + small_buf[9])
     mine, theirs = pl.ds(pl.multiple_of(24 * c, 8), 24), pl.ds(pl.multiple_of(24 - 24 * c, 8), 24)
-    chunks(6)
     down_out[...] = down.total()
     chunks(7)
-    g_sum[0] = gate.total()
+    g_sum[0] = left.total()
     last.put(g_sum.at[0, theirs], g_fin.at[0], 6, place.sib, lambda: g_fin.at[0])
     chunks(8)
     chunks(9)
-    g_sum[1] = rest.total()
+    g_sum[1] = right.total()
     last.put(g_sum.at[1, theirs], g_fin.at[1], 8, place.sib, lambda: g_fin.at[1])
     chunks(10)
-    first = c == 0
     for i, slot in ((0, 6), (1, 8)):
         last.got(g_fin.at[i], slot, place.sib)
         own, other = g_sum[i, mine], g_fin[i]
@@ -797,81 +1025,66 @@
     a_sum[...] = proj.total()
     last.put(a_sum.at[theirs], a_fin, 7, place.sib, lambda: a_fin)
     last.got(a_fin, 7, place.sib)
-    left = jnp.where(first, a_sum[mine], a_fin[...])
-    right = jnp.where(first, a_fin[...], a_sum[mine])
-    qkv_out[:, : 2 * width] = left
-    qkv_out[:, 2 * width :] = right[:, :width]
-    wout_out[...] = right[:, width:]
-
-    @pl.loop(0, pairs)
-    def _(pair):
-        send_dkv(pair).wait_send()
-
+    qkv_out[:, : 2 * width] = jnp.where(first, a_sum[mine], a_fin[...])
+    side = jnp.where(first, a_fin[...], a_sum[mine])
+    qkv_out[:, 2 * width :] = side[:, :width]
+    wout_out[...] = side[:, width:]
     copies.drain(place.sib)
     last.drain(place.sib)
 
 
-def back(heads, tokens, q, k, v, span, lse, att, d_att, d_resid_one, grad_out, a_full, g_grad, d_grad, small):
+def d_shard_rows(width, ff):
+    return ff // 32
+
+
+def back(heads, tokens, q, k, v, span, att, hid_t, norm, inv, gate, up, act, d_hid, d_branch, a_full, g_full, d_full, lse, vectors, small):
     low, wide = jnp.bfloat16, jnp.float32
     tok_rows, width = tokens.shape
-    half_g, half_a = g_grad.shape[-1], 2 * width
+    ff = gate.shape[1]
+    half_g, half_a = ff // 2, 2 * width
     pairs = heads // 2
-    d_rows = d_grad.shape[2]
+    d_rows = d_shard_rows(width, ff)
     bufs = []
-    shapes = ((d_rows, width), (rows_chip, half_g // 2), (rows_chip, half_g // 2), (rows_chip, half_a))
-    for i, (rows, half) in enumerate(shapes):
-        counts = (16, 16, 2, 2, 4, 4, 3)[i == 3 :]
-        bufs += [pltpu.VMEM((count, rows, half), low) for count in counts]
+    for i, (rows, half) in enumerate(((d_rows, width), (rows_chip, half_g), (rows_chip, half_g), (rows_chip, half_a))):
+        bufs += [pltpu.VMEM((count, rows, half), low) for count in (16, 16, 2, 2, 4, 4, 3)[i == 3 :]]
     vmem, hbm = pl.BlockSpec(memory_space=pltpu.VMEM), pl.BlockSpec(memory_space=pl.ANY)
-    keys = k.shape[0]
     dma = lambda *shape: pltpu.SemaphoreType.DMA(shape)
+    shape = jax.ShapeDtypeStruct
     return pl.pallas_call(
         lambda *refs: back_kernel(heads, *refs),
         out_shape=(
-            jax.ShapeDtypeStruct((tok_rows, width), low),
-            jax.ShapeDtypeStruct((24, 3 * width), wide),
-            jax.ShapeDtypeStruct((24, width), wide),
-            jax.ShapeDtypeStruct((24, 2 * half_g), wide),
-            jax.ShapeDtypeStruct((d_rows, width), wide),
-            jax.ShapeDtypeStruct(small.shape, wide),
+            shape((tok_rows, width), low), shape((24, 3 * width), wide), shape((24, width), wide),
+            shape((24, 2 * ff), wide), shape((d_rows, width), wide), shape(small.shape, wide),
         ),
-        in_specs=[vmem, hbm, hbm, hbm, hbm, vmem] + [hbm] * 7 + [vmem],
+        in_specs=[hbm] * 17 + [vmem] * 3,
         out_specs=(vmem,) * 6,
         scratch_shapes=bufs
         + [
             pltpu.VMEM((2, 16, rows_chip, half_a), low),
+            pltpu.VMEM((pairs, 2, tok_rows, lane_width), low),
+            pltpu.VMEM((tok_rows, width), wide),
             pltpu.VMEM((tok_rows, width), low),
-            pltpu.VMEM((pairs, 2, tok_rows, lane_width), wide),
-            pltpu.VMEM((pairs, 2, tok_rows, lane_width), low),
-            pltpu.VMEM((pairs, 2, tok_rows, lane_width), low),
-            pltpu.VMEM((2, rows_chip, half_g // 2), wide),
+            pltpu.VMEM((2, rows_chip, half_g), wide),
             pltpu.VMEM((rows_chip, half_a), wide),
-            pltpu.VMEM((2, 24, half_g // 2), wide),
+            pltpu.VMEM((2, 24, half_g), wide),
             pltpu.VMEM((24, half_a), wide),
             pltpu.VMEM((10,) + small.shape, wide),
             dma(4 * scatter_slots),
             dma(4 * scatter_slots),
-            dma(4 * scatter_slots),
             dma(2, pairs),
             dma(2, 9),
-            dma(6),
+            dma(9),
+            dma(4, 2),
         ],
         compiler_params=pltpu.CompilerParams(
-            collective_id=1, has_side_effects=True, vmem_limit_bytes=62 * 2**20
+            collective_id=1, has_side_effects=True, vmem_limit_bytes=63 * 2**20
         ),
-        cost_estimate=pl.CostEstimate(
-            flops=10 * tok_rows * keys * width, bytes_accessed=40 * width * width, transcendentals=heads * tok_rows * keys
-        ),
-        name="attention_back_and_sums",
-    )(tokens, q, k, v, span, lse, att, d_att, d_resid_one, grad_out, a_full, g_grad, d_grad, small)
+        name="backward_and_sums",
+    )(tokens, q, k, v, span, att, hid_t, norm, inv, gate, up, act, d_hid, d_branch, a_full, g_full, d_full, lse, vectors, small)
 
 
 def window(cells, width):
     count = lax.axis_size("blk")
-    if count == 2:
-        other = lax.ppermute(cells, "blk", [(0, 1), (1, 0)])
-        first = lax.axis_index("blk") == 0
-        return jnp.concatenate([jnp.where(first, cells, other), jnp.where(first, other, cells)], 0)
     before = lax.ppermute(cells, "blk", [(i, i + 1) for i in range(count - 1)])
     after = lax.ppermute(cells, "blk", [(i + 1, i) for i in range(count - 1)])
     return jnp.concatenate([before, cells, after], 0)
@@ -880,11 +1093,6 @@
 def window_back(terms, width):
     count = lax.axis_size("blk")
     low = jnp.bfloat16
-    if count == 2:
-        first = lax.axis_index("blk") == 0
-        upper, lower = terms[:width], terms[width:]
-        other = lax.ppermute(jnp.where(first, lower, upper).astype(low), "blk", [(0, 1), (1, 0)])
-        return jnp.where(first, upper, lower) + other.astype(terms.dtype)
     before = lax.ppermute(terms[2 * width :].astype(low), "blk", [(i, i + 1) for i in range(count - 1)])
     after = lax.ppermute(terms[:width].astype(low), "blk", [(i + 1, i) for i in range(count - 1)])
     return terms[width : 2 * width] + before.astype(terms.dtype) + after.astype(terms.dtype)
@@ -909,48 +1117,56 @@
     return lax.axis_size("rows") == 16 and lax.axis_size("blk") == 2
 
 
-def gathered_weights(w_qkv, w_out, ln1_gain, ln1_bias, w_gate_up, w_down, ln2_gain, ln2_bias):
-    rows, width = w_out.shape
+def packed_shards(w_qkv, w_out, ln1_gain, ln1_bias, w_gate_up, ln2_gain, ln2_bias):
+    width = w_out.shape[1]
     ff = w_gate_up.shape[1] // 2
     table = jnp.stack((ln1_gain, ln1_bias, ln2_gain, ln2_bias), 1)
     table = jnp.pad(table, ((0, 0), (0, lane_width - 4)))
     left = jnp.concatenate([w_qkv[:, : 2 * width], table], 1)
     right = jnp.concatenate([w_qkv[:, 2 * width :], w_out, jnp.zeros_like(table)], 1)
-    a_shard = jnp.stack([left, right])
-    g_shard = jnp.stack([w_gate_up[:, :ff], w_gate_up[:, ff:]])
-    if not on_chip_grid():
-        both = ("rows", "blk")
-        return (
-            lax.all_gather(a_shard, both, axis=1, tiled=True),
-            lax.all_gather(g_shard, both, axis=1, tiled=True),
-            lax.all_gather(w_down, both, axis=0, tiled=True),
-        )
-    spare = ((0, 0), (0, 32 - rows), (0, 0))
-    a_full, g_full, d_full = gather_weights(jnp.pad(a_shard, spare), jnp.pad(g_shard, spare), w_down)
-    return a_full.reshape(2, width, -1), g_full.reshape(2, width, ff), d_full.reshape(-1, width)
-
-
-def back_and_sums(heads, tokens, q, k, v, span, lse, att, d_att, d_resid_one, grad_out, a_full, g_grad, d_grad, small):
+    return jnp.stack([left, right]), jnp.stack([w_gate_up[:, :ff], w_gate_up[:, ff:]])
+
+
+def on_grid(tokens, a_shard, g_shard, w_down, span, valid, out_grad):
+    spare = ((0, 0), (0, 32 - a_shard.shape[1]), (0, 0))
+    (
+        a_full, g_full, d_full, q, k, v, att, hid_t, norm, inv, gate, up, act, output, d_hid, d_branch, lse, vectors, small,
+    ) = fore(HEADS, tokens, jnp.pad(a_shard, spare), jnp.pad(g_shard, spare), w_down, valid, span, out_grad)
+    d_full = d_full.reshape(-1, tokens.shape[1])
+    return output, *back(
+        HEADS, tokens, q, k, v, span, att, hid_t, norm, inv, gate, up, act, d_hid, d_branch, a_full, g_full, d_full, lse,
+        vectors, small,
+    )
+
+
+def on_any(tokens, a_shard, g_shard, w_down, span, valid, out_grad):
     both = ("rows", "blk")
     tok_rows, width = tokens.shape
-    if on_chip_grid():
-        split = lambda g: g.reshape(2, 16, rows_chip, g.shape[2])
-        return back(
-            heads, tokens, q, k, v, span, lse, att, d_att, d_resid_one, grad_out.reshape(16, rows_chip, width),
-            a_full, split(g_grad), d_grad.reshape(16, 2, -1, width), small,
-        )
-    low = jnp.bfloat16
-    dq, dk, dv = attend_back(q, k, v, span, lse, att, d_att, heads)
+    low, wide = jnp.bfloat16, jnp.float32
+    a_full = lax.all_gather(a_shard, both, axis=1, tiled=True)
+    w_gu = lax.all_gather(g_shard, both, axis=1, tiled=True)
+    w_dn = lax.all_gather(w_down, both, axis=0, tiled=True)
+    vectors = jnp.pad(a_full[0, :, 2 * width : 2 * width + 4].astype(wide).T, ((0, 4), (0, 0)))
+    w_qk, w_v = a_full[0, :, : 2 * width], a_full[1, :, :width]
+    qk = jnp.dot(tokens, w_qk, preferred_element_type=wide).astype(low)
+    v = jnp.dot(tokens, w_v, preferred_element_type=wide).astype(low)
+    query = qk[:, :width] * (width // HEADS) ** -0.5
+    kv = window(jnp.concatenate([qk[:, width:], v], 1), tok_rows)
+    keys, values = kv[:, :width], kv[:, width:]
+    attended, lse = attend(query, keys, values, span, HEADS)
+    output, d_resid_one, d_att, grad_out, g_grad, d_grad, small = ffn(
+        tokens, attended, a_full, vectors, valid, out_grad, w_gu, w_dn
+    )
+    dq, dk, dv = attend_back(query, keys, values, span, lse, attended, d_att, HEADS)
     dkv = window_back(jnp.concatenate([dk, dv], 1), tok_rows)
     d_qk = jnp.concatenate([dq, dkv[:, :width].astype(low)], 1)
     d_v = dkv[:, width:].astype(low)
     grad_qkv = transposed_times(tokens, jnp.concatenate([d_qk, d_v], 1))
-    d_tokens = d_resid_one + times_transposed(d_qk, a_full[0, :, : 2 * width])
-    d_tokens = d_tokens + times_transposed(d_v, a_full[1, :, :width])
-    share = lambda g, axis: lax.psum_scatter(g.astype(jnp.float32), both, scatter_dimension=axis, tiled=True)
+    d_tokens = d_resid_one + times_transposed(d_qk, w_qk) + times_transposed(d_v, w_v)
+    share = lambda g, axis: lax.psum_scatter(g.astype(wide), both, scatter_dimension=axis, tiled=True)
     gate, up = share(g_grad, 1)
     return (
-        d_tokens.astype(low), share(grad_qkv, 0), share(grad_out, 0), jnp.concatenate([gate, up], 1),
+        output, d_tokens.astype(low), share(grad_qkv, 0), share(grad_out, 0), jnp.concatenate([gate, up], 1),
         share(d_grad, 0), lax.psum(small, both),
     )
 
@@ -960,28 +1176,14 @@
 ):
     inputs, labels = tokens[0], segments[0]
     tok_rows, width = inputs.shape
-    low, wide = jnp.bfloat16, jnp.float32
     both = ("rows", "blk")
     first = lax.axis_index("blk") * tok_rows
     span = key_spans(labels, first, tok_rows)
-    valid = (lax.dynamic_slice_in_dim(labels, first, tok_rows, 0) != labels.shape[0]).astype(wide)[:, None]
-    a_full, w_gu, w_dn = gathered_weights(
-        w_qkv, w_out, ln1_gain, ln1_bias, w_gate_up, w_down, ln2_gain, ln2_bias
-    )
-    vectors = jnp.pad(a_full[0, :, 2 * width : 2 * width + 4].astype(wide).T, ((0, 4), (0, 0)))
-    w_qk, w_v = a_full[0, :, : 2 * width], a_full[1, :, :width]
-    qk = jnp.dot(inputs, w_qk, preferred_element_type=wide).astype(low)
-    v = jnp.dot(inputs, w_v, preferred_element_type=wide).astype(low)
-    query = qk[:, :width]
-    kv = window(jnp.concatenate([qk[:, width:], v], 1), tok_rows)
-    keys, values = kv[:, :width], kv[:, width:]
-    attended, lse = attend(query, keys, values, span, HEADS)
-    output, d_resid_one, d_att, grad_out, g_grad, d_grad, small = ffn(
-        inputs, attended, a_full, vectors, valid, out_grad[0], w_gu, w_dn
-    )
-    d_tokens, *parts, small = back_and_sums(
-        HEADS, inputs, query, keys, values, span, lse, attended, d_att, d_resid_one, grad_out, a_full, g_grad, d_grad, small
-    )
+    here = lax.dynamic_slice_in_dim(labels, first, tok_rows, 0)
+    valid = (here != labels.shape[0]).astype(jnp.float32)[:, None]
+    a_shard, g_shard = packed_shards(w_qkv, w_out, ln1_gain, ln1_bias, w_gate_up, ln2_gain, ln2_bias)
+    run = on_grid if on_chip_grid() else on_any
+    output, d_tokens, *parts, small = run(inputs, a_shard, g_shard, w_down, span, valid, out_grad[0])
     share = width // lax.axis_size(both)
     mine = lax.axis_index(both) * share
     rows = lax.dynamic_slice_in_dim(small[:4], mine, share, 1)

time: 276 us -> 234 us (0.85)
  Pallas kernels: 242 us -> 214 us
  local copies, waits for them, and re-layouts: 19.3 us -> 10.2 us
    pallas_call x4 -> x2, Pallas kernels: 242 us -> 214 us  [the longest x1 113 us: back(): pl.pallas_call(lambda *refs: back_kernel(heads, *refs), out_shape=(shape(...]
    unnamed x23 -> x20, local copies, waits for them, and re-layouts: 11 us -> 4.64 us
  transfers between devices with their start and end apart: 1 -> 0, of which waited for: 0 -> 0; matrix products, arithmetic and copies ran while one was open for 2% -> 0% of each run, Pallas kernels for 0% -> 0%
where the time goes in v4:
time: 234 us; the launch traced here: 233 us
  Pallas kernels  214 us (91%)
  local copies, waits for them, and re-layouts  10.2 us (4%)
  other arithmetic  7.95 us (3%)
    pallas_call x1, Pallas kernels, back(): pl.pallas_call(lambda *refs: back_kernel(heads, *refs), out_shape=(shape(...  113 us
    pallas_call x1, Pallas kernels, fore(): pl.pallas_call(lambda *refs: fore_kernel(heads, *refs), out_shape=tuple((...  101 us

profile of v4, /device:TPU:0, one launch (start us, length us, event | category | flops | bytes accessed | tf_op | source)
XLA Modules:
  0.0 233.4 jit_solution(15561117600155605479)
XLA Ops:
  0.6 0.0 copy-start.6
  0.7 0.7 pad_maximum_fusion
  1.4 0.7 broadcast_compare_fusion
  2.1 0.7 fusion.11
  2.8 0.1 copy.31
  2.9 0.8 slice.34
  3.7 0.9 slice.33
  4.6 0.8 fusion.10
  5.3 0.7 fusion.7.refs_1_
  6.0 0.9 copy.32.refs_4_
  6.9 1.0 slice_bitcast_fusion.1
  7.9 0.8 fusion.6.refs_2_
  8.7 0.0 copy-done.6
  8.7 2.1 convert_select_fusion.refs_5_.refs_4_
  10.8 101.1 %gather_and_forward.1 = (bf16[2,16,48,1664]{3,2,1,0:T(8,128)(2,1)}, bf16[2,16,48,3072]{3,2,1,0:T(8,128)(2,1)}, bf16[16,2,96,768]{3,2,1,0:T(8,128)(2,1)}, bf16[51...) custom-call(bf16[512,768]{1,0:T(8,128)(2,1)} %bitcast.31, ...), custom_call_target="tpu_custom_call" | custom-call | tf_op jit(solution)/shard_map/gather_and_forward/pallas_call | solution.py:745
  111.9 0.0 copy-start
  111.9 112.8 %backward_and_sums.1 = (bf16[512,768]{1,0:T(8,128)(2,1)}, f32[24,2304]{1,0:T(8,128)}, f32[24,768]{1,0:T(8,128)}, f32[24,6144]{1,0:T(8,128)}, f32[96,768]{1,0:T(8,128)}, /*index=5*/f32[16,768]{1,0:T(8,128)}) custom-call(bf16[512,768]{1,0:T(8,128)(2,1)} %bitcast.32, bf16[512,768]{1,0:T(8,128)(2,1)} %get-tuple-element.37.refs_1_, ...), custom_call_target="tpu_custom_call" | custom-call | tf_op jit(solution)/shard_map/backward_and_sums/pallas_call | solution.py:1053
  224.7 0.0 copy-start.1
  224.7 0.0 copy-start.4
  224.7 0.0 copy-start.5
  224.7 0.0 copy-start.2
  224.7 1.3 slice.43
  226.7 0.9 slice_reduce_fusion
  227.6 0.5 divide_sqrt_fusion
  228.2 0.1 constant_dynamic-slice_fusion
  228.2 0.5 slice_bitcast_fusion.2
  228.8 0.0 copy-done
  228.8 0.0 copy-start.3
  228.8 0.9 copy.39
  229.7 0.0 copy-done.1
  229.7 0.9 copy.40
  230.5 0.0 copy-done.4
  230.5 0.7 copy.41
  231.2 0.0 copy-done.5
  231.2 0.6 copy.42
  231.9 0.0 copy-done.2
  231.9 0.8 copy.43
  232.7 0.0 copy-done.3
  232.7 0.7 copy.44
  (3 shorter events, 0.0 us)
Async XLA Ops:
  0.6 8.0 %copy-start.6 = (s32[1,1024]{1,0:T(1,128)S(1)}, s32[1,1024]{1,0:T(1,128)}, u32[]{:S(2)}) copy-start(s32[1,1024]{1,0:T(1,128)} %param.12) | copy-start | bytes 12292
  111.9 116.9 %copy-start = (bf16[512,768]{1,0:T(8,128)(2,1)S(1)}, bf16[512,768]{1,0:T(8,128)(2,1)}, u32[]{:S(2)}) copy-start(bf16[512,768]{1,0:T(8,128)(2,1)} %get-tuple-element.36) | copy-start | bytes 2359300
  224.7 5.0 %copy-start.1 = (bf16[512,768]{1,0:T(8,128)(2,1)S(1)}, bf16[512,768]{1,0:T(8,128)(2,1)}, u32[]{:S(2)}) copy-start(bf16[512,768]{1,0:T(8,128)(2,1)} %get-tuple-element.55) | copy-start | bytes 2359300
  224.7 5.8 %copy-start.4 = (f32[24,2304]{1,0:T(8,128)S(1)}, f32[24,2304]{1,0:T(8,128)}, u32[]{:S(2)}) copy-start(f32[24,2304]{1,0:T(8,128)} %get-tuple-element.86) | copy-start | bytes 663556
  224.7 6.5 %copy-start.5 = (f32[24,768]{1,0:T(8,128)S(1)}, f32[24,768]{1,0:T(8,128)}, u32[]{:S(2)}) copy-start(f32[24,768]{1,0:T(8,128)} %get-tuple-element.87) | copy-start | bytes 221188
  224.7 7.1 %copy-start.2 = (f32[24,6144]{1,0:T(8,128)S(1)}, f32[24,6144]{1,0:T(8,128)}, u32[]{:S(2)}) copy-start(f32[24,6144]{1,0:T(8,128)} %get-tuple-element.90) | copy-start | bytes 1769476
  228.8 3.9 %copy-start.3 = (f32[96,768]{1,0:T(8,128)S(1)}, f32[96,768]{1,0:T(8,128)}, u32[]{:S(2)}) copy-start(f32[96,768]{1,0:T(8,128)} %get-tuple-element.91) | copy-start | bytes 884740

commit v5 on v4

--- a/solution.py
+++ b/solution.py
@@ -51,11 +51,12 @@
         return self.plane(k) * 4 + y * 2 + x
 
     def greet(self):
-        barrier = pltpu.get_barrier_semaphore()
-        peers = [self.sib, self.xn, self.yn] + [self.zn[k] for k in (1, 2, 3)]
-        for peer in peers:
-            pl.semaphore_signal(barrier, inc=1, device_id=peer, device_id_type=MESH)
-        pl.semaphore_wait(barrier, len(peers))
+        self.barrier = pltpu.get_barrier_semaphore()
+        for peer in (self.sib, self.xn, self.yn, *self.zn.values()):
+            pl.semaphore_signal(self.barrier, inc=1, device_id=peer, device_id_type=MESH)
+
+    def meet(self):
+        pl.semaphore_wait(self.barrier, 6)
 
 
 class Copies:
@@ -98,9 +99,12 @@
     def push(self, src, k, j):
         self.send(src, self.block(k, j), self.slot("s", k, j), self.p.sib)
 
-    def to_z(self, k):
-        if k:
+    def to_z(self):
+        for k in (1, 2):
             self.send(self.block(0, "o"), self.block(0, "o"), self.slot("z", k), self.p.zn[k])
+
+    def to_xy(self):
+        self.spread(self.block(0, "o"), 0)
 
     def spread(self, src, k):
         dst = self.block(k, "o")
@@ -109,12 +113,36 @@
         self.push(src, k, "o")
 
     def from_z(self, k):
-        if k == 0:
-            self.spread(self.block(0, "o"), 0)
-            return
         block = self.block(k, "o")
         self.cp.got(block, self.slot("z", k), self.p.zn[k])
+        if k == 2:
+            self.send(block, block, self.slot("z", 3), self.p.zn[1])
         self.spread(block, k)
+
+    @staticmethod
+    def schedule(mats):
+        work = [(mats[0].to_z,)] + [(m.to_xy,) for m in mats[:3]]
+        for i, m in enumerate(mats):
+            before = mats[i - 1] if i else None
+            work.append((m.from_z, 1))
+            if i + 1 < len(mats):
+                work.append((mats[i + 1].to_z,))
+            if before:
+                work.append((before.from_xy, 3))
+            work += [(m.from_xy, 0), (m.from_z, 2)]
+            if before:
+                work.append((before.from_d, 2))
+            if i + 3 < len(mats):
+                work.append((mats[i + 3].to_xy,))
+            work += [(m.from_xy, 1), (m.from_z, 3)]
+            if before:
+                work.append((before.from_d, 1))
+            work.append((m.from_d, 0))
+            if before:
+                work.append((before.from_d, 3))
+            work.append((m.from_xy, 2))
+        last = mats[-1]
+        return work + [(last.from_xy, 3), (last.from_d, 2), (last.from_d, 1), (last.from_d, 3)]
 
     def from_xy(self, k):
         x, y = self.block(k, "x"), self.block(k, "y")
@@ -126,14 +154,6 @@
             self.send(y, y, self.slot("d", k), self.p.xn)
         self.push(x, k, "x")
         self.push(y, k, "y")
-
-    def from_even(self, k):
-        if k % 2 == 0:
-            self.from_d(k)
-
-    def from_odd(self, k):
-        if k % 2:
-            self.from_d(k)
 
     def from_d(self, k):
         block = self.block(k, "d")
@@ -221,37 +241,47 @@
             self.xin[k].astype(wide) + self.yin[k].astype(wide)
         )
         own[...] = total.astype(jnp.bfloat16)
-        if k:
-            self.cp.put(own, self.zin.at[k - 1], self.slot("z", k), p.zn[k], lambda: self.zin.at[k - 1])
+        if k % 2:
+            self.to_z(own, k, 1)
+
+    def to_z(self, own, k, step):
+        self.cp.put(own, self.zin.at[k - 1], self.slot("z", k), self.p.zn[step], lambda: self.zin.at[k - 1])
+
+    def cross(self):
+        self.cp.got(self.zin.at[2], self.slot("z", 3), self.p.zn[1])
+        own = self.own(self.p.at(2, "o"))
+        own[...] = own[...] + self.zin[2]
+        self.to_z(own, 2, 2)
+
+    def all(self, name, *planes):
+        for k in planes:
+            getattr(self, name)(k)
+
+    def first(self):
+        self.all("pair", 3, 1)
+
+    def rest(self):
+        self.all("pair", 2, 0)
+
+    def diags(self):
+        self.all("diag", 2, 0)
+
+    def relays(self):
+        self.all("relay", 2, 0)
+
+    def odd(self):
+        self.all("plane", 3, 1)
+
+    def even(self):
+        self.all("plane", 2, 0)
+        self.cross()
 
     def total(self):
-        for k in (1, 2, 3):
+        for k in (1, 2):
             self.cp.got(self.zin.at[k - 1], self.slot("z", k), self.p.zn[k])
         wide = jnp.float32
         own = self.own(self.p.at(0, "o"))
-        return (own[...].astype(wide) + self.zin[0].astype(wide)) + (
-            self.zin[1].astype(wide) + self.zin[2].astype(wide)
-        )
-
-
-class Steps:
-    def __init__(self, items, stages):
-        self.items, self.stages = items, stages
-
-    def __call__(self, t):
-        for name, lag in self.stages:
-            if 0 <= t - lag < len(self.items):
-                matrix, planes = self.items[t - lag]
-                for k in planes:
-                    getattr(matrix, name)(k)
-
-    def count(self):
-        return len(self.items) + max(lag for _, lag in self.stages)
-
-
-gather_stages = (("to_z", -2), ("from_z", 0), ("from_xy", 1), ("from_even", 2), ("from_odd", 3))
-scatter_stages = (("pair", 0), ("diag", 1), ("relay", 2), ("plane", 3))
-near_far, far_near = ((0, 1), (2, 3)), ((3, 2), (1, 0))
+        return own[...].astype(wide) + (self.zin[0].astype(wide) + self.zin[1].astype(wide))
 
 
 rows_chip = 48
@@ -557,10 +587,10 @@
 
 
 def fore_kernel(
-    heads, tokens, a_shard, g_shard, d_shard, valid, span, out_grad,
+    heads, tokens, labels, w_qkv, w_out, w_gu, d_shard, norms, out_grad,
     a_full, g_full, d_full, q_out, k_out, v_out, att_out, hid_t_out, norm_out, inv_out, gate_out, up_out, act_out,
-    output_out, d_hid_out, d_branch_out, lse, vectors, small,
-    w_a, w_g, w_d, a_pair, g_pair, q, k, v, att, span_v, grad_v, hid, hid_low, hid_t, norm_one, inv_one,
+    output_out, d_hid_out, d_branch_out, span_out, lse, vectors, small,
+    w_a, w_g, w_d, a_give, g_give, a_pair, g_pair, turned, q, k, v, att, span_v, grad_v, hid, hid_low, hid_t, norm_one, inv_one,
     slope_gate, slope_up, act, output, d_hid, d_branch, pair_sem, send, recv, in_sem, out_sem,
 ):
     place = Place()
@@ -571,12 +601,22 @@
     ff = w_g.shape[3]
     half_g = ff // 2
     pairs = heads // 2
-    loads = [pltpu.make_async_copy(src, dst, in_sem.at[i]) for i, (src, dst) in enumerate(((span, span_v), (out_grad, grad_v)))]
-    for copy in loads:
-        copy.start()
+    load = pltpu.make_async_copy(out_grad, grad_v, in_sem.at[0])
+    load.start()
+    core_one = c == 1
+    turned[...] = jnp.zeros_like(turned)
+    turned[0:4, 0 : norms.shape[1]] = norms[...].astype(wide)
+    table = turned[...].T[: norms.shape[1]].astype(low)
+    left = jnp.concatenate([w_qkv[:, : 2 * width], table], 1)
+    right = jnp.concatenate([w_qkv[:, 2 * width :], w_out[...], jnp.zeros_like(table)], 1)
+    gate, up = w_gu[:, :ff], w_gu[:, ff:]
+    rows = w_qkv.shape[0]
+    a_give[:rows, :] = jnp.where(core_one, left, right)
+    g_give[:rows, :] = jnp.where(core_one, gate, up)
     swaps = Copies(pair_sem.at[0], pair_sem.at[1])
-    for i, (shard, other) in enumerate(((a_shard, a_pair), (g_shard, g_pair))):
-        swaps.put(shard.at[1 - c], other, i, place.sib)
+    place.meet()
+    for i, (give, other) in enumerate(((a_give, a_pair), (g_give, g_pair))):
+        swaps.put(give, other, i, place.sib)
     copies = Copies(send, recv)
     outs = [
         lambda half, r: w_a.at[half, r],
@@ -585,26 +625,44 @@
         lambda half, r: w_d.at[r, half],
     ]
     mats = [Gather(place, copies, i * gather_slots, out) for i, out in enumerate(outs)]
-    steps = Steps([(m, planes) for m in mats for planes in near_far], gather_stages)
+    first, second, third, fourth = mats
     me = place.at(0, "o")
 
-    def assemble(shard, other, full, i):
+    def assemble(mine, other, full, i):
         swaps.got(other, i, place.sib)
-        mine = shard[c, :24, :].astype(wide)
-        theirs = other[:24, :].astype(wide)
-        first = c == 0
-        top = jnp.where(first, mine, theirs)
-        rest = jnp.where(first, theirs, mine)
+        mine = mine.astype(wide)
+        theirs = other[:rows, :].astype(wide)
+        top = jnp.where(core_one, theirs, mine)
+        rest = jnp.where(core_one, mine, theirs)
         full[c, me] = jnp.concatenate([top, rest], 0).astype(low)
 
-    assemble(a_shard, a_pair, w_a, 0)
-    steps(-2)
-    steps(-1)
-    assemble(g_shard, g_pair, w_g, 1)
+    work = Gather.schedule(mats)
+
+    def go(count):
+        for step, *plane in work[:count]:
+            step(*plane)
+        del work[:count]
+
+    def upto(matrix):
+        done = [i for i, (step, *_) in enumerate(work) if step == matrix.from_d]
+        go(done[-1] + 1 if done else 0)
+
+    assemble(jnp.where(core_one, right, left), a_pair, w_a, 0)
+    go(2)
+    assemble(jnp.where(core_one, up, gate), g_pair, w_g, 1)
     w_d[me, c] = d_shard[...]
-    for t in range(5):
-        steps(t)
-    mats[0].from_sib()
+    seq_len = labels.shape[1]
+    label_row = labels[...].astype(wide)
+    label_column = jnp.broadcast_to(label_row, (lane_width, seq_len)).T[:, 0:1]
+    half = pl.ds(pl.multiple_of(c * tok_rows, tok_rows), tok_rows)
+    same = (label_column == labels[:, half].astype(wide)) & (label_column != seq_len)
+    key_at = lax.broadcasted_iota(jnp.int32, span_v.shape, 0)
+    gap = jnp.abs(key_at - lax.broadcasted_iota(jnp.int32, span_v.shape, 1) - c * tok_rows)
+    span_v[...] = jnp.where(same | (gap == 0), gap.astype(wide), far)
+    mask = jnp.broadcast_to(labels[:, half].astype(wide), (lane_width, tok_rows)).T[:, 0:1]
+    mask = (mask != seq_len).astype(wide)
+    upto(first)
+    first.from_sib()
     saved = []
 
     def save(src, dst):
@@ -613,33 +671,39 @@
         saved.append((src, dst))
 
     save(w_a, a_full)
+    save(span_v, span_out)
     part = lambda half, at, size: w_a[half, :, :, at : at + size].reshape(width, size)
     vectors[...] = part(0, 2 * width, lane_width).astype(wide).T[:8]
     x = tokens[...]
-    half = pl.ds(pl.multiple_of(c * tok_rows, tok_rows), tok_rows)
     k[half, :] = dot(x, part(0, width, width)).astype(low)
     swaps.put(k.at[half], k.at[half], 2, place.sib, lambda: k.at[pl.ds(0, tok_rows)])
     v[half, :] = dot(x, part(1, 0, width)).astype(low)
     swaps.put(v.at[half], v.at[half], 3, place.sib, lambda: v.at[pl.ds(0, tok_rows)])
     depth = width // heads
     q[...] = dot(x, part(0, 0, width)).astype(low) * depth**-0.5
-    steps(5)
+    go(3)
     other = pl.ds(pl.multiple_of((1 - c) * tok_rows, tok_rows), tok_rows)
     swaps.got(k.at[other], 2, place.sib)
     swaps.got(v.at[other], 3, place.sib)
     save(q, q_out)
     save(k, k_out)
     save(v, v_out)
-    loads[0].wait()
+
+    shares = (4, 4, 4, 4, 3, 3)
+    todo = []
+    for count in shares:
+        todo.append(work[:count])
+        del work[:count]
 
     @pl.loop(0, pairs)
     def _(pair):
         attend_pair(pair, heads, q, k, v, span_v, lse, att)
-        for i in range(3):
-
-            @pl.when(pair == 2 * i + 1)
-            def _(i=i):
-                steps(6 + i)
+        for at, steps in enumerate(todo):
+
+            @pl.when(pair == at)
+            def _(steps=steps):
+                for step, *plane in steps:
+                    step(*plane)
 
     save(att, att_out)
     branch = dot(att[...], part(1, width, width))
@@ -654,7 +718,6 @@
     save(hid_t, hid_t_out)
     save(norm_one, norm_out)
     save(inv_one, inv_out)
-    mask = valid[...]
     small[0:4, :] = jnp.zeros((4, width), wide)
     small[4:5, :] = column_sum(mask * toks * toks)
     small[5:6, :] = column_sum(mask * branch * branch)
@@ -675,25 +738,28 @@
         slope_gate[:, cols] = (up * (cdf + gate * density)).astype(low)
         act[:, cols] = (mixed * up).astype(low)
 
-    mats[1].from_sib()
+    upto(second)
+    second.from_sib()
+    save(w_g.at[:, :, :, :half_g], g_full.at[:, :, :, :half_g])
 
     @pl.loop(0, half_g // tile)
     def _(j):
         glu(j)
 
-    steps(9)
-    mats[2].from_sib()
-    save(w_g, g_full)
+    upto(third)
+    third.from_sib()
+    save(w_g.at[:, :, :, half_g:], g_full.at[:, :, :, half_g:])
+    for src, dst in ((slope_gate, gate_out), (slope_up, up_out), (act, act_out)):
+        save(src.at[:, :half_g], dst.at[:, :half_g])
 
     @pl.loop(half_g // tile, ff // tile)
     def _(j):
         glu(j)
 
-    save(slope_gate, gate_out)
-    save(slope_up, up_out)
-    save(act, act_out)
-    steps(10)
-    mats[3].from_sib()
+    for src, dst in ((slope_gate, gate_out), (slope_up, up_out), (act, act_out)):
+        save(src.at[:, half_g:], dst.at[:, half_g:])
+    upto(fourth)
+    fourth.from_sib()
     save(w_d, d_full)
     d_hid[...] = jnp.zeros_like(d_hid)
     chips = 4
@@ -710,7 +776,7 @@
     gain = vectors[2:3, :]
     output[...] = (norm * gain + vectors[3:4, :]).astype(low)
     save(output, output_out)
-    loads[1].wait()
+    load.wait()
     grad = grad_v[...].astype(wide)
     small[2:3, :] = column_sum(grad * norm)
     small[3:4, :] = column_sum(grad)
@@ -725,11 +791,12 @@
     copies.drain(place.sib)
 
 
-def fore(heads, tokens, a_shard, g_shard, d_shard, valid, span, out_grad):
+def fore(heads, tokens, labels, w_qkv, w_out, w_gu, d_shard, norms, out_grad):
     low, wide = jnp.bfloat16, jnp.float32
     rows, width = tokens.shape
-    half_a, ff = a_shard.shape[-1], g_shard.shape[-1]
-    keys = span.shape[0]
+    ff = w_gu.shape[1] // 2
+    half_a = 2 * width + lane_width
+    keys = labels.shape[1]
     vmem, hbm = pl.BlockSpec(memory_space=pltpu.VMEM), pl.BlockSpec(memory_space=pl.ANY)
     dma = lambda *shape: pltpu.SemaphoreType.DMA(shape)
     shape = jax.ShapeDtypeStruct
@@ -738,7 +805,7 @@
         (w_a, low), (w_g, low), (w_d, low), ((rows, width), low), ((keys, width), low), ((keys, width), low),
         ((rows, width), low), ((width, rows), low), ((rows, width), wide), ((rows, lane_width), wide),
         ((rows, ff), low), ((rows, ff), low), ((rows, ff), low), ((rows, width), low), ((rows, width), wide),
-        ((rows, width), low),
+        ((rows, width), low), ((keys, rows), wide),
     ]
     block = lambda *dims: pltpu.VMEM(dims, low)
     block_wide = lambda *dims: pltpu.VMEM(dims, wide)
@@ -746,26 +813,27 @@
         lambda *refs: fore_kernel(heads, *refs),
         out_shape=tuple(shape(dims, kind) for dims, kind in stored)
         + (shape((16, rows), wide), shape((8, width), wide), shape((16, width), wide)),
-        in_specs=[vmem] * 5 + [hbm] * 2,
+        in_specs=[vmem] * 7 + [hbm],
         out_specs=(hbm,) * len(stored) + (vmem,) * 3,
         scratch_shapes=[
-            block(*w_a), block(*w_g), block(*w_d), block(*a_shard.shape[1:]), block(*g_shard.shape[1:]),
+            block(*w_a), block(*w_g), block(*w_d), block(32, half_a), block(32, ff), block(32, half_a), block(32, ff),
+            block_wide(lane_width, lane_width),
             block(rows, width), block(keys, width), block(keys, width), block(rows, width),
             block_wide(keys, rows), block(rows, width), block_wide(rows, width), block(rows, width),
             block(width, rows), block_wide(rows, width), block_wide(rows, lane_width),
             block(rows, ff), block(rows, ff), block(rows, ff), block(rows, width), block_wide(rows, width),
-            block(rows, width), dma(2, 4), dma(4 * gather_slots), dma(4 * gather_slots), dma(2), dma(len(stored)),
+            block(rows, width), dma(2, 4), dma(4 * gather_slots), dma(4 * gather_slots), dma(1), dma(len(stored) + 4),
         ],
         compiler_params=pltpu.CompilerParams(
             collective_id=0, has_side_effects=True, vmem_limit_bytes=62 * 2**20
         ),
         name="gather_and_forward",
-    )(tokens, a_shard, g_shard, d_shard, valid, span, out_grad)
+    )(tokens, labels, w_qkv, w_out, w_gu, d_shard, norms, out_grad)
 
 
 def back_kernel(
     heads, tokens, q, k, v, span, att, hid_t, norm, inv, gate, up, act, d_hid, d_branch, a_full, g_full, d_full,
-    lse, vectors, small, d_tokens, qkv_out, wout_out, gu_out, down_out, small_out, *scratch,
+    lse, vectors, small, d_tokens, qkv_out, wout_out, gu_out, down_out, tail, *scratch,
 ):
     place = Place()
     place.greet()
@@ -775,23 +843,24 @@
     tok_rows, width = tokens.shape
     ff = gate.shape[1]
     pairs = heads // 2
-    bufs, rest = scratch[:27], scratch[27:]
+    bufs, rest = scratch[:33], scratch[33:]
     a_grad, dkv_in, resid, d_att, g_sum, a_sum, g_fin, a_fin, small_buf, send, recv, pair_sem, fin_sem, in_sem, tile_sem = rest
     copies = Copies(send, recv)
-    gives = Copies(send, recv)
+    gives, gives_down = Copies(send, recv), Copies(send, recv)
     last = Copies(fin_sem.at[0], fin_sem.at[1])
-    half_g = ff // 2
+    half_g, part = ff // 2, width // 2
 
     def scatter(i, own, *more):
-        give = lambda four: None
-        return Scatter(place, copies, gives, i * scatter_slots, give, lambda at: own.at[at], *more)
+        return Scatter(place, copies, gives if i else gives_down, i * scatter_slots, None, lambda at: own.at[at], *more)
+
+    def projection(i, *more):
+        give = lambda four: a_grad.at[i, 1 - c, four]
+        own = lambda at: a_grad.at[i, c, at]
+        return Scatter(place, copies, copies, (3 + i) * scatter_slots, give, own, *more)
 
     down, left, right = (scatter(i, *bufs[7 * i : 7 * i + 7]) for i in range(3))
-    proj = Scatter(
-        place, copies, copies, 3 * scatter_slots, lambda four: a_grad.at[1 - c, four],
-        lambda at: a_grad.at[c, at], *bufs[21:],
-    )
-    chunks = Steps([(m, planes) for m in (down, left, right, proj) for planes in far_near], scatter_stages)
+    projs = [projection(i, *bufs[21 + 6 * i : 27 + 6 * i]) for i in range(2)]
+    early, late = projs
     planes = (3, 2, 1, 0)
     hops = ((place.sib, 0), (place.xn, 1), (place.yn, 2))
 
@@ -810,9 +879,9 @@
 
     tile = 256
 
-    def feed_forward(give_d, give_g, act_v, db, ht, w_gu, w_dn, gate_v, up_v, att_v, norm_v, inv_v, w_out):
-        down.give = lambda four: give_d.at[four]
-        left.give = right.give = lambda four: give_g.at[four]
+    def feed_forward(given, act_v, db, ht, w_gu, w_dn, gate_v, up_v, att_v, norm_v, inv_v, w_out):
+        for i, m in enumerate((down, left, right)):
+            m.give = lambda four, i=i: given.at[i % 2, four]
         load = lambda i, src, dst: pltpu.make_async_copy(src, dst, in_sem.at[i])
         loads = [
             load(0, d_branch, db), load(1, hid_t, ht), load(2, d_hid, resid), load(3, att, att_v),
@@ -842,18 +911,33 @@
         own_d = bufs[0]
         for i, z in enumerate(planes):
             act_load(i, z).wait()
-            term = dot(act_v[i % 2].T, db[...]).astype(low).reshape(4, 2, d_shard_rows(width, ff), width)
+            term = dot(act_v[i % 2].T, db[...]).astype(low).reshape(4, 2, 2, rows_chip, width)
             if i < 2:
                 act_load(i + 2, planes[i + 2]).start()
             four = pl.ds(place.plane(z) * 4, 4)
-            own_d[four] = jnp.where(first, term[:, 0], term[:, 1])
-            give_d[four] = jnp.where(first, term[:, 1], term[:, 0])
+            mine = jnp.where(first, term[:, 0], term[:, 1])
+            other = jnp.where(first, term[:, 1], term[:, 0])
+            for j in range(2):
+                cols = slice(j * width, (j + 1) * width)
+                bufs[0][four, :, cols] = mine[:, j]
+                given[0, four, :, cols] = other[:, j]
+            if i == 0:
+                place.meet()
             down.begin(z)
-        chunks(0)
+        down.first()
+        down.rest()
         for copy in loads[1:3]:
             copy.wait()
 
-        def tiles(begin, own_g):
+        def between(i, todo):
+            for at, *work in todo:
+
+                @pl.when(i == at)
+                def _(work=work):
+                    for step in work:
+                        step()
+
+        def tiles(begin, own_g, give_g, todo):
             @pl.loop(begin, begin + half_g // tile)
             def _(j):
                 slot = j % 2
@@ -876,16 +960,15 @@
                 own_g[:, :, cols] = mine.reshape(16, rows_chip, tile)
                 other = dot(ht[...], jnp.where(first, d_up, d_gate)).astype(low)
                 give_g[:, :, cols] = other.reshape(16, rows_chip, tile)
-
-        tiles(0, bufs[7])
+                between(j - begin, todo)
+
+        tiles(0, bufs[7], given.at[1], [(5, down.diags)])
         for z in planes:
             left.begin(z)
-        chunks(1)
-        gives.drain(place.sib)
-        tiles(half_g // tile, bufs[14])
+        gives_down.drain(place.sib)
+        tiles(half_g // tile, bufs[14], given.at[0], [(2, down.relays, left.first, left.rest), (5, down.odd)])
         for z in planes:
             right.begin(z)
-        chunks(2)
         for copy in loads[3:]:
             copy.wait()
         grad = resid[...]
@@ -898,13 +981,18 @@
         resid[...] = back
         d_one = back.astype(low)
         d_att[...] = dot(d_one, w_out[...].reshape(width, width), ((1,), (1,))).astype(low)
-        a_grad[1, :, :, width:] = dot(att_v[...].T, d_one).astype(low).reshape(16, rows_chip, width)
+        grad_out = dot(att_v[...].T, d_one).astype(low).reshape(16, rows_chip, width)
+        for i in range(2):
+            a_grad[i, 1, :, :, part:] = grad_out[:, :, i * part : (i + 1) * part]
+        left.diags()
+        right.first()
+        right.rest()
         gives.drain(place.sib)
 
     block = lambda *dims: pltpu.VMEM(dims, low)
     block_wide = lambda *dims: pltpu.VMEM(dims, wide)
     pl.run_scoped(
-        feed_forward, block(*bufs[0].shape), block(*bufs[7].shape), block(2, tok_rows, width),
+        feed_forward, block(2, *bufs[0].shape), block(2, tok_rows, width),
         block(tok_rows, width), block(width, tok_rows), block(2, 2, 16, rows_chip, tile), block(2, tile, width),
         block(2, tok_rows, tile), block(2, tok_rows, tile), block(tok_rows, width), block_wide(tok_rows, width),
         block_wide(tok_rows, lane_width), block(16, rows_chip, width),
@@ -912,141 +1000,161 @@
 
     half = lambda side: pl.ds(pl.multiple_of(side * tok_rows, tok_rows), tok_rows)
 
-    def attention_part(dq, dkv_own, dkv_out):
+    def attention_part(dq, dkv_own, dkv_out, x_t, d_k, d_v):
+        slots = dkv_own.shape[0]
+
         def send_dkv(pair):
             return pltpu.make_async_remote_copy(
                 src_ref=dkv_out.at[pair], dst_ref=dkv_in.at[pair], send_sem=pair_sem.at[0, pair],
                 recv_sem=pair_sem.at[1, pair], device_id=place.sib, device_id_type=MESH,
             )
 
-        def attention(q_v, k_v, v_v, span_v, att_v, dk_sum, dv_sum):
+        def project(i):
+            for pair in range(i * pairs // 2, (i + 1) * pairs // 2):
+                send_dkv(pair).wait_recv()
+                at = slice(pair * lane_width, (pair + 1) * lane_width)
+                for j, dst in enumerate((d_k, d_v)):
+                    dst[:, at] = (dkv_own[pair % slots, j] + dkv_in[pair, j].astype(wide)).astype(low)
+            cols = slice(i * part, (i + 1) * part)
+            for side, at, src in ((0, 0, dq), (0, part, d_k), (1, 0, d_v)):
+                term = dot(x_t[...], src[:, cols]).astype(low)
+                a_grad[i, side, :, :, at : at + part] = term.reshape(16, rows_chip, part)
+            for z in planes:
+                projs[i].begin(z)
+
+        def attention(q_v, k_v, v_v, span_v, att_v, x, dk_sum, dv_sum):
             loads = [
                 pltpu.make_async_copy(src, dst, in_sem.at[i])
-                for i, (src, dst) in enumerate(((q, q_v), (k, k_v), (v, v_v), (span, span_v), (att, att_v)))
+                for i, (src, dst) in enumerate(((q, q_v), (k, k_v), (v, v_v), (span, span_v), (att, att_v), (tokens, x)))
             ]
             for copy in loads:
                 copy.start()
             for copy in loads:
                 copy.wait()
-
-            @pl.loop(0, pairs)
-            def _(pair):
-                attend_back_pair(pair, heads, q_v, k_v, v_v, span_v, lse, att_v, d_att, dq, dk_sum, dv_sum)
-                for i, part in enumerate((dk_sum, dv_sum)):
-                    dkv_own[pair, i] = part[half(c), :]
-                    dkv_out[pair, i] = part[half(1 - c), :].astype(low)
-                send_dkv(pair).start()
-                for i in range(3):
-
-                    @pl.when(pair == 2 * i)
-                    def _(i=i):
-                        chunks(3 + i)
-                        combine(i)
-                        if i < 2:
-                            exchange(i + 1)
-                        else:
-                            spread()
+            x_t[...] = x[...].T
+
+            def heads_back(begin, end, todo):
+                @pl.loop(begin, end)
+                def _(pair):
+                    attend_back_pair(pair, heads, q_v, k_v, v_v, span_v, lse, att_v, d_att, dq, dk_sum, dv_sum)
+                    for i, side in enumerate((dk_sum, dv_sum)):
+                        dkv_own[lax.rem(pair, slots), i] = side[half(c), :]
+                        dkv_out[pair, i] = side[half(1 - c), :].astype(low)
+                    send_dkv(pair).start()
+                    for at, *work in todo:
+
+                        @pl.when(pair == at)
+                        def _(at=at, work=work):
+                            for step in work:
+                                step()
+                            if at % 2:
+                                combine(at // 2)
+                                if at < 5:
+                                    exchange(at // 2 + 1)
+                                else:
+                                    spread()
+
+            heads_back(0, 4, [(0, down.even), (1, left.odd), (2, left.relays, right.diags), (3, right.odd)])
+            project(0)
+            heads_back(4, pairs, [(4, left.even, early.first, early.rest), (5, right.relays)])
+            project(1)
 
         key_rows = k.shape[0]
         pl.run_scoped(
             attention, block(*q.shape), block(*k.shape), block(*v.shape), block_wide(*span.shape), block(*att.shape),
-            block_wide(key_rows, lane_width), block_wide(key_rows, lane_width),
+            block(tok_rows, width), block_wide(key_rows, lane_width), block_wide(key_rows, lane_width),
         )
 
-        def finish(w_left, w_right, x, d_k, d_v):
+        def finish(w_left, w_right):
             loads = [
-                pltpu.make_async_copy(src, dst, in_sem.at[i])
-                for i, (src, dst) in enumerate(
-                    (
-                        (tokens, x),
-                        (a_full.at[0, :, :, : 2 * width], w_left),
-                        (a_full.at[1, :, :, :width], w_right),
-                    )
-                )
+                pltpu.make_async_copy(a_full.at[0, :, :, : 2 * width], w_left, in_sem.at[0]),
+                pltpu.make_async_copy(a_full.at[1, :, :, :width], w_right, in_sem.at[1]),
             ]
             for copy in loads:
                 copy.start()
-            for pair in range(pairs):
-                send_dkv(pair).wait_recv()
-                at = slice(pair * lane_width, (pair + 1) * lane_width)
-                d_k[:, at] = (dkv_own[pair, 0] + dkv_in[pair, 0].astype(wide)).astype(low)
-                d_v[:, at] = (dkv_own[pair, 1] + dkv_in[pair, 1].astype(wide)).astype(low)
-            loads[0].wait()
-            x_t = x[...].T
-            size = width // 2
-            for side, at, src in ((0, 0, dq), (0, width, d_k), (1, 0, d_v)):
-                for part in range(2):
-                    term = dot(x_t, src[:, part * size : (part + 1) * size]).astype(low)
-                    here = at + part * size
-                    a_grad[side, :, :, here : here + size] = term.reshape(16, rows_chip, size)
-            for z in planes:
-                proj.begin(z)
-            for copy in loads[1:]:
+            for copy in loads:
                 copy.wait()
             w_q = w_left[:, :, :width].reshape(width, width)
             total = resid[...] + dot(dq[...], w_q, ((1,), (1,)))
-            chunks(6)
+            early.diags()
+            late.first()
+            late.rest()
             w_k = w_left[:, :, width:].reshape(width, width)
             total += dot(d_k[...], w_k, ((1,), (1,)))
+            early.relays()
+            late.diags()
+            early.odd()
+            right.even()
             total += dot(d_v[...], w_right[...].reshape(width, width), ((1,), (1,)))
             d_tokens[...] = total.astype(low)
-
-        pl.run_scoped(
-            finish, block(16, rows_chip, 2 * width), block(16, rows_chip, width), block(tok_rows, width),
-            block(tok_rows, width), block(tok_rows, width),
-        )
+            late.relays()
+            early.even()
+            late.odd()
+
+        pl.run_scoped(finish, block(16, rows_chip, 2 * width), block(16, rows_chip, width))
 
         @pl.loop(0, pairs)
         def _(pair):
             send_dkv(pair).wait_send()
 
     pl.run_scoped(
-        attention_part, block(tok_rows, width), block_wide(pairs, 2, tok_rows, lane_width),
-        block(pairs, 2, tok_rows, lane_width),
+        attention_part, block(tok_rows, width), block_wide(4, 2, tok_rows, lane_width),
+        block(pairs, 2, tok_rows, lane_width), block(width, tok_rows), block(tok_rows, width), block(tok_rows, width),
     )
     for z in (1, 2, 3):
         last.got(small_buf.at[6 + z], 2 + z, place.zn[z])
-    small_out[...] = (small_buf[3] + small_buf[7]) + (small_buf[8] + small_buf[9])
+    sums = (small_buf[3] + small_buf[7]) + (small_buf[8] + small_buf[9])
+    share = width // 32
+    mine = (lax.axis_index("rows") * 2 + c) * share
+    tail[0:8, :] = pltpu.roll(sums[:8], lax.rem(width - mine, width), 1)[:, :lane_width]
+    squares = jnp.sum(sums[:8], 1, keepdims=True) / (sums[8:9, 0:1] * width)
+    at = lambda axis: lax.broadcasted_iota(jnp.int32, (8, lane_width), axis)
+    stats = jnp.where(at(0) == at(1) + 4, jnp.broadcast_to(jnp.sqrt(squares), (8, lane_width)), 0.0)
+    tail[8:16, :] = jnp.broadcast_to(column_sum(stats), (8, lane_width))
     mine, theirs = pl.ds(pl.multiple_of(24 * c, 8), 24), pl.ds(pl.multiple_of(24 - 24 * c, 8), 24)
-    down_out[...] = down.total()
-    chunks(7)
-    g_sum[0] = left.total()
-    last.put(g_sum.at[0, theirs], g_fin.at[0], 6, place.sib, lambda: g_fin.at[0])
-    chunks(8)
-    chunks(9)
-    g_sum[1] = right.total()
-    last.put(g_sum.at[1, theirs], g_fin.at[1], 8, place.sib, lambda: g_fin.at[1])
-    chunks(10)
-    for i, slot in ((0, 6), (1, 8)):
-        last.got(g_fin.at[i], slot, place.sib)
+    total = down.total()
+    down_out[:rows_chip] = total[:, :width]
+    down_out[rows_chip:] = total[:, width:]
+
+    def swap(i, m, total, other, slot):
+        total[i] = m.total()
+        last.put(total.at[i, theirs], other.at[i], slot, place.sib, lambda: other.at[i])
+
+    swap(0, left, g_sum, g_fin, 6)
+    swap(1, right, g_sum, g_fin, 7)
+    swap(0, early, a_sum, a_fin, 8)
+    late.even()
+    for i in range(2):
+        last.got(g_fin.at[i], 6 + i, place.sib)
         own, other = g_sum[i, mine], g_fin[i]
         gu_out[:, i * half_g : (i + 1) * half_g] = jnp.where(first, own, other)
         gu_out[:, (i + 2) * half_g : (i + 3) * half_g] = jnp.where(first, other, own)
-    a_sum[...] = proj.total()
-    last.put(a_sum.at[theirs], a_fin, 7, place.sib, lambda: a_fin)
-    last.got(a_fin, 7, place.sib)
-    qkv_out[:, : 2 * width] = jnp.where(first, a_sum[mine], a_fin[...])
-    side = jnp.where(first, a_fin[...], a_sum[mine])
-    qkv_out[:, 2 * width :] = side[:, :width]
-    wout_out[...] = side[:, width:]
+    swap(1, late, a_sum, a_fin, 9)
+    for i in range(2):
+        last.got(a_fin.at[i], 8 + i, place.sib)
+        own, other = a_sum[i, mine], a_fin[i]
+        qk, vo = jnp.where(first, own, other), jnp.where(first, other, own)
+        for j, term in enumerate((qk[:, :part], qk[:, part:], vo[:, :part])):
+            at = j * width + i * part
+            qkv_out[:, at : at + part] = term
+        wout_out[:, i * part : (i + 1) * part] = vo[:, part:]
     copies.drain(place.sib)
     last.drain(place.sib)
 
 
-def d_shard_rows(width, ff):
-    return ff // 32
-
-
-def back(heads, tokens, q, k, v, span, att, hid_t, norm, inv, gate, up, act, d_hid, d_branch, a_full, g_full, d_full, lse, vectors, small):
+def back(
+    heads, tokens, q, k, v, span, att, hid_t, norm, inv, gate, up, act, d_hid, d_branch, a_full, g_full, d_full,
+    lse, vectors, small,
+):
     low, wide = jnp.bfloat16, jnp.float32
     tok_rows, width = tokens.shape
     ff = gate.shape[1]
-    half_g, half_a = ff // 2, 2 * width
+    half_g = ff // 2
     pairs = heads // 2
-    d_rows = d_shard_rows(width, ff)
+    d_rows = ff // 32
     bufs = []
-    for i, (rows, half) in enumerate(((d_rows, width), (rows_chip, half_g), (rows_chip, half_g), (rows_chip, half_a))):
-        bufs += [pltpu.VMEM((count, rows, half), low) for count in (16, 16, 2, 2, 4, 4, 3)[i == 3 :]]
+    for i, cols in enumerate((2 * width, half_g, half_g, width, width)):
+        bufs += [pltpu.VMEM((count, rows_chip, cols), low) for count in (16, 16, 2, 2, 4, 4, 3)[i >= 3 :]]
     vmem, hbm = pl.BlockSpec(memory_space=pltpu.VMEM), pl.BlockSpec(memory_space=pl.ANY)
     dma = lambda *shape: pltpu.SemaphoreType.DMA(shape)
     shape = jax.ShapeDtypeStruct
@@ -1054,25 +1162,25 @@
         lambda *refs: back_kernel(heads, *refs),
         out_shape=(
             shape((tok_rows, width), low), shape((24, 3 * width), wide), shape((24, width), wide),
-            shape((24, 2 * ff), wide), shape((d_rows, width), wide), shape(small.shape, wide),
+            shape((24, 2 * ff), wide), shape((d_rows, width), wide), shape((16, lane_width), wide),
         ),
         in_specs=[hbm] * 17 + [vmem] * 3,
         out_specs=(vmem,) * 6,
         scratch_shapes=bufs
         + [
-            pltpu.VMEM((2, 16, rows_chip, half_a), low),
+            pltpu.VMEM((2, 2, 16, rows_chip, width), low),
             pltpu.VMEM((pairs, 2, tok_rows, lane_width), low),
             pltpu.VMEM((tok_rows, width), wide),
             pltpu.VMEM((tok_rows, width), low),
             pltpu.VMEM((2, rows_chip, half_g), wide),
-            pltpu.VMEM((rows_chip, half_a), wide),
+            pltpu.VMEM((2, rows_chip, width), wide),
             pltpu.VMEM((2, 24, half_g), wide),
-            pltpu.VMEM((24, half_a), wide),
+            pltpu.VMEM((2, 24, width), wide),
             pltpu.VMEM((10,) + small.shape, wide),
-            dma(4 * scatter_slots),
-            dma(4 * scatter_slots),
+            dma(5 * scatter_slots),
+            dma(5 * scatter_slots),
             dma(2, pairs),
-            dma(2, 9),
+            dma(2, 10),
             dma(9),
             dma(4, 2),
         ],
@@ -1081,6 +1189,30 @@
         ),
         name="backward_and_sums",
     )(tokens, q, k, v, span, att, hid_t, norm, inv, gate, up, act, d_hid, d_branch, a_full, g_full, d_full, lse, vectors, small)
+
+
+def close_kernel(share, *refs):
+    parts, tail, outs = refs[:6], refs[6], refs[7:]
+    for part, out in zip(parts, outs):
+        out[...] = part[...]
+    for i, out in enumerate(outs[6:10]):
+        out[...] = tail[i : i + 1, :share]
+    outs[10][...] = tail[8:9, :4]
+
+
+def close(share, *parts):
+    vmem = pl.BlockSpec(memory_space=pltpu.VMEM)
+    wide = jnp.float32
+    return pl.pallas_call(
+        lambda *refs: close_kernel(share, *refs),
+        out_shape=tuple(jax.ShapeDtypeStruct(part.shape, part.dtype) for part in parts[:6])
+        + (jax.ShapeDtypeStruct((1, share), wide),) * 4
+        + (jax.ShapeDtypeStruct((1, 4), wide),),
+        in_specs=[vmem] * 7,
+        out_specs=(vmem,) * 11,
+        compiler_params=pltpu.CompilerParams(vmem_limit_bytes=62 * 2**20),
+        name="results",
+    )(*parts)
 
 
 def window(cells, width):
@@ -1127,21 +1259,29 @@
     return jnp.stack([left, right]), jnp.stack([w_gate_up[:, :ff], w_gate_up[:, ff:]])
 
 
-def on_grid(tokens, a_shard, g_shard, w_down, span, valid, out_grad):
-    spare = ((0, 0), (0, 32 - a_shard.shape[1]), (0, 0))
+def on_grid(tokens, labels, w_qkv, w_out, w_gate_up, w_down, norms, out_grad):
+    width = tokens.shape[1]
     (
-        a_full, g_full, d_full, q, k, v, att, hid_t, norm, inv, gate, up, act, output, d_hid, d_branch, lse, vectors, small,
-    ) = fore(HEADS, tokens, jnp.pad(a_shard, spare), jnp.pad(g_shard, spare), w_down, valid, span, out_grad)
-    d_full = d_full.reshape(-1, tokens.shape[1])
-    return output, *back(
-        HEADS, tokens, q, k, v, span, att, hid_t, norm, inv, gate, up, act, d_hid, d_branch, a_full, g_full, d_full, lse,
-        vectors, small,
+        a_full, g_full, d_full, q, k, v, att, hid_t, norm, inv, gate, up, act, output, d_hid, d_branch, span,
+        lse, vectors, small,
+    ) = fore(HEADS, tokens, labels, w_qkv, w_out, w_gate_up, w_down, jnp.stack(norms), out_grad)
+    parts = back(
+        HEADS, tokens, q, k, v, span, att, hid_t, norm, inv, gate, up, act, d_hid, d_branch, a_full, g_full,
+        d_full.reshape(-1, width), lse, vectors, small,
     )
-
-
-def on_any(tokens, a_shard, g_shard, w_down, span, valid, out_grad):
+    *parts, one, two, three, four, stats = close(norms[0].shape[0], output, *parts)
+    rows = [row.reshape(-1) for row in (one, two, three, four)]
+    return *parts, rows, stats.reshape(-1)
+
+
+def on_any(tokens, labels, w_qkv, w_out, w_gate_up, w_down, norms, out_grad):
     both = ("rows", "blk")
     tok_rows, width = tokens.shape
+    first = lax.axis_index("blk") * tok_rows
+    span = key_spans(labels[0], first, tok_rows)
+    here = lax.dynamic_slice_in_dim(labels[0], first, tok_rows, 0)
+    valid = (here != labels.shape[1]).astype(jnp.float32)[:, None]
+    a_shard, g_shard = packed_shards(w_qkv, w_out, *norms[:2], w_gate_up, *norms[2:])
     low, wide = jnp.bfloat16, jnp.float32
     a_full = lax.all_gather(a_shard, both, axis=1, tiled=True)
     w_gu = lax.all_gather(g_shard, both, axis=1, tiled=True)
@@ -1165,32 +1305,26 @@
     d_tokens = d_resid_one + times_transposed(d_qk, w_qk) + times_transposed(d_v, w_v)
     share = lambda g, axis: lax.psum_scatter(g.astype(wide), both, scatter_dimension=axis, tiled=True)
     gate, up = share(g_grad, 1)
+    small = lax.psum(small, both)
+    size = norms[0].shape[0]
+    rows = lax.dynamic_slice_in_dim(small[:4], lax.axis_index(both) * size, size, 1)
+    stats = jnp.sqrt(jnp.sum(small[4:8], 1) / (small[8, 0] * width))
     return (
         output, d_tokens.astype(low), share(grad_qkv, 0), share(grad_out, 0), jnp.concatenate([gate, up], 1),
-        share(d_grad, 0), lax.psum(small, both),
+        share(d_grad, 0), rows, stats,
     )
 
 
 def body(
     tokens, segments, w_qkv, w_out, ln1_gain, ln1_bias, w_gate_up, w_down, ln2_gain, ln2_bias, out_grad,
 ):
-    inputs, labels = tokens[0], segments[0]
-    tok_rows, width = inputs.shape
-    both = ("rows", "blk")
-    first = lax.axis_index("blk") * tok_rows
-    span = key_spans(labels, first, tok_rows)
-    here = lax.dynamic_slice_in_dim(labels, first, tok_rows, 0)
-    valid = (here != labels.shape[0]).astype(jnp.float32)[:, None]
-    a_shard, g_shard = packed_shards(w_qkv, w_out, ln1_gain, ln1_bias, w_gate_up, ln2_gain, ln2_bias)
     run = on_grid if on_chip_grid() else on_any
-    output, d_tokens, *parts, small = run(inputs, a_shard, g_shard, w_down, span, valid, out_grad[0])
-    share = width // lax.axis_size(both)
-    mine = lax.axis_index(both) * share
-    rows = lax.dynamic_slice_in_dim(small[:4], mine, share, 1)
-    stats = jnp.sqrt(jnp.sum(small[4:8], 1) / (small[8, 0] * width))
+    norms = (ln1_gain, ln1_bias, ln2_gain, ln2_bias)
+    output, d_tokens, qkv, wout, gate_up, down, rows, stats = run(
+        tokens[0], segments, w_qkv, w_out, w_gate_up, w_down, norms, out_grad[0]
+    )
     return (
-        output[None], d_tokens[None], parts[0], parts[1], rows[0], rows[1],
-        parts[2], parts[3], rows[2], rows[3], stats,
+        output[None], d_tokens[None], qkv, wout, rows[0], rows[1], gate_up, down, rows[2], rows[3], stats,
     )
 
 

time: 234 us -> 205 us (0.88)
  Pallas kernels: 214 us -> 203 us
  local copies, waits for them, and re-layouts: 10.2 us -> 0 us
  other arithmetic: 7.95 us -> 1.28 us
    pallas_call x1, Pallas kernels: 113 us -> 93.1 us  [back(): pl.pallas_call(lambda *refs: back_kernel(heads, *refs), out_shape=(shape(...]
    pallas_call x1, Pallas kernels: 101 us -> 106 us  [fore(): pl.pallas_call(lambda *refs: fore_kernel(heads, *refs), out_shape=tuple((...]
    unnamed x20 -> x0, local copies, waits for them, and re-layouts: 4.64 us -> none
    pallas_call x0 -> x1, Pallas kernels: none -> 3.34 us  [close(): pl.pallas_call(lambda *refs: close_kernel(share, *refs), out_shape=tuple(...]
    slice x3 -> x0, local copies, waits for them, and re-layouts: 2.97 us -> none  [the longest x1 1.31 us: body(): stats = jnp.sqrt(jnp.sum(small[4:8], 1) / (small[8, 0] * width))]
where the time goes in v5:
time: 205 us
  Pallas kernels  203 us (99%)
    pallas_call x1, Pallas kernels, fore(): pl.pallas_call(lambda *refs: fore_kernel(heads, *refs), out_shape=tuple((...  106 us
    pallas_call x1, Pallas kernels, back(): pl.pallas_call(lambda *refs: back_kernel(heads, *refs), out_shape=(shape(...  93.1 us

profile of v5, /device:TPU:0, one launch (start us, length us, event | category | flops | bytes accessed | tf_op | source)
XLA Modules:
  0.0 204.6 jit_solution(6355742907649684512)
XLA Ops:
  0.6 1.3 pad_maximum_fusion.refs_6_
  1.9 106.1 %gather_and_forward.1 = (bf16[2,16,48,1664]{3,2,1,0:T(8,128)(2,1)}, bf16[2,16,48,3072]{3,2,1,0:T(8,128)(2,1)}, bf16[16,2,96,768]{3,2,1,0:T(8,128)(2,1)}, bf16[51...) custom-call(bf16[512,768]{1,0:T(8,128)(2,1)} %bitcast.15, ...), custom_call_target="tpu_custom_call" | custom-call | tf_op jit(solution)/shard_map/gather_and_forward/pallas_call | solution.py:812
  108.0 93.1 %backward_and_sums.1 = (bf16[512,768]{1,0:T(8,128)(2,1)}, f32[24,2304]{1,0:T(8,128)}, f32[24,768]{1,0:T(8,128)}, f32[24,6144]{1,0:T(8,128)}, f32[96,768]{1,0:T(8,128)}, /*index=5*/f32[16,128]{1,0:T(8,128)}) custom-call(bf16[512,768]{1,0:T(8,128)(2,1)} %bitcast.16, bf16[512,768]{1,0:T(8,128)(2,1)} %get-tuple-element.49.refs_1_, ...), custom_call_target="tpu_custom_call" | custom-call | tf_op jit(solution)/shard_map/backward_and_sums/pallas_call | solution.py:1161
  201.2 3.3 %results.1 = (bf16[512,768]{1,0:T(8,128)(2,1)}, bf16[512,768]{1,0:T(8,128)(2,1)}, f32[24,2304]{1,0:T(8,128)}, f32[24,768]{1,0:T(8,128)}, f32[24,6144]{1,0:T(8,12...) custom-call(bf16[512,768]{1,0:T(8,128)(2,1)} %get-tuple-element.48.r, ...), custom_call_target="tpu_custom_call" | custom-call | tf_op jit(solution)/shard_map/results/pallas_call | solution.py:1206

commit v6 on v5

--- a/solution.py
+++ b/solution.py
@@ -61,43 +61,43 @@
 
 class Copies:
     def __init__(self, send, recv):
-        self.send, self.recv, self.open = send, recv, []
-
-    def of(self, src, dst, slot, peer):
+        self.send, self.recv = send, recv
+
+    def of(self, src, dst, pool, slot, peer):
         return pltpu.make_async_remote_copy(
-            src_ref=src, dst_ref=dst, send_sem=self.send.at[slot], recv_sem=self.recv.at[slot],
+            src_ref=src, dst_ref=dst, send_sem=self.send.at[pool], recv_sem=self.recv.at[slot],
             device_id=peer, device_id_type=MESH,
         )
 
-    def put(self, src, dst, slot, peer, like=None):
-        self.of(src, dst, slot, peer).start()
-        self.open.append((like or (lambda: dst), slot))
+    def put(self, src, dst, pool, slot, peer):
+        self.of(src, dst, pool, slot, peer).start()
 
     def got(self, dst, slot, peer):
-        self.of(dst, dst, slot, peer).wait_recv()
-
-    def drain(self, peer):
-        for like, slot in self.open:
-            self.of(like(), like(), slot, peer).wait_send()
-        self.open = []
+        self.of(dst, dst, 0, slot, peer).wait_recv()
+
+    def sent(self, all_of_pool, pool, peer):
+        self.of(all_of_pool, all_of_pool, pool, 0, peer).wait_send()
 
 
 class Gather:
-    def __init__(self, place, copies, base, out):
-        self.p, self.cp, self.base, self.out = place, copies, base, out
-
-    def slot(self, kind, k, j="o"):
-        start = {"z": -1, "x": 3, "y": 7, "d": 11, "s": 15}[kind]
-        return self.base + start + (4 * k + "oxyd".index(j) if kind == "s" else k)
+    def __init__(self, place, copies, i, side):
+        self.p, self.cp, self.side = place, copies, side
+        self.base, self.pool = i * gather_slots, 2 * i
+
+    def slot(self, kind, k=0):
+        return self.base + {"z": -1, "x": 3, "y": 7, "d": 11, "s": 15}[kind] + k
+
+    def out(self, half, r):
+        return self.side(half).at[r]
 
     def block(self, k, j):
         return self.out(self.p.c, self.p.at(k, j))
 
     def send(self, src, dst, slot, peer):
-        self.cp.put(src, dst, slot, peer, lambda: self.out(0, 0))
+        self.cp.put(src, dst, self.pool, slot, peer)
 
     def push(self, src, k, j):
-        self.send(src, self.block(k, j), self.slot("s", k, j), self.p.sib)
+        self.cp.put(src, self.block(k, j), self.pool + 1, self.slot("s"), self.p.sib)
 
     def to_z(self):
         for k in (1, 2):
@@ -163,15 +163,19 @@
         self.push(block, k, "d")
 
     def from_sib(self):
-        for k in range(4):
-            for j in "oxyd":
-                block = self.out(1 - self.p.c, self.p.at(k, j))
-                self.cp.got(block, self.slot("s", k, j), self.p.sib)
+        self.cp.got(self.side(1 - self.p.c), self.slot("s"), self.p.sib)
+
+    def drain(self):
+        side = self.side(self.p.c)
+        self.cp.sent(side.at[pl.ds(0, 15)], self.pool, self.p.sib)
+        self.cp.sent(side, self.pool + 1, self.p.sib)
 
 
 class Scatter:
-    def __init__(self, place, copies, gives, base, give, own, sib, rly, dia, xin, yin, zin):
-        self.p, self.cp, self.gives, self.base, self.give, self.own = place, copies, gives, base, give, own
+    def __init__(self, place, copies, i, give, own, sib, rly, dia, xin, yin, zin, straight=False, flat=False):
+        self.p, self.cp, self.give, self.own = place, copies, give, own
+        self.base, self.pool = i * scatter_slots, 2 * i
+        self.straight, self.flat = straight, flat
         self.sib, self.rly, self.dia, self.xin, self.yin, self.zin = sib, rly, dia, xin, yin, zin
 
     def slot(self, kind, k):
@@ -182,13 +186,19 @@
 
     def begin(self, k):
         four = self.four(k)
-        self.gives.put(self.give(four), self.sib.at[four], self.slot("s", k), self.p.sib, lambda: self.sib.at[pl.ds(0, 4)])
+        self.cp.put(self.give(four), self.sib.at[four], self.pool + 1, self.slot("s", k), self.p.sib)
+
+    def given(self):
+        self.cp.sent(self.sib, self.pool + 1, self.p.sib)
+
+    def drain(self):
+        self.cp.sent(self.sib.at[pl.ds(0, 15)], self.pool, self.p.sib)
 
     def to_x(self, own, k):
-        self.cp.put(own, self.xin.at[k], self.slot("x", k), self.p.xn, lambda: self.xin.at[k])
+        self.cp.put(own, self.xin.at[k], self.pool, self.slot("x", k), self.p.xn)
 
     def to_y(self, own, k):
-        self.cp.put(own, self.yin.at[k], self.slot("y", k), self.p.yn, lambda: self.yin.at[k])
+        self.cp.put(own, self.yin.at[k], self.pool, self.slot("y", k), self.p.yn)
 
     def both(self, k, j, *more):
         at = self.p.at(k, j)
@@ -202,33 +212,36 @@
     def pair(self, k):
         four = self.four(k)
         self.cp.got(self.sib.at[four], self.slot("s", k), self.p.sib)
-        if k % 2:
+        if self.flat:
+            self.to_relay(self.both(k, "d"), k)
+        elif k % 2:
             i = k // 2
-            dia = lambda: self.dia.at[i]
-            self.cp.put(self.both(k, "d"), dia(), self.slot("d", 2 * i), self.p.zn[1], dia)
-        if k != 2:
+            self.cp.put(self.both(k, "d"), self.dia.at[i], self.pool, self.slot("d", 2 * i), self.p.zn[1])
+        odd = k % 2 and not self.flat
+        if odd or k < 2:
             self.to_x(self.both(k, "x"), k)
-        if k != 0:
+        if odd or k >= 2:
             self.to_y(self.both(k, "y"), k)
 
+    def relay_at(self, k):
+        return (self.dia if k % 2 else self.rly).at[k // 2]
+
+    def to_relay(self, own, k):
+        slot = self.slot("d", k - 1) if k % 2 else self.slot("r", k)
+        self.cp.put(own, self.relay_at(k), self.pool, slot, self.p.xn if k < 2 else self.p.yn)
+
     def diag(self, k):
-        if k % 2:
-            return
         i = k // 2
         self.cp.got(self.dia.at[i], self.slot("d", k), self.p.zn[1])
-        own = self.both(k, "d", self.dia.at[i])
-        peer = self.p.xn if k == 0 else self.p.yn
-        self.cp.put(own, self.rly.at[i], self.slot("r", k), peer, lambda: self.rly.at[i])
+        self.to_relay(self.both(k, "d", self.dia.at[i]), k)
 
     def relay(self, k):
-        if k % 2:
-            return
-        i = k // 2
-        self.cp.got(self.rly.at[i], self.slot("r", k), self.p.xn)
-        if k == 0:
-            self.to_y(self.both(k, "y", self.rly.at[i]), k)
+        rly = self.relay_at(k)
+        self.cp.got(rly, self.slot("d", k - 1) if k % 2 else self.slot("r", k), self.p.xn)
+        if k < 2:
+            self.to_y(self.both(k, "y", rly), k)
         else:
-            self.to_x(self.both(k, "x", self.rly.at[i]), k)
+            self.to_x(self.both(k, "x", rly), k)
 
     def plane(self, k):
         p = self.p
@@ -241,11 +254,13 @@
             self.xin[k].astype(wide) + self.yin[k].astype(wide)
         )
         own[...] = total.astype(jnp.bfloat16)
-        if k % 2:
+        if self.straight and k:
+            self.to_z(own, k, k)
+        elif k % 2:
             self.to_z(own, k, 1)
 
     def to_z(self, own, k, step):
-        self.cp.put(own, self.zin.at[k - 1], self.slot("z", k), self.p.zn[step], lambda: self.zin.at[k - 1])
+        self.cp.put(own, self.zin.at[k - 1], self.pool, self.slot("z", k), self.p.zn[step])
 
     def cross(self):
         self.cp.got(self.zin.at[2], self.slot("z", 3), self.p.zn[1])
@@ -264,28 +279,31 @@
         self.all("pair", 2, 0)
 
     def diags(self):
-        self.all("diag", 2, 0)
+        if not self.flat:
+            self.all("diag", 2, 0)
 
     def relays(self):
-        self.all("relay", 2, 0)
+        self.all("relay", *((3, 1, 2, 0) if self.flat else (2, 0)))
 
     def odd(self):
         self.all("plane", 3, 1)
 
     def even(self):
         self.all("plane", 2, 0)
-        self.cross()
+        if not self.straight:
+            self.cross()
 
     def total(self):
-        for k in (1, 2):
+        wide = jnp.float32
+        total = self.own(self.p.at(0, "o"))[...].astype(wide)
+        for k in (1, 2, 3) if self.straight else (1, 2):
             self.cp.got(self.zin.at[k - 1], self.slot("z", k), self.p.zn[k])
-        wide = jnp.float32
-        own = self.own(self.p.at(0, "o"))
-        return own[...].astype(wide) + (self.zin[0].astype(wide) + self.zin[1].astype(wide))
+            total = total + self.zin[k - 1].astype(wide)
+        return total
 
 
 rows_chip = 48
-gather_slots, scatter_slots = 31, 19
+gather_slots, scatter_slots = 16, 19
 
 
 def dot(left, right, dims=((1,), (0,))):
@@ -616,15 +634,15 @@
     swaps = Copies(pair_sem.at[0], pair_sem.at[1])
     place.meet()
     for i, (give, other) in enumerate(((a_give, a_pair), (g_give, g_pair))):
-        swaps.put(give, other, i, place.sib)
+        swaps.put(give, other, i, i, place.sib)
     copies = Copies(send, recv)
-    outs = [
-        lambda half, r: w_a.at[half, r],
-        lambda half, r: w_g.at[half, r, :, :half_g],
-        lambda half, r: w_g.at[half, r, :, half_g:],
-        lambda half, r: w_d.at[r, half],
+    sides = [
+        lambda half: w_a.at[half],
+        lambda half: w_g.at[half, :, :, :half_g],
+        lambda half: w_g.at[half, :, :, half_g:],
+        lambda half: w_d.at[:, half],
     ]
-    mats = [Gather(place, copies, i * gather_slots, out) for i, out in enumerate(outs)]
+    mats = [Gather(place, copies, i, side) for i, side in enumerate(sides)]
     first, second, third, fourth = mats
     me = place.at(0, "o")
 
@@ -676,9 +694,9 @@
     vectors[...] = part(0, 2 * width, lane_width).astype(wide).T[:8]
     x = tokens[...]
     k[half, :] = dot(x, part(0, width, width)).astype(low)
-    swaps.put(k.at[half], k.at[half], 2, place.sib, lambda: k.at[pl.ds(0, tok_rows)])
+    swaps.put(k.at[half], k.at[half], 2, 2, place.sib)
     v[half, :] = dot(x, part(1, 0, width)).astype(low)
-    swaps.put(v.at[half], v.at[half], 3, place.sib, lambda: v.at[pl.ds(0, tok_rows)])
+    swaps.put(v.at[half], v.at[half], 3, 3, place.sib)
     depth = width // heads
     q[...] = dot(x, part(0, 0, width)).astype(low) * depth**-0.5
     go(3)
@@ -740,13 +758,13 @@
 
     upto(second)
     second.from_sib()
+    go(1)
     save(w_g.at[:, :, :, :half_g], g_full.at[:, :, :, :half_g])
 
     @pl.loop(0, half_g // tile)
     def _(j):
         glu(j)
 
-    upto(third)
     third.from_sib()
     save(w_g.at[:, :, :, half_g:], g_full.at[:, :, :, half_g:])
     for src, dst in ((slope_gate, gate_out), (slope_up, up_out), (act, act_out)):
@@ -787,8 +805,10 @@
     save(d_branch, d_branch_out)
     for i, (src, dst) in enumerate(saved):
         pltpu.make_async_copy(src, dst, out_sem.at[i]).wait()
-    swaps.drain(place.sib)
-    copies.drain(place.sib)
+    for i, ref in enumerate((a_give, g_give, k.at[half], v.at[half])):
+        swaps.sent(ref, i, place.sib)
+    for m in mats:
+        m.drain()
 
 
 def fore(heads, tokens, labels, w_qkv, w_out, w_gu, d_shard, norms, out_grad):
@@ -822,7 +842,7 @@
             block_wide(keys, rows), block(rows, width), block_wide(rows, width), block(rows, width),
             block(width, rows), block_wide(rows, width), block_wide(rows, lane_width),
             block(rows, ff), block(rows, ff), block(rows, ff), block(rows, width), block_wide(rows, width),
-            block(rows, width), dma(2, 4), dma(4 * gather_slots), dma(4 * gather_slots), dma(1), dma(len(stored) + 4),
+            block(rows, width), dma(2, 4), dma(8), dma(4 * gather_slots), dma(1), dma(len(stored) + 4),
         ],
         compiler_params=pltpu.CompilerParams(
             collective_id=0, has_side_effects=True, vmem_limit_bytes=62 * 2**20
@@ -846,17 +866,16 @@
     bufs, rest = scratch[:33], scratch[33:]
     a_grad, dkv_in, resid, d_att, g_sum, a_sum, g_fin, a_fin, small_buf, send, recv, pair_sem, fin_sem, in_sem, tile_sem = rest
     copies = Copies(send, recv)
-    gives, gives_down = Copies(send, recv), Copies(send, recv)
     last = Copies(fin_sem.at[0], fin_sem.at[1])
     half_g, part = ff // 2, width // 2
 
     def scatter(i, own, *more):
-        return Scatter(place, copies, gives if i else gives_down, i * scatter_slots, None, lambda at: own.at[at], *more)
+        return Scatter(place, copies, i, None, lambda at: own.at[at], *more)
 
     def projection(i, *more):
         give = lambda four: a_grad.at[i, 1 - c, four]
         own = lambda at: a_grad.at[i, c, at]
-        return Scatter(place, copies, copies, (3 + i) * scatter_slots, give, own, *more)
+        return Scatter(place, copies, 3 + i, give, own, *more, straight=i == 1)
 
     down, left, right = (scatter(i, *bufs[7 * i : 7 * i + 7]) for i in range(3))
     projs = [projection(i, *bufs[21 + 6 * i : 27 + 6 * i]) for i in range(2)]
@@ -866,7 +885,7 @@
 
     def exchange(i):
         peer, slot = hops[i]
-        last.put(small_buf.at[i], small_buf.at[4 + i], slot, peer, lambda: small_buf.at[4 + i])
+        last.put(small_buf.at[i], small_buf.at[4 + i], slot, slot, peer)
 
     def combine(i):
         peer, slot = hops[i]
@@ -875,7 +894,7 @@
 
     def spread():
         for z in (1, 2, 3):
-            last.put(small_buf.at[3], small_buf.at[6 + z], 2 + z, place.zn[z], lambda z=z: small_buf.at[6 + z])
+            last.put(small_buf.at[3], small_buf.at[6 + z], 2 + z, 2 + z, place.zn[z])
 
     tile = 256
 
@@ -924,8 +943,9 @@
             if i == 0:
                 place.meet()
             down.begin(z)
-        down.first()
-        down.rest()
+            if i > 1:
+                down.pair(planes[i - 2])
+        down.all("pair", 1, 0)
         for copy in loads[1:3]:
             copy.wait()
 
@@ -965,7 +985,7 @@
         tiles(0, bufs[7], given.at[1], [(5, down.diags)])
         for z in planes:
             left.begin(z)
-        gives_down.drain(place.sib)
+        down.given()
         tiles(half_g // tile, bufs[14], given.at[0], [(2, down.relays, left.first, left.rest), (5, down.odd)])
         for z in planes:
             right.begin(z)
@@ -987,7 +1007,8 @@
         left.diags()
         right.first()
         right.rest()
-        gives.drain(place.sib)
+        left.given()
+        right.given()
 
     block = lambda *dims: pltpu.VMEM(dims, low)
     block_wide = lambda *dims: pltpu.VMEM(dims, wide)
@@ -1023,15 +1044,27 @@
                 projs[i].begin(z)
 
         def attention(q_v, k_v, v_v, span_v, att_v, x, dk_sum, dv_sum):
-            loads = [
-                pltpu.make_async_copy(src, dst, in_sem.at[i])
-                for i, (src, dst) in enumerate(((q, q_v), (k, k_v), (v, v_v), (span, span_v), (att, att_v), (tokens, x)))
-            ]
-            for copy in loads:
+            load = lambda i, src, dst: pltpu.make_async_copy(src, dst, in_sem.at[i])
+            sources = ((q, q_v), (k, k_v), (v, v_v), (att, att_v))
+            head, rest = slice(0, lane_width), slice(lane_width, width)
+            loads = [load(0, span, span_v)]
+            loads += [load(1 + i, src.at[:, head], dst.at[:, head]) for i, (src, dst) in enumerate(sources)]
+            later = [load(5 + i, src.at[:, rest], dst.at[:, rest]) for i, (src, dst) in enumerate(sources)]
+            later.append(load(9, tokens, x))
+            for copy in loads + later:
                 copy.start()
             for copy in loads:
                 copy.wait()
-            x_t[...] = x[...].T
+
+            def arrive():
+                for i, (src, dst) in enumerate(sources):
+                    load(5 + i, src.at[:, rest], dst.at[:, rest]).wait()
+                load(9, tokens, x).wait()
+                x_t[...] = x[...].T
+
+            def meet_small(i):
+                combine(i)
+                exchange(i + 1)
 
             def heads_back(begin, end, todo):
                 @pl.loop(begin, end)
@@ -1047,16 +1080,13 @@
                         def _(at=at, work=work):
                             for step in work:
                                 step()
-                            if at % 2:
-                                combine(at // 2)
-                                if at < 5:
-                                    exchange(at // 2 + 1)
-                                else:
-                                    spread()
-
-            heads_back(0, 4, [(0, down.even), (1, left.odd), (2, left.relays, right.diags), (3, right.odd)])
+
+            small_step = lambda i: lambda: meet_small(i)
+            heads_back(0, 4, [
+                (0, arrive, down.even, small_step(0)), (1, left.odd), (2, left.relays, right.diags), (3, right.odd),
+            ])
             project(0)
-            heads_back(4, pairs, [(4, left.even, early.first, early.rest), (5, right.relays)])
+            heads_back(4, pairs, [(4, left.even, early.first, early.rest, small_step(1)), (5, right.relays)])
             project(1)
 
         key_rows = k.shape[0]
@@ -1064,6 +1094,10 @@
             attention, block(*q.shape), block(*k.shape), block(*v.shape), block_wide(*span.shape), block(*att.shape),
             block(tok_rows, width), block_wide(key_rows, lane_width), block_wide(key_rows, lane_width),
         )
+
+        def meet_last():
+            combine(2)
+            spread()
 
         def finish(w_left, w_right):
             loads = [
@@ -1079,12 +1113,13 @@
             early.diags()
             late.first()
             late.rest()
+            right.even()
+            meet_last()
             w_k = w_left[:, :, width:].reshape(width, width)
             total += dot(d_k[...], w_k, ((1,), (1,)))
             early.relays()
             late.diags()
             early.odd()
-            right.even()
             total += dot(d_v[...], w_right[...].reshape(width, width), ((1,), (1,)))
             d_tokens[...] = total.astype(low)
             late.relays()
@@ -1101,29 +1136,29 @@
         attention_part, block(tok_rows, width), block_wide(4, 2, tok_rows, lane_width),
         block(pairs, 2, tok_rows, lane_width), block(width, tok_rows), block(tok_rows, width), block(tok_rows, width),
     )
+    mine, theirs = pl.ds(pl.multiple_of(24 * c, 8), 24), pl.ds(pl.multiple_of(24 - 24 * c, 8), 24)
+    total = down.total()
+    down_out[:rows_chip] = total[:, :width]
+    down_out[rows_chip:] = total[:, width:]
+
+    def swap(i, m, total, other, slot):
+        total[i] = m.total()
+        last.put(total.at[i, theirs], other.at[i], slot, slot, place.sib)
+
+    swap(0, left, g_sum, g_fin, 6)
+    swap(1, right, g_sum, g_fin, 7)
+    late.even()
+    swap(0, early, a_sum, a_fin, 8)
     for z in (1, 2, 3):
         last.got(small_buf.at[6 + z], 2 + z, place.zn[z])
     sums = (small_buf[3] + small_buf[7]) + (small_buf[8] + small_buf[9])
     share = width // 32
-    mine = (lax.axis_index("rows") * 2 + c) * share
-    tail[0:8, :] = pltpu.roll(sums[:8], lax.rem(width - mine, width), 1)[:, :lane_width]
+    at_row = (lax.axis_index("rows") * 2 + c) * share
+    tail[0:8, :] = pltpu.roll(sums[:8], lax.rem(width - at_row, width), 1)[:, :lane_width]
     squares = jnp.sum(sums[:8], 1, keepdims=True) / (sums[8:9, 0:1] * width)
     at = lambda axis: lax.broadcasted_iota(jnp.int32, (8, lane_width), axis)
     stats = jnp.where(at(0) == at(1) + 4, jnp.broadcast_to(jnp.sqrt(squares), (8, lane_width)), 0.0)
     tail[8:16, :] = jnp.broadcast_to(column_sum(stats), (8, lane_width))
-    mine, theirs = pl.ds(pl.multiple_of(24 * c, 8), 24), pl.ds(pl.multiple_of(24 - 24 * c, 8), 24)
-    total = down.total()
-    down_out[:rows_chip] = total[:, :width]
-    down_out[rows_chip:] = total[:, width:]
-
-    def swap(i, m, total, other, slot):
-        total[i] = m.total()
-        last.put(total.at[i, theirs], other.at[i], slot, place.sib, lambda: other.at[i])
-
-    swap(0, left, g_sum, g_fin, 6)
-    swap(1, right, g_sum, g_fin, 7)
-    swap(0, early, a_sum, a_fin, 8)
-    late.even()
     for i in range(2):
         last.got(g_fin.at[i], 6 + i, place.sib)
         own, other = g_sum[i, mine], g_fin[i]
@@ -1138,8 +1173,13 @@
             at = j * width + i * part
             qkv_out[:, at : at + part] = term
         wout_out[:, i * part : (i + 1) * part] = vo[:, part:]
-    copies.drain(place.sib)
-    last.drain(place.sib)
+    for m in (down, left, right, early, late):
+        m.drain()
+    for m in (early, late):
+        m.given()
+    sent = [small_buf.at[0]] * 6 + [g_fin.at[0]] * 2 + [a_fin.at[0]] * 2
+    for slot, ref in enumerate(sent):
+        last.sent(ref, slot, place.sib)
 
 
 def back(
@@ -1177,11 +1217,11 @@
             pltpu.VMEM((2, 24, half_g), wide),
             pltpu.VMEM((2, 24, width), wide),
             pltpu.VMEM((10,) + small.shape, wide),
-            dma(5 * scatter_slots),
+            dma(10),
             dma(5 * scatter_slots),
             dma(2, pairs),
             dma(2, 10),
-            dma(9),
+            dma(10),
             dma(4, 2),
         ],
         compiler_params=pltpu.CompilerParams(

time: 205 us -> 200 us (0.976)
  Pallas kernels: 203 us -> 197 us
    pallas_call x1, Pallas kernels: 106 us -> 98.5 us  [fore(): pl.pallas_call(lambda *refs: fore_kernel(heads, *refs), out_shape=tuple((...]
    pallas_call x1, Pallas kernels: 93.1 us -> 95.6 us  [back(): pl.pallas_call(lambda *refs: back_kernel(heads, *refs), out_shape=(shape(...]
where the time goes in v6:
time: 200 us
  Pallas kernels  197 us (98%)
    pallas_call x1, Pallas kernels, fore(): pl.pallas_call(lambda *refs: fore_kernel(heads, *refs), out_shape=tuple((...  98.5 us
    pallas_call x1, Pallas kernels, back(): pl.pallas_call(lambda *refs: back_kernel(heads, *refs), out_shape=(shape(...  95.6 us

profile of v6, /device:TPU:0, one launch (start us, length us, event | category | flops | bytes accessed | tf_op | source)
XLA Modules:
  0.0 199.5 jit_solution(5718032584153716971)
XLA Ops:
  0.6 1.3 pad_maximum_fusion.refs_6_
  1.9 98.5 %gather_and_forward.1 = (bf16[2,16,48,1664]{3,2,1,0:T(8,128)(2,1)}, bf16[2,16,48,3072]{3,2,1,0:T(8,128)(2,1)}, bf16[16,2,96,768]{3,2,1,0:T(8,128)(2,1)}, bf16[51...) custom-call(bf16[512,768]{1,0:T(8,128)(2,1)} %bitcast.15, ...), custom_call_target="tpu_custom_call" | custom-call | tf_op jit(solution)/shard_map/gather_and_forward/pallas_call | solution.py:832
  100.4 95.6 %backward_and_sums.1 = (bf16[512,768]{1,0:T(8,128)(2,1)}, f32[24,2304]{1,0:T(8,128)}, f32[24,768]{1,0:T(8,128)}, f32[24,6144]{1,0:T(8,128)}, f32[96,768]{1,0:T(8,128)}, /*index=5*/f32[16,128]{1,0:T(8,128)}) custom-call(bf16[512,768]{1,0:T(8,128)(2,1)} %bitcast.16, bf16[512,768]{1,0:T(8,128)(2,1)} %get-tuple-element.49.refs_1_, ...), custom_call_target="tpu_custom_call" | custom-call | tf_op jit(solution)/shard_map/backward_and_sums/pallas_call | solution.py:1201
  196.0 3.3 %results.1 = (bf16[512,768]{1,0:T(8,128)(2,1)}, bf16[512,768]{1,0:T(8,128)(2,1)}, f32[24,2304]{1,0:T(8,128)}, f32[24,768]{1,0:T(8,128)}, f32[24,6144]{1,0:T(8,12...) custom-call(bf16[512,768]{1,0:T(8,128)(2,1)} %get-tuple-element.48.r, ...), custom_call_target="tpu_custom_call" | custom-call | tf_op jit(solution)/shard_map/results/pallas_call | solution.py:1246

commit v7 on v6

--- a/solution.py
+++ b/solution.py
@@ -97,7 +97,7 @@
         self.cp.put(src, dst, self.pool, slot, peer)
 
     def push(self, src, k, j):
-        self.cp.put(src, self.block(k, j), self.pool + 1, self.slot("s"), self.p.sib)
+        self.cp.put(src, self.block(k, j), self.pool + 1, self.slot("s", k), self.p.sib)
 
     def to_z(self):
         for k in (1, 2):
@@ -162,8 +162,10 @@
             self.send(block, block, self.slot("d", k + 1), self.p.zn[1])
         self.push(block, k, "d")
 
-    def from_sib(self):
-        self.cp.got(self.side(1 - self.p.c), self.slot("s"), self.p.sib)
+    def from_sib(self, *planes):
+        for k in planes or range(4):
+            four = pl.ds(self.p.plane(k) * 4, 4)
+            self.cp.got(self.side(1 - self.p.c).at[four], self.slot("s", k), self.p.sib)
 
     def drain(self):
         side = self.side(self.p.c)
@@ -303,7 +305,7 @@
 
 
 rows_chip = 48
-gather_slots, scatter_slots = 16, 19
+gather_slots, scatter_slots = 19, 19
 
 
 def dot(left, right, dims=((1,), (0,))):
@@ -707,7 +709,7 @@
     save(k, k_out)
     save(v, v_out)
 
-    shares = (4, 4, 4, 4, 3, 3)
+    shares = (4, 4, 4, 4, 3, 2)
     todo = []
     for count in shares:
         todo.append(work[:count])
@@ -757,14 +759,15 @@
         act[:, cols] = (mixed * up).astype(low)
 
     upto(second)
+    go(1)
     second.from_sib()
-    go(1)
     save(w_g.at[:, :, :, :half_g], g_full.at[:, :, :, :half_g])
 
     @pl.loop(0, half_g // tile)
     def _(j):
         glu(j)
 
+    go(1)
     third.from_sib()
     save(w_g.at[:, :, :, half_g:], g_full.at[:, :, :, half_g:])
     for src, dst in ((slope_gate, gate_out), (slope_up, up_out), (act, act_out)):
@@ -776,18 +779,21 @@
 
     for src, dst in ((slope_gate, gate_out), (slope_up, up_out), (act, act_out)):
         save(src.at[:, half_g:], dst.at[:, half_g:])
+
+    def down(plane):
+        at = place.plane(plane)
+        cols = pl.ds(pl.multiple_of(at * width, width), width)
+        return dot(act[:, cols], w_d[pl.ds(at * 4, 4)].reshape(width, width))
+
+    go(1)
+    fourth.from_sib(0, 2, 1)
+    d_hid[...] = down(0)
+    for plane in (2, 1):
+        d_hid[...] += down(plane)
     upto(fourth)
-    fourth.from_sib()
+    fourth.from_sib(3)
     save(w_d, d_full)
-    d_hid[...] = jnp.zeros_like(d_hid)
-    chips = 4
-    deep = 2 * chips * w_d.shape[2]
-
-    @pl.loop(0, 16 // chips)
-    def _(j):
-        cols = pl.ds(pl.multiple_of(j * deep, deep), deep)
-        d_hid[...] += dot(act[:, cols], w_d[pl.ds(j * chips, chips)].reshape(deep, width))
-
+    d_hid[...] += down(3)
     branch = d_hid[...]
     small[7:8, :] = column_sum(mask * branch * branch)
     norm, inverse = normalized(hid[...] + branch)
@@ -864,7 +870,7 @@
     ff = gate.shape[1]
     pairs = heads // 2
     bufs, rest = scratch[:33], scratch[33:]
-    a_grad, dkv_in, resid, d_att, g_sum, a_sum, g_fin, a_fin, small_buf, send, recv, pair_sem, fin_sem, in_sem, tile_sem = rest
+    a_grad, dkv_in, resid, d_att, g_sum, a_sum, g_fin, a_fin, small_buf, send, recv, tokens_v, down_v, gu_v, pair_sem, fin_sem, in_sem, tile_sem = rest
     copies = Copies(send, recv)
     last = Copies(fin_sem.at[0], fin_sem.at[1])
     half_g, part = ff // 2, width // 2
@@ -875,12 +881,13 @@
     def projection(i, *more):
         give = lambda four: a_grad.at[i, 1 - c, four]
         own = lambda at: a_grad.at[i, c, at]
-        return Scatter(place, copies, 3 + i, give, own, *more, straight=i == 1)
+        return Scatter(place, copies, 3 + i, give, own, *more)
 
     down, left, right = (scatter(i, *bufs[7 * i : 7 * i + 7]) for i in range(3))
     projs = [projection(i, *bufs[21 + 6 * i : 27 + 6 * i]) for i in range(2)]
     early, late = projs
     planes = (3, 2, 1, 0)
+    hand_over = lambda i, src, dst: pltpu.make_async_copy(src, dst, in_sem.at[i])
     hops = ((place.sib, 0), (place.xn, 1), (place.yn, 2))
 
     def exchange(i):
@@ -945,7 +952,6 @@
             down.begin(z)
             if i > 1:
                 down.pair(planes[i - 2])
-        down.all("pair", 1, 0)
         for copy in loads[1:3]:
             copy.wait()
 
@@ -982,7 +988,7 @@
                 give_g[:, :, cols] = other.reshape(16, rows_chip, tile)
                 between(j - begin, todo)
 
-        tiles(0, bufs[7], given.at[1], [(5, down.diags)])
+        tiles(0, bufs[7], given.at[1], [(0, lambda: down.pair(1)), (1, lambda: down.pair(0)), (5, down.diags)])
         for z in planes:
             left.begin(z)
         down.given()
@@ -1120,10 +1126,11 @@
             early.relays()
             late.diags()
             early.odd()
+            early.even()
             total += dot(d_v[...], w_right[...].reshape(width, width), ((1,), (1,)))
-            d_tokens[...] = total.astype(low)
+            tokens_v[...] = total.astype(low)
+            hand_over(0, tokens_v, d_tokens).start()
             late.relays()
-            early.even()
             late.odd()
 
         pl.run_scoped(finish, block(16, rows_chip, 2 * width), block(16, rows_chip, width))
@@ -1138,8 +1145,9 @@
     )
     mine, theirs = pl.ds(pl.multiple_of(24 * c, 8), 24), pl.ds(pl.multiple_of(24 - 24 * c, 8), 24)
     total = down.total()
-    down_out[:rows_chip] = total[:, :width]
-    down_out[rows_chip:] = total[:, width:]
+    down_v[:rows_chip] = total[:, :width]
+    down_v[rows_chip:] = total[:, width:]
+    hand_over(1, down_v, down_out).start()
 
     def swap(i, m, total, other, slot):
         total[i] = m.total()
@@ -1162,8 +1170,9 @@
     for i in range(2):
         last.got(g_fin.at[i], 6 + i, place.sib)
         own, other = g_sum[i, mine], g_fin[i]
-        gu_out[:, i * half_g : (i + 1) * half_g] = jnp.where(first, own, other)
-        gu_out[:, (i + 2) * half_g : (i + 3) * half_g] = jnp.where(first, other, own)
+        gu_v[:, i * half_g : (i + 1) * half_g] = jnp.where(first, own, other)
+        gu_v[:, (i + 2) * half_g : (i + 3) * half_g] = jnp.where(first, other, own)
+    hand_over(2, gu_v, gu_out).start()
     swap(1, late, a_sum, a_fin, 9)
     for i in range(2):
         last.got(a_fin.at[i], 8 + i, place.sib)
@@ -1180,6 +1189,8 @@
     sent = [small_buf.at[0]] * 6 + [g_fin.at[0]] * 2 + [a_fin.at[0]] * 2
     for slot, ref in enumerate(sent):
         last.sent(ref, slot, place.sib)
+    for i, pair in enumerate(((tokens_v, d_tokens), (down_v, down_out), (gu_v, gu_out))):
+        hand_over(i, *pair).wait()
 
 
 def back(
@@ -1205,7 +1216,7 @@
             shape((24, 2 * ff), wide), shape((d_rows, width), wide), shape((16, lane_width), wide),
         ),
         in_specs=[hbm] * 17 + [vmem] * 3,
-        out_specs=(vmem,) * 6,
+        out_specs=(hbm, vmem, vmem, hbm, hbm, vmem),
         scratch_shapes=bufs
         + [
             pltpu.VMEM((2, 2, 16, rows_chip, width), low),
@@ -1219,6 +1230,9 @@
             pltpu.VMEM((10,) + small.shape, wide),
             dma(10),
             dma(5 * scatter_slots),
+            pltpu.VMEM((tok_rows, width), low),
+            pltpu.VMEM((d_rows, width), wide),
+            pltpu.VMEM((24, 2 * ff), wide),
             dma(2, pairs),
             dma(2, 10),
             dma(10),

time: 200 us -> 196 us (0.980)
  Pallas kernels: 197 us -> 194 us
    pallas_call x1, Pallas kernels: 95.6 us -> 92.9 us  [back(): pl.pallas_call(lambda *refs: back_kernel(heads, *refs), out_shape=(shape(...]
where the time goes in v7:
time: 196 us
  Pallas kernels  194 us (99%)
    pallas_call x1, Pallas kernels, fore(): pl.pallas_call(lambda *refs: fore_kernel(heads, *refs), out_shape=tuple((...  97.3 us
    pallas_call x1, Pallas kernels, back(): pl.pallas_call(lambda *refs: back_kernel(heads, *refs), out_shape=(shape(...  92.9 us

profile of v7, /device:TPU:0, one launch (start us, length us, event | category | flops | bytes accessed | tf_op | source)
XLA Modules:
  0.0 195.7 jit_solution(8018824548794092148)
XLA Ops:
  0.6 1.3 pad_maximum_fusion.refs_6_
  1.9 97.3 %gather_and_forward.1 = (bf16[2,16,48,1664]{3,2,1,0:T(8,128)(2,1)}, bf16[2,16,48,3072]{3,2,1,0:T(8,128)(2,1)}, bf16[16,2,96,768]{3,2,1,0:T(8,128)(2,1)}, bf16[51...) custom-call(bf16[512,768]{1,0:T(8,128)(2,1)} %bitcast.15, ...), custom_call_target="tpu_custom_call" | custom-call | tf_op jit(solution)/shard_map/gather_and_forward/pallas_call | solution.py:838
  99.2 92.9 %backward_and_sums.1 = (bf16[512,768]{1,0:T(8,128)(2,1)}, f32[24,2304]{1,0:T(8,128)}, f32[24,768]{1,0:T(8,128)}, f32[24,6144]{1,0:T(8,128)}, f32[96,768]{1,0:T(8,128)}, /*index=5*/f32[16,128]{1,0:T(8,128)}) custom-call(bf16[512,768]{1,0:T(8,128)(2,1)} %bitcast.16, bf16[512,768]{1,0:T(8,128)(2,1)} %get-tuple-element.49.refs_1_, ...), custom_call_target="tpu_custom_call" | custom-call | tf_op jit(solution)/shard_map/backward_and_sums/pallas_call | solution.py:1212
  192.2 3.3 %results.1 = (bf16[512,768]{1,0:T(8,128)(2,1)}, bf16[512,768]{1,0:T(8,128)(2,1)}, f32[24,2304]{1,0:T(8,128)}, f32[24,768]{1,0:T(8,128)}, f32[24,6144]{1,0:T(8,12...) custom-call(bf16[512,768]{1,0:T(8,128)(2,1)} %get-tuple-element.48.r, ...), custom_call_target="tpu_custom_call" | custom-call | tf_op jit(solution)/shard_map/results/pallas_call | solution.py:1260

commit v8 on v7

--- a/solution.py
+++ b/solution.py
@@ -607,7 +607,7 @@
 
 
 def fore_kernel(
-    heads, tokens, labels, w_qkv, w_out, w_gu, d_shard, norms, out_grad,
+    heads, tokens, labels, w_qkv, w_out, w_gu, d_shard, gain_one, bias_one, gain_two, bias_two, out_grad,
     a_full, g_full, d_full, q_out, k_out, v_out, att_out, hid_t_out, norm_out, inv_out, gate_out, up_out, act_out,
     output_out, d_hid_out, d_branch_out, span_out, lse, vectors, small,
     w_a, w_g, w_d, a_give, g_give, a_pair, g_pair, turned, q, k, v, att, span_v, grad_v, hid, hid_low, hid_t, norm_one, inv_one,
@@ -625,8 +625,10 @@
     load.start()
     core_one = c == 1
     turned[...] = jnp.zeros_like(turned)
-    turned[0:4, 0 : norms.shape[1]] = norms[...].astype(wide)
-    table = turned[...].T[: norms.shape[1]].astype(low)
+    share = w_out.shape[0]
+    for i, norm in enumerate((gain_one, bias_one, gain_two, bias_two)):
+        turned[i : i + 1, 0:share] = norm[...].astype(wide).reshape(1, share)
+    table = turned[...].T[:share].astype(low)
     left = jnp.concatenate([w_qkv[:, : 2 * width], table], 1)
     right = jnp.concatenate([w_qkv[:, 2 * width :], w_out[...], jnp.zeros_like(table)], 1)
     gate, up = w_gu[:, :ff], w_gu[:, ff:]
@@ -709,7 +711,7 @@
     save(k, k_out)
     save(v, v_out)
 
-    shares = (4, 4, 4, 4, 3, 2)
+    shares = (3, 4, 4, 4, 4, 2)
     todo = []
     for count in shares:
         todo.append(work[:count])
@@ -839,7 +841,7 @@
         lambda *refs: fore_kernel(heads, *refs),
         out_shape=tuple(shape(dims, kind) for dims, kind in stored)
         + (shape((16, rows), wide), shape((8, width), wide), shape((16, width), wide)),
-        in_specs=[vmem] * 7 + [hbm],
+        in_specs=[vmem] * 10 + [hbm],
         out_specs=(hbm,) * len(stored) + (vmem,) * 3,
         scratch_shapes=[
             block(*w_a), block(*w_g), block(*w_d), block(32, half_a), block(32, ff), block(32, half_a), block(32, ff),
@@ -854,7 +856,7 @@
             collective_id=0, has_side_effects=True, vmem_limit_bytes=62 * 2**20
         ),
         name="gather_and_forward",
-    )(tokens, labels, w_qkv, w_out, w_gu, d_shard, norms, out_grad)
+    )(tokens, labels, w_qkv, w_out, w_gu, d_shard, *norms, out_grad)
 
 
 def back_kernel(
@@ -1318,7 +1320,7 @@
     (
         a_full, g_full, d_full, q, k, v, att, hid_t, norm, inv, gate, up, act, output, d_hid, d_branch, span,
         lse, vectors, small,
-    ) = fore(HEADS, tokens, labels, w_qkv, w_out, w_gate_up, w_down, jnp.stack(norms), out_grad)
+    ) = fore(HEADS, tokens, labels, w_qkv, w_out, w_gate_up, w_down, norms, out_grad)
     parts = back(
         HEADS, tokens, q, k, v, span, att, hid_t, norm, inv, gate, up, act, d_hid, d_branch, a_full, g_full,
         d_full.reshape(-1, width), lse, vectors, small,

time: 196 us -> 191 us (0.974)
  Pallas kernels: 194 us -> 190 us
    pallas_call x1, Pallas kernels: 97.3 us -> 95 us  [fore(): pl.pallas_call(lambda *refs: fore_kernel(heads, *refs), out_shape=tuple((...]
where the time goes in v8:
time: 191 us
  Pallas kernels  190 us (99%)
    pallas_call x1, Pallas kernels, fore(): pl.pallas_call(lambda *refs: fore_kernel(heads, *refs), out_shape=tuple((...  95 us
    pallas_call x1, Pallas kernels, back(): pl.pallas_call(lambda *refs: back_kernel(heads, *refs), out_shape=(shape(...  92 us

profile of v8, /device:TPU:0, one launch (start us, length us, event | category | flops | bytes accessed | tf_op | source)
XLA Modules:
  0.0 191.1 jit_solution(18127146268095215735)
XLA Ops:
  0.6 95.0 %gather_and_forward.1 = (bf16[2,16,48,1664]{3,2,1,0:T(8,128)(2,1)}, bf16[2,16,48,3072]{3,2,1,0:T(8,128)(2,1)}, bf16[16,2,96,768]{3,2,1,0:T(8,128)(2,1)}, bf16[51...) custom-call(bf16[512,768]{1,0:T(8,128)(2,1)} %bitcast.11, ...), custom_call_target="tpu_custom_call" | custom-call | tf_op jit(solution)/shard_map/gather_and_forward/pallas_call | solution.py:840
  95.6 92.0 %backward_and_sums.1 = (bf16[512,768]{1,0:T(8,128)(2,1)}, f32[24,2304]{1,0:T(8,128)}, f32[24,768]{1,0:T(8,128)}, f32[24,6144]{1,0:T(8,128)}, f32[96,768]{1,0:T(8,128)}, /*index=5*/f32[16,128]{1,0:T(8,128)}) custom-call(bf16[512,768]{1,0:T(8,128)(2,1)} %bitcast.12, bf16[512,768]{1,0:T(8,128)(2,1)} %get-tuple-element.49.refs_1_, ...), custom_call_target="tpu_custom_call" | custom-call | tf_op jit(solution)/shard_map/backward_and_sums/pallas_call | solution.py:1214
  187.7 3.3 %results.1 = (bf16[512,768]{1,0:T(8,128)(2,1)}, bf16[512,768]{1,0:T(8,128)(2,1)}, f32[24,2304]{1,0:T(8,128)}, f32[24,768]{1,0:T(8,128)}, f32[24,6144]{1,0:T(8,12...) custom-call(bf16[512,768]{1,0:T(8,128)(2,1)} %get-tuple-element.48.r, ...), custom_call_target="tpu_custom_call" | custom-call | tf_op jit(solution)/shard_map/results/pallas_call | solution.py:1262

commit v9 on v8

--- a/solution.py
+++ b/solution.py
@@ -607,13 +607,21 @@
 
 
 def fore_kernel(
-    heads, tokens, labels, w_qkv, w_out, w_gu, d_shard, gain_one, bias_one, gain_two, bias_two, out_grad,
-    a_full, g_full, d_full, q_out, k_out, v_out, att_out, hid_t_out, norm_out, inv_out, gate_out, up_out, act_out,
+    heads, tokens_at, labels_at, w_qkv_at, w_out_at, w_gu_at, d_shard_at, gain_one_at, bias_one_at, gain_two_at, bias_two_at,
+    out_grad, a_full, g_full, d_full, q_out, k_out, v_out, att_out, hid_t_out, norm_out, inv_out, gate_out, up_out, act_out,
     output_out, d_hid_out, d_branch_out, span_out, lse, vectors, small,
     w_a, w_g, w_d, a_give, g_give, a_pair, g_pair, turned, q, k, v, att, span_v, grad_v, hid, hid_low, hid_t, norm_one, inv_one,
-    slope_gate, slope_up, act, output, d_hid, d_branch, pair_sem, send, recv, in_sem, out_sem,
+    slope_gate, slope_up, act, output, d_hid, d_branch,
+    tokens, labels, w_qkv, w_out, w_gu, d_shard, gain_one, bias_one, gain_two, bias_two, pair_sem, send, recv, in_sem, out_sem,
 ):
     place = Place()
+    sources = (
+        w_gu_at, w_qkv_at, w_out_at, gain_one_at, bias_one_at, gain_two_at, bias_two_at, d_shard_at, labels_at, tokens_at,
+    )
+    held = (w_gu, w_qkv, w_out, gain_one, bias_one, gain_two, bias_two, d_shard, labels, tokens)
+    inward = [pltpu.make_async_copy(src, dst, in_sem.at[1 + i]) for i, (src, dst) in enumerate(zip(sources, held))]
+    for copy in inward:
+        copy.start()
     place.greet()
     c = place.c
     low, wide = jnp.bfloat16, jnp.float32
@@ -624,6 +632,8 @@
     load = pltpu.make_async_copy(out_grad, grad_v, in_sem.at[0])
     load.start()
     core_one = c == 1
+    for copy in inward:
+        copy.wait()
     turned[...] = jnp.zeros_like(turned)
     share = w_out.shape[0]
     for i, norm in enumerate((gain_one, bias_one, gain_two, bias_two)):
@@ -841,7 +851,7 @@
         lambda *refs: fore_kernel(heads, *refs),
         out_shape=tuple(shape(dims, kind) for dims, kind in stored)
         + (shape((16, rows), wide), shape((8, width), wide), shape((16, width), wide)),
-        in_specs=[vmem] * 10 + [hbm],
+        in_specs=[hbm] * 11,
         out_specs=(hbm,) * len(stored) + (vmem,) * 3,
         scratch_shapes=[
             block(*w_a), block(*w_g), block(*w_d), block(32, half_a), block(32, ff), block(32, half_a), block(32, ff),
@@ -850,7 +860,9 @@
             block_wide(keys, rows), block(rows, width), block_wide(rows, width), block(rows, width),
             block(width, rows), block_wide(rows, width), block_wide(rows, lane_width),
             block(rows, ff), block(rows, ff), block(rows, ff), block(rows, width), block_wide(rows, width),
-            block(rows, width), dma(2, 4), dma(8), dma(4 * gather_slots), dma(1), dma(len(stored) + 4),
+            block(rows, width),
+            *(pltpu.VMEM(part.shape, part.dtype) for part in (tokens, labels, w_qkv, w_out, w_gu, d_shard, *norms)),
+            dma(2, 4), dma(8), dma(4 * gather_slots), dma(11), dma(len(stored) + 4),
         ],
         compiler_params=pltpu.CompilerParams(
             collective_id=0, has_side_effects=True, vmem_limit_bytes=62 * 2**20
@@ -861,7 +873,7 @@
 
 def back_kernel(
     heads, tokens, q, k, v, span, att, hid_t, norm, inv, gate, up, act, d_hid, d_branch, a_full, g_full, d_full,
-    lse, vectors, small, d_tokens, qkv_out, wout_out, gu_out, down_out, tail, *scratch,
+    lse_at, vectors_at, small_at, d_tokens, qkv_out, wout_out, gu_out, down_out, tail, *scratch,
 ):
     place = Place()
     place.greet()
@@ -872,7 +884,7 @@
     ff = gate.shape[1]
     pairs = heads // 2
     bufs, rest = scratch[:33], scratch[33:]
-    a_grad, dkv_in, resid, d_att, g_sum, a_sum, g_fin, a_fin, small_buf, send, recv, tokens_v, down_v, gu_v, pair_sem, fin_sem, in_sem, tile_sem = rest
+    a_grad, dkv_in, resid, d_att, g_sum, a_sum, g_fin, a_fin, small_buf, send, recv, tokens_v, down_v, gu_v, lse, vectors, small, pair_sem, fin_sem, in_sem, tile_sem = rest
     copies = Copies(send, recv)
     last = Copies(fin_sem.at[0], fin_sem.at[1])
     half_g, part = ff // 2, width // 2
@@ -931,9 +943,10 @@
             ]
 
         loads[0].start()
+        tables = [load(9 + i, src, dst) for i, (src, dst) in enumerate(((lse_at, lse), (vectors_at, vectors), (small_at, small)))]
         act_load(0, planes[0]).start()
         act_load(1, planes[1]).start()
-        for copy in loads[1:] + fetch(0):
+        for copy in loads[1:] + fetch(0) + tables:
             copy.start()
         loads[0].wait()
         own_d = bufs[0]
@@ -997,7 +1010,7 @@
         tiles(half_g // tile, bufs[14], given.at[0], [(2, down.relays, left.first, left.rest), (5, down.odd)])
         for z in planes:
             right.begin(z)
-        for copy in loads[3:]:
+        for copy in loads[3:] + tables:
             copy.wait()
         grad = resid[...]
         unit = norm_v[...]
@@ -1217,7 +1230,7 @@
             shape((tok_rows, width), low), shape((24, 3 * width), wide), shape((24, width), wide),
             shape((24, 2 * ff), wide), shape((d_rows, width), wide), shape((16, lane_width), wide),
         ),
-        in_specs=[hbm] * 17 + [vmem] * 3,
+        in_specs=[hbm] * 20,
         out_specs=(hbm, vmem, vmem, hbm, hbm, vmem),
         scratch_shapes=bufs
         + [
@@ -1235,9 +1248,10 @@
             pltpu.VMEM((tok_rows, width), low),
             pltpu.VMEM((d_rows, width), wide),
             pltpu.VMEM((24, 2 * ff), wide),
+            *(pltpu.VMEM(part.shape, wide) for part in (lse, vectors, small)),
             dma(2, pairs),
             dma(2, 10),
-            dma(10),
+            dma(12),
             dma(4, 2),
         ],
         compiler_params=pltpu.CompilerParams(

time: 191 us -> 190 us (level)
  no operation moved by 1% of the time
where the time goes in v9:
time: 190 us; the launch traced here: 189 us
  Pallas kernels  189 us (99%)
    pallas_call x1, Pallas kernels, fore(): pl.pallas_call(lambda *refs: fore_kernel(heads, *refs), out_shape=tuple((...  93.5 us
    pallas_call x1, Pallas kernels, back(): pl.pallas_call(lambda *refs: back_kernel(heads, *refs), out_shape=(shape(...  91.7 us

profile of v9, /device:TPU:0, one launch (start us, length us, event | category | flops | bytes accessed | tf_op | source)
XLA Modules:
  0.0 189.4 jit_solution(9475158743461877939)
XLA Ops:
  0.6 93.5 %gather_and_forward.1 = (bf16[2,16,48,1664]{3,2,1,0:T(8,128)(2,1)}, bf16[2,16,48,3072]{3,2,1,0:T(8,128)(2,1)}, bf16[16,2,96,768]{3,2,1,0:T(8,128)(2,1)}, bf16[51...) custom-call(bf16[512,768]{1,0:T(8,128)(2,1)} %bitcast.11, ...), custom_call_target="tpu_custom_call" | custom-call | tf_op jit(solution)/shard_map/gather_and_forward/pallas_call | solution.py:850
  94.2 91.7 %backward_and_sums.1 = (bf16[512,768]{1,0:T(8,128)(2,1)}, f32[24,2304]{1,0:T(8,128)}, f32[24,768]{1,0:T(8,128)}, f32[24,6144]{1,0:T(8,128)}, f32[96,768]{1,0:T(8,128)}, /*index=5*/f32[16,128]{1,0:T(8,128)}) custom-call(bf16[512,768]{1,0:T(8,128)(2,1)} %bitcast.12, bf16[512,768]{1,0:T(8,128)(2,1)} %get-tuple-element.49.refs_1_, ...), custom_call_target="tpu_custom_call" | custom-call | tf_op jit(solution)/shard_map/backward_and_sums/pallas_call | solution.py:1227
  185.9 3.3 %results.1 = (bf16[512,768]{1,0:T(8,128)(2,1)}, bf16[512,768]{1,0:T(8,128)(2,1)}, f32[24,2304]{1,0:T(8,128)}, f32[24,768]{1,0:T(8,128)}, f32[24,6144]{1,0:T(8,12...) custom-call(bf16[512,768]{1,0:T(8,128)(2,1)} %get-tuple-element.48.r, ...), custom_call_target="tpu_custom_call" | custom-call | tf_op jit(solution)/shard_map/results/pallas_call | solution.py:1276

commit v10 on v9

--- a/solution.py
+++ b/solution.py
@@ -609,7 +609,7 @@
 def fore_kernel(
     heads, tokens_at, labels_at, w_qkv_at, w_out_at, w_gu_at, d_shard_at, gain_one_at, bias_one_at, gain_two_at, bias_two_at,
     out_grad, a_full, g_full, d_full, q_out, k_out, v_out, att_out, hid_t_out, norm_out, inv_out, gate_out, up_out, act_out,
-    output_out, d_hid_out, d_branch_out, span_out, lse, vectors, small,
+    output_out, d_branch_out, span_out, lse, vectors, small,
     w_a, w_g, w_d, a_give, g_give, a_pair, g_pair, turned, q, k, v, att, span_v, grad_v, hid, hid_low, hid_t, norm_one, inv_one,
     slope_gate, slope_up, act, output, d_hid, d_branch,
     tokens, labels, w_qkv, w_out, w_gu, d_shard, gain_one, bias_one, gain_two, bias_two, pair_sem, send, recv, in_sem, out_sem,
@@ -817,9 +817,7 @@
     small[2:3, :] = column_sum(grad * norm)
     small[3:4, :] = column_sum(grad)
     back = norm_back(grad, gain, norm, inverse)
-    d_hid[...] = back
     d_branch[...] = back.astype(low)
-    save(d_hid, d_hid_out)
     save(d_branch, d_branch_out)
     for i, (src, dst) in enumerate(saved):
         pltpu.make_async_copy(src, dst, out_sem.at[i]).wait()
@@ -842,7 +840,7 @@
     stored = [
         (w_a, low), (w_g, low), (w_d, low), ((rows, width), low), ((keys, width), low), ((keys, width), low),
         ((rows, width), low), ((width, rows), low), ((rows, width), wide), ((rows, lane_width), wide),
-        ((rows, ff), low), ((rows, ff), low), ((rows, ff), low), ((rows, width), low), ((rows, width), wide),
+        ((rows, ff), low), ((rows, ff), low), ((rows, ff), low), ((rows, width), low),
         ((rows, width), low), ((keys, rows), wide),
     ]
     block = lambda *dims: pltpu.VMEM(dims, low)
@@ -872,7 +870,7 @@
 
 
 def back_kernel(
-    heads, tokens, q, k, v, span, att, hid_t, norm, inv, gate, up, act, d_hid, d_branch, a_full, g_full, d_full,
+    heads, tokens, q, k, v, span, att, hid_t, norm, inv, gate, up, act, d_branch, a_full, g_full, d_full,
     lse_at, vectors_at, small_at, d_tokens, qkv_out, wout_out, gu_out, down_out, tail, *scratch,
 ):
     place = Place()
@@ -924,7 +922,7 @@
             m.give = lambda four, i=i: given.at[i % 2, four]
         load = lambda i, src, dst: pltpu.make_async_copy(src, dst, in_sem.at[i])
         loads = [
-            load(0, d_branch, db), load(1, hid_t, ht), load(2, d_hid, resid), load(3, att, att_v),
+            load(0, d_branch, db), load(1, hid_t, ht), load(3, att, att_v),
             load(4, norm, norm_v), load(5, inv, inv_v), load(6, a_full.at[1, :, :, width : 2 * width], w_out),
         ]
 
@@ -967,8 +965,8 @@
             down.begin(z)
             if i > 1:
                 down.pair(planes[i - 2])
-        for copy in loads[1:3]:
-            copy.wait()
+        loads[1].wait()
+        resid[...] = db[...].astype(wide)
 
         def between(i, todo):
             for at, *work in todo:
@@ -1010,7 +1008,7 @@
         tiles(half_g // tile, bufs[14], given.at[0], [(2, down.relays, left.first, left.rest), (5, down.odd)])
         for z in planes:
             right.begin(z)
-        for copy in loads[3:] + tables:
+        for copy in loads[2:] + tables:
             copy.wait()
         grad = resid[...]
         unit = norm_v[...]
@@ -1209,7 +1207,7 @@
 
 
 def back(
-    heads, tokens, q, k, v, span, att, hid_t, norm, inv, gate, up, act, d_hid, d_branch, a_full, g_full, d_full,
+    heads, tokens, q, k, v, span, att, hid_t, norm, inv, gate, up, act, d_branch, a_full, g_full, d_full,
     lse, vectors, small,
 ):
     low, wide = jnp.bfloat16, jnp.float32
@@ -1230,7 +1228,7 @@
             shape((tok_rows, width), low), shape((24, 3 * width), wide), shape((24, width), wide),
             shape((24, 2 * ff), wide), shape((d_rows, width), wide), shape((16, lane_width), wide),
         ),
-        in_specs=[hbm] * 20,
+        in_specs=[hbm] * 19,
         out_specs=(hbm, vmem, vmem, hbm, hbm, vmem),
         scratch_shapes=bufs
         + [
@@ -1258,7 +1256,7 @@
             collective_id=1, has_side_effects=True, vmem_limit_bytes=63 * 2**20
         ),
         name="backward_and_sums",
-    )(tokens, q, k, v, span, att, hid_t, norm, inv, gate, up, act, d_hid, d_branch, a_full, g_full, d_full, lse, vectors, small)
+    )(tokens, q, k, v, span, att, hid_t, norm, inv, gate, up, act, d_branch, a_full, g_full, d_full, lse, vectors, small)
 
 
 def close_kernel(share, *refs):
@@ -1332,11 +1330,11 @@
 def on_grid(tokens, labels, w_qkv, w_out, w_gate_up, w_down, norms, out_grad):
     width = tokens.shape[1]
     (
-        a_full, g_full, d_full, q, k, v, att, hid_t, norm, inv, gate, up, act, output, d_hid, d_branch, span,
+        a_full, g_full, d_full, q, k, v, att, hid_t, norm, inv, gate, up, act, output, d_branch, span,
         lse, vectors, small,
     ) = fore(HEADS, tokens, labels, w_qkv, w_out, w_gate_up, w_down, norms, out_grad)
     parts = back(
-        HEADS, tokens, q, k, v, span, att, hid_t, norm, inv, gate, up, act, d_hid, d_branch, a_full, g_full,
+        HEADS, tokens, q, k, v, span, att, hid_t, norm, inv, gate, up, act, d_branch, a_full, g_full,
         d_full.reshape(-1, width), lse, vectors, small,
     )
     *parts, one, two, three, four, stats = close(norms[0].shape[0], output, *parts)

time: 190 us -> 189 us (level)
  no operation moved by 1% of the time
where the time goes in v10:
time: 189 us
  Pallas kernels  188 us (99%)
    pallas_call x1, Pallas kernels, fore(): pl.pallas_call(lambda *refs: fore_kernel(heads, *refs), out_shape=tuple((...  93 us
    pallas_call x1, Pallas kernels, back(): pl.pallas_call(lambda *refs: back_kernel(heads, *refs), out_shape=(shape(...  91.5 us

profile of v10, /device:TPU:0, one launch (start us, length us, event | category | flops | bytes accessed | tf_op | source)
XLA Modules:
  0.0 188.6 jit_solution(6973170539416898363)
XLA Ops:
  0.6 93.0 %gather_and_forward.1 = (bf16[2,16,48,1664]{3,2,1,0:T(8,128)(2,1)}, bf16[2,16,48,3072]{3,2,1,0:T(8,128)(2,1)}, bf16[16,2,96,768]{3,2,1,0:T(8,128)(2,1)}, bf16[51...) custom-call(bf16[512,768]{1,0:T(8,128)(2,1)} %bitcast.11, ...), custom_call_target="tpu_custom_call" | custom-call | tf_op jit(solution)/shard_map/gather_and_forward/pallas_call | solution.py:848
  93.6 91.5 %backward_and_sums.1 = (bf16[512,768]{1,0:T(8,128)(2,1)}, f32[24,2304]{1,0:T(8,128)}, f32[24,768]{1,0:T(8,128)}, f32[24,6144]{1,0:T(8,128)}, f32[96,768]{1,0:T(8,128)}, /*index=5*/f32[16,128]{1,0:T(8,128)}) custom-call(bf16[512,768]{1,0:T(8,128)(2,1)} %bitcast.12, bf16[512,768]{1,0:T(8,128)(2,1)} %get-tuple-element.48.refs_1_, ...), custom_call_target="tpu_custom_call" | custom-call | tf_op jit(solution)/shard_map/backward_and_sums/pallas_call | solution.py:1225
  185.1 3.3 %results.1 = (bf16[512,768]{1,0:T(8,128)(2,1)}, bf16[512,768]{1,0:T(8,128)(2,1)}, f32[24,2304]{1,0:T(8,128)}, f32[24,768]{1,0:T(8,128)}, f32[24,6144]{1,0:T(8,12...) custom-call(bf16[512,768]{1,0:T(8,128)(2,1)} %get-tuple-element.47.r, ...), custom_call_target="tpu_custom_call" | custom-call | tf_op jit(solution)/shard_map/results/pallas_call | solution.py:1274
